TPU v7x, 32 devices: a whole 2x2x4 slice. The times are simulated.
32 devices in a mesh: groups: 2 (over y), lat: 4 (over z), chan: 4 (over x, core).
Axes of the slice: x: 2, y: 2, z: 4, core: 2. Of those that a mesh axis runs over, the one named last changes fastest.
Arguments:
- grid_input: bfloat16 [16, 1440, 1024], P(('groups', 'lat'), None, 'chan'), parts along dimension 0, may hold values from -6 to 6
- legendre: bfloat16 [64, 512, 8], P(('lat', 'chan')), may hold values from -2 to 2
- mix_weight: bfloat16 [1024, 1024], P(None, 'lat'), may hold values from -0.1875 to 0.1875
- degree_gain: float32 [512], replicated, may hold values from 0.3 to 3
- order_slot: int32 [64], replicated, may hold values from 0 to 63, as said below
Outputs:
- grid_output: bfloat16 [16, 1440, 1024], P(('groups', 'lat'), None, 'chan'), parts along dimension 0
There are 2 independent parts, one for each index of `groups`. A program takes and returns all parts, laid end to end along the dimension named above; an argument that names none is the same for every part. Nothing has to cross between parts.
Inputs may be any that keep to these rules, and one draw needn't show every extreme that they name: order_slot is a permutation of the orders 0 to 63.
All inputs are finite; a program needn't handle non-finite values.
Results may differ from a plain program's by a relative error of at most 0.0067.
Values may be sent and summed in bfloat16 or wider, within the bound.
No kernel may reach another device: no remote copies, remote signals or barrier semaphores. Data moves between devices by JAX's collectives and lax.ppermute only.
A program may use at most 64 MiB of HBM per device.

v0:
```python
import math

import jax
import jax.numpy as jnp
from jax import lax
from jax.sharding import PartitionSpec as P


def transform_tables(order_index, longitudes):
    steps_along = jnp.arange(longitudes, dtype=jnp.int32)
    residue = steps_along[:, None] * order_index[None, :] % longitudes
    angle_value = residue.astype(jnp.float32) * (2.0 * math.pi / longitudes)
    factor = 1.0 / math.sqrt(longitudes)
    weight = jnp.where(order_index == 0, 1.0, 2.0).astype(jnp.float32)
    cosine = jnp.cos(angle_value) * factor
    sine_part = jnp.sin(angle_value) * factor
    forward_table = jnp.concatenate([cosine, -sine_part], axis=1).astype(jnp.bfloat16)
    inverse_table = jnp.concatenate(
        [weight[None, :] * cosine, -weight[None, :] * sine_part], axis=1
    ).astype(jnp.bfloat16)
    return (forward_table, inverse_table)


def masked_analysis(table_part, rows_here, blocks, offset):
    coefficients = jnp.einsum(
        "slt,trsc->slrc", table_part, rows_here, preferred_element_type=jnp.float32
    )
    degree_block = (offset + jnp.arange(table_part.shape[1], dtype=jnp.int32)) // 64
    alive_mask = degree_block[None, :] >= blocks[:, None]
    return jnp.where(alive_mask[:, :, None, None], coefficients, 0.0).astype(jnp.bfloat16)


def mix_degrees(coefficients, weights_full, gain_part):
    mixed_coef = jnp.einsum(
        "slrc,cd->slrd", coefficients, weights_full, preferred_element_type=jnp.float32
    )
    return (mixed_coef * gain_part[None, :, None, None]).astype(jnp.bfloat16)


def owner_products(owned_rows, legendre, first_block, weights_full, degree_gain, factor):
    slot_count, degrees, latitudes = legendre.shape
    running_sum = jnp.zeros(
        (latitudes, owned_rows.shape[1], slot_count, owned_rows.shape[3]), jnp.float32
    )
    for offset in range(0, degrees, 128):
        table_part = legendre[:, offset : offset + 128, :]
        coefficients = masked_analysis(table_part, owned_rows, first_block, offset)
        mixed_coef = mix_degrees(coefficients, weights_full, degree_gain[offset : offset + 128])
        running_sum = running_sum + jnp.einsum(
            "slt,slrd->trsd", table_part, mixed_coef, preferred_element_type=jnp.float32
        )
    return (running_sum * factor).astype(jnp.bfloat16)


def shards(grid_input, legendre, mix_weight, degree_gain, order_slot):
    lat_dev, longitudes, chan_dev = grid_input.shape
    orders = order_slot.shape[0]
    degrees = legendre.shape[1]
    slot_count = legendre.shape[0]
    factor = math.sqrt(legendre.shape[2] / degrees)
    lat_count = lax.axis_size("lat")
    chan_count = lax.axis_size("chan")
    own_start = (lax.axis_index("lat") * chan_count + lax.axis_index("chan")) * slot_count
    first_block = lax.dynamic_slice_in_dim(order_slot, own_start, slot_count, 0) // 64
    forward_table, unused_table = transform_tables(order_slot, longitudes)
    spectrum = jnp.einsum(
        "akc,kn->anc", grid_input, forward_table, preferred_element_type=jnp.float32
    )
    spectrum = spectrum.reshape(lat_dev, 2, orders, chan_dev).astype(jnp.bfloat16)
    weights_full = lax.all_gather(mix_weight, "lat", axis=1, tiled=True)
    owned_rows = lax.all_to_all(
        lax.all_to_all(spectrum, "lat", split_axis=2, concat_axis=0, tiled=True),
        "chan",
        split_axis=2,
        concat_axis=3,
        tiled=True,
    )
    synthesis = owner_products(owned_rows, legendre, first_block, weights_full, degree_gain, factor)
    returned = lax.all_to_all(
        lax.all_to_all(synthesis, "lat", split_axis=0, concat_axis=2, tiled=True),
        "chan",
        split_axis=3,
        concat_axis=2,
        tiled=True,
    )
    positions = jnp.arange(orders, dtype=jnp.int32).reshape(lat_count, chan_count, slot_count)
    positions = positions.transpose(1, 0, 2).reshape(orders)
    order_of_position = jnp.take(order_slot, positions)
    unused_forward, inverse_table = transform_tables(order_of_position, longitudes)
    field_sum = jnp.einsum(
        "anc,kn->akc",
        returned.reshape(lat_dev, 2 * orders, chan_dev),
        inverse_table,
        preferred_element_type=jnp.float32,
    )
    return (grid_input.astype(jnp.float32) + jax.nn.gelu(field_sum)).astype(jnp.bfloat16)


def solution(mesh):
    placed = (
        P(("groups", "lat"), None, "chan"),
        P(("lat", "chan"), None, None),
        P(None, "lat"),
        P(),
        P(),
    )
    return jax.shard_map(
        shards,
        mesh=mesh,
        in_specs=placed,
        out_specs=P(("groups", "lat"), None, "chan"),
        check_vma=False,
    )
```

profile of v0, /device:TPU:0, one launch (start us, length us, event | category | flops | bytes accessed | tf_op | source)
XLA Modules:
  0.0 114.3 jit_solution(8344166700187515374)
XLA Ops:
  6.5 0.7 all-gather.2.cloned.1.call-update
  7.3 2.5 %multiply_convert_fusion.4 = (bf16[1440,64]{0,1:T(8,128)(2,1)S(1)}, bf16[1440,64]{0,1:T(8,128)(2,1)S(1)}) fusion(s32[64]{0:T(128)} %param.9), kind=kLoop, calls=%fused_computation.48 | loop fusion | flops 1290240 | bytes 368896 | tf_op jit(solution)/shard_map/convert.1
  9.8 1.8 %convolution_convert_fusion = bf16[128,2,256]{2,0,1:T(8,128)(2,1)S(1)} fusion(bf16[2,1440,256]{2,1,0:T(8,128)(2,1)} %param.5, bf16[1440,64]{0,1:T(8,128)(2,1)S(1)} %get-tuple-element.18, bf16[1440,64]{0,1:T(8,128)(2,1)S(1)} %get-tuple-element.17), kind=kOutput, calls=%fused_computation.33 | convolution fusion | flops 189546496 | bytes 1974272 | tf_op jit(solution)/shard_map/akc,kn->anc/dot_general | solution.py:66
  11.6 0.8 copy.47
  12.3 6.3 %all-to-all-start = ((bf16[2,2,64,256]{3,1,0,2:T(2,128)(2,1)}), bf16[2,2,64,256]{3,1,0,2:T(2,128)(2,1)S(1)}, u32[]{:S(2)}, u32[]{:S(2)}) async-start(bf16[2,2,64,256]{3,1,0,2:T(2,128)(2,1)} %copy.47), calls=%async_computation | async-start | bytes 262144 | tf_op jit(solution)/shard_map/all_to_all | solution.py:72
  18.8 0.1 reshape.337
  18.9 0.8 gather_fusion
  19.9 12.2 %all-to-all-done = bf16[2,2,64,256]{3,1,0,2:T(2,128)(2,1)S(1)} async-done(((bf16[2,2,64,256]{3,1,0,2:T(2,128)(2,1)}), bf16[2,2,64,256]{3,1,0,2:T(2,128)(2,1)S(1)}, u32[]{:S(2)}, u32[]{:S(2)}) %all-to-all-start) | async-done | bytes 131104 | tf_op jit(solution)/shard_map/all_to_all | solution.py:72
  32.1 0.8 copy.50
  32.9 3.3 %all-to-all-start.1 = ((bf16[8,2,16,256]{3,1,0,2:T(2,128)(2,1)}), bf16[8,2,16,256]{3,1,0,2:T(2,128)(2,1)S(1)}, u32[]{:S(2)}, u32[]{:S(2)}) async-start(bf16[8,2,16,256]{3,1,0,2:T(2,128)(2,1)} %copy.50), calls=%async_computation.1 | async-start | bytes 262144 | tf_op jit(solution)/shard_map/all_to_all | solution.py:71
  36.2 4.6 %all-to-all-done.1 = bf16[8,2,16,256]{3,1,0,2:T(2,128)(2,1)S(1)} async-done(((bf16[8,2,16,256]{3,1,0,2:T(2,128)(2,1)}), bf16[8,2,16,256]{3,1,0,2:T(2,128)(2,1)S(1)}, u32[]{:S(2)}, u32[]{:S(2)}) %all-to-all-start.1) | async-done | bytes 131104 | tf_op jit(solution)/shard_map/all_to_all | solution.py:71
  40.8 20.7 %all-gather.2.cloned.1.call-done = bf16[1024,1024]{1,0:T(8,128)(2,1)} async-done(((bf16[1024,256]{1,0:T(8,128)(2,1)}), bf16[1024,1024]{1,0:T(8,128)(2,1)}) %all-gather.2.cloned.1.call-update) | async-done | bytes 2097168 | tf_op jit(solution)/shard_map/all_gather | solution.py:70
  61.5 4.5 %multiply_convert_fusion.3 = bf16[4,128,2,1024]{3,1,2,0:T(8,128)(2,1)S(1)} fusion(bf16[1024,1024]{1,0:T(8,128)(2,1)} %all-gather.2.cloned.1.call-done, f32[128]{0:T(128)S(1)} %get-tuple-element.9, bf16[8,2,4,1024]{3,0,1,2:T(8,128)(2,1)S(1)} %bitcast.111, pred[4,128]{1,0:T(4,128)(4,1)S(1)} %get-tuple-element.16, bf16[4,512,8]{1,2,0:T(8,128)(2,1)S(1)} %copy-done.1), kind=kOutput, calls=%fused_computation.8 | convolution fusion | flops 2168455168 | bytes 4334592 | tf_op jit(solution)/shard_map/slrc,cd->slrd/dot_general | solution.py:34
  66.0 0.4 fusion.43
  66.4 4.6 %multiply_convert_fusion.2 = bf16[4,128,2,1024]{3,1,2,0:T(8,128)(2,1)S(1)} fusion(bf16[1024,1024]{1,0:T(8,128)(2,1)} %all-gather.2.cloned.1.call-done, f32[128]{0:T(128)S(1)} %get-tuple-element.8, bf16[8,2,4,1024]{3,0,1,2:T(8,128)(2,1)S(1)} %bitcast.112, pred[4,128]{1,0:T(4,128)(4,1)S(1)} %get-tuple-element.14, bf16[4,512,8]{1,2,0:T(8,128)(2,1)S(1)} %copy-done.1), kind=kOutput, calls=%fused_computation.6 | convolution fusion | flops 2168455168 | bytes 4334592 | tf_op jit(solution)/shard_map/slrc,cd->slrd/dot_general | solution.py:34
  71.0 0.4 convolution_add_fusion.2
  71.4 4.5 %multiply_convert_fusion.1 = bf16[4,128,2,1024]{3,1,2,0:T(8,128)(2,1)S(1)} fusion(bf16[1024,1024]{1,0:T(8,128)(2,1)} %all-gather.2.cloned.1.call-done, f32[128]{0:T(128)S(1)} %get-tuple-element.10, bf16[8,2,4,1024]{3,0,1,2:T(8,128)(2,1)S(1)} %bitcast.113, pred[4,128]{1,0:T(4,128)(4,1)S(1)} %get-tuple-element.15, bf16[4,512,8]{1,2,0:T(8,128)(2,1)S(1)} %copy-done.1), kind=kOutput, calls=%fused_computation.4 | convolution fusion | flops 2168455168 | bytes 4334592 | tf_op jit(solution)/shard_map/slrc,cd->slrd/dot_general | solution.py:34
  75.9 0.4 convolution_add_fusion.1
  76.3 4.6 %multiply_convert_fusion = bf16[4,128,2,1024]{3,1,2,0:T(8,128)(2,1)S(1)} fusion(bf16[1024,1024]{1,0:T(8,128)(2,1)} %all-gather.2.cloned.1.call-done, f32[128]{0:T(128)S(1)} %get-tuple-element.7, bf16[8,2,4,1024]{3,0,1,2:T(8,128)(2,1)S(1)} %bitcast.114, pred[4,128]{1,0:T(4,128)(4,1)S(1)} %get-tuple-element.13, bf16[4,512,8]{1,2,0:T(8,128)(2,1)S(1)} %copy-done.1), kind=kOutput, calls=%fused_computation.2 | convolution fusion | flops 2168455168 | bytes 4334592 | tf_op jit(solution)/shard_map/slrc,cd->slrd/dot_general | solution.py:34
  80.9 0.6 fusion.19
  81.4 0.8 copy.56
  82.2 3.9 %all-to-all-start.2 = ((bf16[8,2,4,1024]{3,1,2,0:T(2,128)(2,1)}), bf16[8,2,4,1024]{3,1,2,0:T(2,128)(2,1)S(1)}, u32[]{:S(2)}, u32[]{:S(2)}) async-start(bf16[8,2,4,1024]{3,1,2,0:T(2,128)(2,1)} %copy.56), calls=%async_computation.2 | async-start | bytes 262144 | tf_op jit(solution)/shard_map/all_to_all | solution.py:80
  86.2 6.1 %all-to-all-done.2 = bf16[8,2,4,1024]{3,1,2,0:T(2,128)(2,1)S(1)} async-done(((bf16[8,2,4,1024]{3,1,2,0:T(2,128)(2,1)}), bf16[8,2,4,1024]{3,1,2,0:T(2,128)(2,1)S(1)}, u32[]{:S(2)}, u32[]{:S(2)}) %all-to-all-start.2) | async-done | bytes 131104 | tf_op jit(solution)/shard_map/all_to_all | solution.py:80
  92.3 0.1 copy.57
  92.4 0.8 copy.58
  93.2 1.7 %reshape.361 = bf16[4,2,8192]{2,1,0:T(2,128)(2,1)} reshape(bf16[1024,2,2,16]{3,2,1,0:T(2,128)(2,1)S(1)} %bitcast.103) | data formatting | bytes 262144
  94.9 3.3 %all-to-all-start.3 = ((bf16[4,2,8192]{2,1,0:T(2,128)(2,1)}), bf16[4,2,8192]{2,1,0:T(2,128)(2,1)S(1)}, u32[]{:S(2)}, u32[]{:S(2)}) async-start(bf16[4,2,8192]{2,1,0:T(2,128)(2,1)} %reshape.361), calls=%async_computation.3 | async-start | bytes 262144 | tf_op jit(solution)/shard_map/all_to_all | solution.py:79
  98.3 1.9 %multiply_convert_fusion.6 = (bf16[1440,64]{0,1:T(8,128)(2,1)S(1)}, bf16[1440,64]{0,1:T(8,128)(2,1)S(1)}) fusion(f32[64]{0:T(128)S(1)} %get-tuple-element.5, s32[64]{0:T(128)S(1)} %get-tuple-element.6, f32[64]{0:T(128)S(1)} %negate_multiply_fusion), kind=kLoop, calls=%fused_computation.53 | loop fusion | flops 1198080 | bytes 369408 | tf_op jit(solution)/shard_map/convert.3
  100.1 2.7 %all-to-all-done.3 = bf16[4,2,8192]{2,1,0:T(2,128)(2,1)S(1)} async-done(((bf16[4,2,8192]{2,1,0:T(2,128)(2,1)}), bf16[4,2,8192]{2,1,0:T(2,128)(2,1)S(1)}, u32[]{:S(2)}, u32[]{:S(2)}) %all-to-all-start.3) | async-done | bytes 131104 | tf_op jit(solution)/shard_map/all_to_all | solution.py:79
  102.9 0.7 reshape.362
  103.6 1.4 %copy.75 = bf16[2,2,16,4,256]{4,3,2,1,0:T(4,128)(2,1)S(1)} copy(bf16[2,2,16,4,256]{2,1,0,4,3:T(2,128)(2,1)S(1)} %bitcast.104) | data formatting | bytes 262144 | tf_op jit(solution)/shard_map/all_to_all | solution.py:79
  105.0 2.4 %fusion.8 = bf16[2,1440,256]{2,1,0:T(8,128)(2,1)} fusion(bf16[2,128,256]{2,1,0:T(8,128)(2,1)S(1)} %bitcast.115, bf16[2,1440,256]{2,1,0:T(8,128)(2,1)S(1)} %copy-done.3, bf16[1440,64]{0,1:T(8,128)(2,1)S(1)} %get-tuple-element.12, bf16[1440,64]{0,1:T(8,128)(2,1)S(1)} %get-tuple-element.11), kind=kOutput, calls=%fused_computation.19 | convolution fusion | flops 197591040 | bytes 3448832 | tf_op jit(solution)/shard_map/anc,kn->akc/dot_general | solution.py:90
  (24 shorter events, 0.4 us)
Async XLA Ops:
  6.5 12.4 %copy-start = (s32[64]{0:T(128)S(1)}, s32[64]{0:T(128)}, u32[]{:S(2)}) copy-start(s32[64]{0:T(128)} %param.9) | copy-start | bytes 772
  6.5 13.3 %copy-start.2 = (f32[512]{0:T(512)S(1)}, f32[512]{0:T(512)}, u32[]{:S(2)}) copy-start(f32[512]{0:T(512)} %param.8) | copy-start | bytes 6148
  6.5 55.0 %all-gather.2.cloned.1.call-start = ((), (), s32[]{:S(2)}) async-start(), calls=%async_computation.4 | async-start | bytes 2621440 | tf_op jit(solution)/shard_map/all_gather | solution.py:70
  9.8 51.7 %copy-start.1 = (bf16[4,512,8]{1,2,0:T(8,128)(2,1)S(1)}, bf16[4,512,8]{1,2,0:T(8,128)(2,1)}, u32[]{:S(2)}) copy-start(bf16[4,512,8]{1,2,0:T(8,128)(2,1)} %param.6) | copy-start | bytes 98308
  12.3 19.7 %all-to-all-start = ((bf16[2,2,64,256]{3,1,0,2:T(2,128)(2,1)}), bf16[2,2,64,256]{3,1,0,2:T(2,128)(2,1)S(1)}, u32[]{:S(2)}, u32[]{:S(2)}) async-start(bf16[2,2,64,256]{3,1,0,2:T(2,128)(2,1)} %copy.47), calls=%async_computation | async-start | bytes 262144 | tf_op jit(solution)/shard_map/all_to_all | solution.py:72
  32.9 7.9 %all-to-all-start.1 = ((bf16[8,2,16,256]{3,1,0,2:T(2,128)(2,1)}), bf16[8,2,16,256]{3,1,0,2:T(2,128)(2,1)S(1)}, u32[]{:S(2)}, u32[]{:S(2)}) async-start(bf16[8,2,16,256]{3,1,0,2:T(2,128)(2,1)} %copy.50), calls=%async_computation.1 | async-start | bytes 262144 | tf_op jit(solution)/shard_map/all_to_all | solution.py:71
  82.2 10.0 %all-to-all-start.2 = ((bf16[8,2,4,1024]{3,1,2,0:T(2,128)(2,1)}), bf16[8,2,4,1024]{3,1,2,0:T(2,128)(2,1)S(1)}, u32[]{:S(2)}, u32[]{:S(2)}) async-start(bf16[8,2,4,1024]{3,1,2,0:T(2,128)(2,1)} %copy.56), calls=%async_computation.2 | async-start | bytes 262144 | tf_op jit(solution)/shard_map/all_to_all | solution.py:80
  93.2 11.8 %copy-start.3 = (bf16[2,1440,256]{2,1,0:T(8,128)(2,1)S(1)}, bf16[2,1440,256]{2,1,0:T(8,128)(2,1)}, u32[]{:S(2)}) copy-start(bf16[2,1440,256]{2,1,0:T(8,128)(2,1)} %param.5) | copy-start | bytes 4423684
  94.9 7.9 %all-to-all-start.3 = ((bf16[4,2,8192]{2,1,0:T(2,128)(2,1)}), bf16[4,2,8192]{2,1,0:T(2,128)(2,1)S(1)}, u32[]{:S(2)}, u32[]{:S(2)}) async-start(bf16[4,2,8192]{2,1,0:T(2,128)(2,1)} %reshape.361), calls=%async_computation.3 | async-start | bytes 262144 | tf_op jit(solution)/shard_map/all_to_all | solution.py:79
Sparse Core Ops, SparseCore 0:
  8.9 52.5 all-gather.1
where the time goes:
time: 115 us; the launch traced here: 114 us
  waiting for transfers between devices  47 us (41%)
  matrix products  24.1 us (21%)
  starting transfers between devices  16.9 us (15%)
  between operations  13.6 us (12%)
  local copies, waits for them, and re-layouts  8.12 us (7%)
  other arithmetic  4.56 us (4%)
    all_gather x1, waiting for transfers between devices, shards(): weights_full = lax.all_gather(mix_weight, 'lat', axis=1, tiled=True)  20.7 us
    dot_general x4, matrix products, mix_degrees(): jnp.einsum('slrc,cd->slrd', coefficients, weights_full, preferred_element...  18.2 us
    all_to_all x1, waiting for transfers between devices, shards(): lax.all_to_all(spectrum, 'lat', split_axis=2, concat_axis=0, tiled=True)  12.2 us
    all_to_all x1, starting transfers between devices, shards(): lax.all_to_all(spectrum, 'lat', split_axis=2, concat_axis=0, tiled=True)  6.32 us
    all_to_all x1, waiting for transfers between devices, shards(): lax.all_to_all(synthesis, 'lat', split_axis=0, concat_axis=2, tiled=True)  6.09 us
    all_to_all x1, waiting for transfers between devices, shards(): lax.all_to_all(lax.all_to_all(spectrum, 'lat', split_axis=2, concat_axis=...  4.58 us
    another operation x2, other arithmetic  4.37 us
    all_to_all x1, starting transfers between devices, shards(): lax.all_to_all(synthesis, 'lat', split_axis=0, concat_axis=2, tiled=True)  3.95 us
  transfers between devices with their start and end apart: 5, of which 5 were waited for; matrix products, arithmetic and copies ran while one was open for 8% of the time, Pallas kernels for 0%

commit v1 on v0

v1 whole, which is shorter than its diff:
```python
import functools
import math

import jax
import jax.numpy as jnp
import numpy as np
from jax import lax
from jax.experimental import pallas as pl
from jax.experimental.pallas import tpu as pltpu
from jax.sharding import PartitionSpec as P

LATITUDE_ROWS = 16


def transform_table(orders, longitudes):
    residue = np.arange(longitudes)[:, None] * np.arange(orders)[None, :] % longitudes
    angle = residue.astype(np.float32) * np.float32(2.0 * math.pi / longitudes)
    scale = np.float32(1.0 / math.sqrt(longitudes))
    return np.concatenate([np.cos(angle) * scale, -np.sin(angle) * scale], axis=1).astype(jnp.bfloat16)


def slot_of_row(lat_count, chan_count, slot_count):
    slots = np.arange(lat_count * chan_count * slot_count).reshape(lat_count, chan_count, slot_count)
    groups = slots.transpose(1, 0, 2).reshape(chan_count, 1, -1)
    return np.broadcast_to(groups, (chan_count, 2, groups.shape[2])).reshape(-1)


def place_matrix(lat_count, chan_count, slot_count):
    slots = slot_of_row(lat_count, chan_count, slot_count)
    orders = lat_count * chan_count * slot_count
    part = np.arange(2 * orders) // (orders // chan_count) % 2
    hit = np.arange(orders)[:, None] == slots[None, :]
    return np.stack([hit & (part == 0), hit & (part == 1)]).astype(jnp.bfloat16)


def order_rows(order_ref, place_ref, weighted):
    orders = order_ref.shape[1]
    natural = lax.broadcasted_iota(jnp.int32, (orders, orders), 0)
    value = jnp.where(natural == 0, 1.0, 2.0) if weighted else 1.0
    held = jnp.where(natural == order_ref[...], value, 0.0).astype(jnp.bfloat16)
    halves = [jnp.dot(held, place_ref[r], preferred_element_type=jnp.float32) for r in range(2)]
    return jnp.concatenate(halves, axis=0).astype(jnp.bfloat16)


def analysis_kernel(factor, grid_ref, table_ref, order_ref, place_ref, legendre_ref, gain_ref, slot_ref, rows_ref, pair_ref):
    chan_count, _, group_rows, channels = rows_ref.shape
    spectrum = jnp.dot(table_ref[...], grid_ref[0], preferred_element_type=jnp.float32)
    rows = lax.dot_general(
        order_rows(order_ref, place_ref, False),
        spectrum.astype(jnp.bfloat16),
        (((0,), (0,)), ((), ())),
        preferred_element_type=jnp.float32,
    )
    rows_ref[:, 0] = rows.astype(jnp.bfloat16).reshape(chan_count, group_rows, channels)

    @pl.when(pl.program_id(0) == 0)
    def _():
        slot_count, latitudes, degrees = legendre_ref.shape
        own = (lax.axis_index("lat") * lax.axis_size("chan") + lax.axis_index("chan")) * slot_count
        block = lax.broadcasted_iota(jnp.int32, (latitudes, degrees), 1) // 64
        pieces = []
        for s in range(slot_count):
            alive = block >= slot_ref[own + s] // 64
            degree_rows = legendre_ref[s].astype(jnp.float32)
            pair = lax.dot_general(
                jnp.where(alive, degree_rows * (gain_ref[...] * factor), 0.0),
                degree_rows,
                (((1,), (1,)), ((), ())),
                precision=lax.Precision.HIGHEST,
                preferred_element_type=jnp.float32,
            )
            high = pair.astype(jnp.bfloat16)
            pieces += [high.astype(jnp.float32), pair - high.astype(jnp.float32)]
        pairs = jnp.concatenate(pieces, axis=1)
        spare = pair_ref.shape[0] - latitudes
        if spare:
            pairs = jnp.concatenate([pairs, jnp.zeros((spare, pairs.shape[1]), jnp.float32)], axis=0)
        pair_ref[...] = pairs.astype(jnp.bfloat16)


def mixing_matrices(lat_count, lat_dev, slots_here, slot_count):
    latitudes = lat_count * lat_dev
    row = np.arange(latitudes * 2 * slots_here)
    t, r, s = row // (2 * slots_here), row // slots_here % 2, row % slots_here
    owner, place = s // slot_count, s % slot_count
    lane = np.arange(slot_count * 2 * latitudes)
    lane_place, lane_t = lane // (2 * latitudes), lane % latitudes
    take = np.arange(lat_count * LATITUDE_ROWS)[None, :] == (owner * LATITUDE_ROWS + t)[:, None]
    own = place[:, None] == lane_place[None, :]
    spread = lane_t[:, None] == t[None, :]
    same = (s[:, None] == s[None, :]) & (r[:, None] == r[None, :])
    return [m.astype(jnp.bfloat16) for m in (take, own, spread, same)]


def mixing_kernel(rows_ref, pair_ref, weight_ref, take_ref, own_ref, spread_ref, same_ref, mixed_ref):
    lat_count, chan_count, part_rows, channels = rows_ref.shape
    count = lat_count * part_rows
    mixed = jnp.zeros((count, weight_ref.shape[1]), jnp.float32)
    for b in range(chan_count):
        mixed = mixed + jnp.dot(
            rows_ref[:, b].reshape(count, channels),
            weight_ref[b * channels : (b + 1) * channels, :],
            preferred_element_type=jnp.float32,
        )
    pairs = pair_ref[...].reshape(lat_count * pair_ref.shape[1], pair_ref.shape[2])
    taken = jnp.dot(take_ref[...], pairs, preferred_element_type=jnp.float32) * own_ref[...].astype(jnp.float32)
    matrix = jnp.dot(taken.astype(jnp.bfloat16), spread_ref[...], preferred_element_type=jnp.float32)
    matrix = matrix * same_ref[...].astype(jnp.float32)
    synthesis = jnp.dot(matrix, mixed, precision=lax.Precision.HIGHEST, preferred_element_type=jnp.float32)
    mixed_ref[...] = synthesis.astype(jnp.bfloat16).reshape(mixed_ref.shape)


def mixing_plain(rows, pairs, weight, lat_dev, slots_here, slot_count):
    lat_count, chan_count, _, channels = rows.shape
    latitudes = lat_count * lat_dev
    wide = pairs[:, :latitudes].astype(jnp.float32).reshape(lat_count, latitudes, slot_count, 2, latitudes)
    matrix = wide.sum(axis=3).transpose(0, 2, 1, 3).reshape(slots_here, latitudes, latitudes)
    mixed = jnp.einsum(
        "abnc,bcd->and", rows, weight.reshape(chan_count, channels, -1), preferred_element_type=jnp.float32
    ).reshape(latitudes, 2, slots_here, -1)
    synthesis = jnp.einsum(
        "svt,trsd->vrsd", matrix, mixed, precision=lax.Precision.HIGHEST, preferred_element_type=jnp.float32
    )
    return synthesis.astype(jnp.bfloat16).reshape(lat_count, lat_dev * 2 * slots_here, -1)


def synthesis_kernel(rows_ref, grid_ref, table_ref, order_ref, place_ref, out_ref):
    chan_count, _, group_rows, channels = rows_ref.shape
    rows = rows_ref[...].reshape(chan_count * group_rows, channels)
    natural = jnp.dot(order_rows(order_ref, place_ref, True), rows, preferred_element_type=jnp.float32)
    field = jnp.dot(table_ref[...], natural.astype(jnp.bfloat16), preferred_element_type=jnp.float32)
    inner = math.sqrt(2.0 / math.pi) * (field + 0.044715 * (field * field * field))
    out_ref[0] = (grid_ref[0].astype(jnp.float32) + 0.5 * field * (1.0 + jnp.tanh(inner))).astype(jnp.bfloat16)


def shards(grid_input, legendre, mix_weight, degree_gain, order_slot):
    lat_dev, longitudes, chan_dev = grid_input.shape
    orders = order_slot.shape[0]
    slot_count, degrees, latitudes = legendre.shape
    lat_count = lax.axis_size("lat")
    chan_count = lax.axis_size("chan")
    slots_here = lat_count * slot_count
    group_rows = 2 * slots_here
    pair_rows = max(latitudes, LATITUDE_ROWS)
    pair_lanes = slot_count * 2 * latitudes
    params = pltpu.CompilerParams(vmem_limit_bytes=40 * 1024 * 1024)

    table = transform_table(orders, longitudes)
    place = jnp.asarray(place_matrix(lat_count, chan_count, slot_count))
    order_row = order_slot.reshape(1, orders)
    whole = lambda shape: pl.BlockSpec(shape, lambda *_: (0,) * len(shape))

    rows, pairs = pl.pallas_call(
        functools.partial(analysis_kernel, math.sqrt(latitudes / degrees)),
        grid=(lat_dev,),
        in_specs=[
            pl.BlockSpec((1, longitudes, chan_dev), lambda t: (t, 0, 0)),
            whole((2 * orders, longitudes)),
            whole((1, orders)),
            whole(place.shape),
            whole((slot_count, latitudes, degrees)),
            whole((1, degrees)),
            pl.BlockSpec(memory_space=pltpu.SMEM),
        ],
        out_specs=[
            pl.BlockSpec((chan_count, 1, group_rows, chan_dev), lambda t: (0, t, 0, 0)),
            whole((pair_rows, pair_lanes)),
        ],
        out_shape=[
            jax.ShapeDtypeStruct((chan_count, lat_dev, group_rows, chan_dev), jnp.bfloat16),
            jax.ShapeDtypeStruct((pair_rows, pair_lanes), jnp.bfloat16),
        ],
        compiler_params=params,
    )(
        grid_input,
        jnp.asarray(np.ascontiguousarray(table.T)),
        order_row,
        place,
        jnp.swapaxes(legendre, 1, 2),
        degree_gain.reshape(1, degrees),
        order_slot,
    )

    rows = rows.reshape(chan_count, lat_dev * group_rows, chan_dev)
    rows = lax.all_to_all(rows, "chan", split_axis=0, concat_axis=0, tiled=True)
    rows, pairs = lax.all_gather((rows, pairs), "lat", axis=0, tiled=False)

    count = latitudes * group_rows
    if count <= 512 and latitudes <= LATITUDE_ROWS:
        helpers = [jnp.asarray(m) for m in mixing_matrices(lat_count, lat_dev, slots_here, slot_count)]
        mixed = pl.pallas_call(
            mixing_kernel,
            out_shape=jax.ShapeDtypeStruct((lat_count, lat_dev * group_rows, mix_weight.shape[1]), jnp.bfloat16),
            compiler_params=params,
        )(rows, pairs, mix_weight, *helpers)
    else:
        mixed = mixing_plain(rows, pairs, mix_weight, lat_dev, slots_here, slot_count)

    back = lax.all_to_all(mixed, "lat", split_axis=0, concat_axis=0, tiled=True)
    if mix_weight.shape[1] != chan_dev:
        back = back.transpose(1, 0, 2).reshape(lat_dev * group_rows, chan_count, chan_dev).transpose(1, 0, 2)
    back = lax.all_to_all(back, "chan", split_axis=0, concat_axis=0, tiled=True)
    back = back.reshape(chan_count, lat_dev, group_rows, chan_dev)

    return pl.pallas_call(
        synthesis_kernel,
        grid=(lat_dev,),
        in_specs=[
            pl.BlockSpec((chan_count, 1, group_rows, chan_dev), lambda t: (0, t, 0, 0)),
            pl.BlockSpec((1, longitudes, chan_dev), lambda t: (t, 0, 0)),
            whole((longitudes, 2 * orders)),
            whole((1, orders)),
            whole(place.shape),
        ],
        out_specs=pl.BlockSpec((1, longitudes, chan_dev), lambda t: (t, 0, 0)),
        out_shape=jax.ShapeDtypeStruct(grid_input.shape, jnp.bfloat16),
        compiler_params=params,
    )(back, grid_input, jnp.asarray(table), order_row, place)


def solution(mesh):
    placed = (
        P(("groups", "lat"), None, "chan"),
        P(("lat", "chan"), None, None),
        P(None, "lat"),
        P(),
        P(),
    )
    return jax.shard_map(
        shards,
        mesh=mesh,
        in_specs=placed,
        out_specs=P(("groups", "lat"), None, "chan"),
        check_vma=False,
    )
```

time: 115 us -> 63.3 us (0.55)
  waiting for transfers between devices: 47 us -> 0.01 us
  blocking collectives: 0 us -> 46.9 us
  matrix products: 24.1 us -> 0 us
  between operations: 13.6 us -> 0.07 us
  starting transfers between devices: 16.9 us -> 4.35 us
  Pallas kernels: 0 us -> 6.21 us
  other arithmetic: 4.56 us -> 0 us
  local copies, waits for them, and re-layouts: 8.12 us -> 5.25 us
    all_gather x0 -> x2, blocking collectives: none -> 29.4 us  [shards(): rows, pairs = lax.all_gather((rows, pairs), 'lat', axis=0, tiled=False)]
    all_to_all x4 -> x1, waiting for transfers between devices: 25.6 us -> 0.01 us  [shards(): rows = lax.all_to_all(rows, 'chan', split_axis=0, concat_axis=0, tiled=True)]
    dot_general x10 -> x0, matrix products: 24.1 us -> none  [the longest x4 18.2 us: mix_degrees(): jnp.einsum('slrc,cd->slrd', coefficients, weights_full, preferred_element...]
    all_gather x1 -> x0, waiting for transfers between devices: 20.7 us -> none  [shards(): weights_full = lax.all_gather(mix_weight, 'lat', axis=1, tiled=True)]
    all_to_all x0 -> x2, blocking collectives: none -> 17.5 us  [the longest x1 9.83 us: shards(): back = lax.all_to_all(mixed, 'lat', split_axis=0, concat_axis=0, tiled=True)]
    all_to_all x4 -> x1, starting transfers between devices: 16.9 us -> 4.35 us  [shards(): rows = lax.all_to_all(rows, 'chan', split_axis=0, concat_axis=0, tiled=True)]
    pallas_call x0 -> x3, Pallas kernels: none -> 6.21 us  [the longest x1 2.82 us: shards(): pl.pallas_call(synthesis_kernel, grid=(lat_dev,), in_specs=[pl.BlockSpec(...]
    another operation x2 -> x0, other arithmetic: 4.37 us -> none
  transfers between devices with their start and end apart: 5 -> 1, of which waited for: 5 -> 0; matrix products, arithmetic and copies ran while one was open for 8% -> 0% of each run, Pallas kernels for 0% -> 0%
where the time goes in v1:
time: 63.3 us; the launch traced here: 62.8 us
  blocking collectives  46.9 us (74%)
  Pallas kernels  6.21 us (10%)
  local copies, waits for them, and re-layouts  5.25 us (8%)
  starting transfers between devices  4.35 us (7%)
    all_gather x2, blocking collectives, shards(): rows, pairs = lax.all_gather((rows, pairs), 'lat', axis=0, tiled=False)  29.4 us
    all_to_all x1, blocking collectives, shards(): back = lax.all_to_all(mixed, 'lat', split_axis=0, concat_axis=0, tiled=True)  9.83 us
    all_to_all x1, blocking collectives, shards(): back = lax.all_to_all(back, 'chan', split_axis=0, concat_axis=0, tiled=True)  7.67 us
    unnamed x30, local copies, waits for them, and re-layouts  5.25 us
    all_to_all x1, starting transfers between devices, shards(): rows = lax.all_to_all(rows, 'chan', split_axis=0, concat_axis=0, tiled=True)  4.35 us
    pallas_call x1, Pallas kernels, shards(): pl.pallas_call(synthesis_kernel, grid=(lat_dev,), in_specs=[pl.BlockSpec(...  2.82 us
    pallas_call x1, Pallas kernels, shards(): pl.pallas_call(functools.partial(analysis_kernel, math.sqrt(latitudes / d...  2.46 us
  transfers between devices with their start and end apart: 1, of which 0 were waited for; matrix products, arithmetic and copies ran while one was open for 0% of the time, Pallas kernels for 0%

profile of v1, /device:TPU:0, one launch (start us, length us, event | category | flops | bytes accessed | tf_op | source)
XLA Modules:
  0.0 62.8 jit_solution(10023915596143686930)
XLA Ops:
  0.0 0.0 copy-start
  0.0 1.4 %copy-done = bf16[2,1440,256]{2,1,0:T(8,128)(2,1)S(1)} copy-done((bf16[2,1440,256]{2,1,0:T(8,128)(2,1)S(1)}, bf16[2,1440,256]{2,1,0:T(8,128)(2,1)}, u32[]{:S(2)}) %copy-start) | copy-done | bytes 1474584
  1.4 1.0 %copy-done.3 = bf16[128,1440]{1,0:T(8,128)(2,1)S(1)} copy-done((bf16[128,1440]{1,0:T(8,128)(2,1)S(1)}, bf16[128,1440]{1,0:T(8,128)(2,1)}, u32[]{:S(2)}) %copy-start.3) | copy-done | bytes 368664
  2.4 0.0 copy-start.5
  2.4 0.8 %copy-done.5 = bf16[2,64,128]{2,1,0:T(8,128)(2,1)S(1)} copy-done((bf16[2,64,128]{2,1,0:T(8,128)(2,1)S(1)}, bf16[2,64,128]{2,1,0:T(8,128)(2,1)}, u32[]{:S(2)}) %copy-start.5) | copy-done | bytes 32792
  3.1 0.0 copy-start.10
  3.1 0.8 %copy-done.10 = bf16[4,512,8]{1,2,0:T(8,128)(2,1)S(1)} copy-done((bf16[4,512,8]{1,2,0:T(8,128)(2,1)S(1)}, bf16[4,512,8]{1,2,0:T(8,128)(2,1)}, u32[]{:S(2)}) %copy-start.10) | copy-done | bytes 32792
  3.9 0.0 copy-start.12
  3.9 0.7 %copy-done.12 = s32[64]{0:T(128)S(1)} copy-done((s32[64]{0:T(128)S(1)}, s32[64]{0:T(128)}, u32[]{:S(2)}) %copy-start.12) | copy-done | bytes 280
  4.5 0.0 copy-start.14
  4.5 0.7 %copy-done.14 = f32[512]{0:T(512)S(1)} copy-done((f32[512]{0:T(512)S(1)}, f32[512]{0:T(512)}, u32[]{:S(2)}) %copy-start.14) | copy-done | bytes 2072
  5.2 0.0 copy-start.2
  5.2 0.0 copy-start.7
  5.2 0.0 copy-start.11
  5.2 2.5 %shard_map.118 = (bf16[4,2,32,256]{3,2,1,0:T(8,128)(2,1)}, bf16[16,64]{1,0:T(8,128)(2,1)S(1)}) custom-call(bf16[2,1440,256]{2,1,0:T(8,128)(2,1)S(1)} %copy-done, bf16[128,1440]{1,0:T(8,128)(2,1)S(1)} %copy-done.3, s32[1,64]{1,0:T(1,128)S(1)} %bitcast.11, bf16[2,64,128]{2,1,0:T(8,128)(2,1)S(1)} %copy-done.5, bf16[4,8,512]{2,1,0:T(8,128)(2,1)S(1)} %bitcast.10, ...), custom_call_target="tpu_custom_call" | custom-call | tf_op jit(solution)/shard_map/pallas_call | solution.py:153
  7.7 4.4 %all-to-all-start = ((bf16[4,64,256]{2,1,0:T(8,128)(2,1)}), bf16[4,64,256]{2,1,0:T(8,128)(2,1)S(1)}, u32[]{:S(2)}, u32[]{:S(2)}) async-start(bf16[4,64,256]{2,1,0:T(8,128)(2,1)} %bitcast.3), calls=%async_computation | async-start | bytes 262144 | tf_op jit(solution)/shard_map/all_to_all | solution.py:185
  12.1 13.9 %all-gather.1 = bf16[64,64]{1,0:T(8,128)(2,1)S(1)} all-gather(bf16[16,64]{1,0:T(8,128)(2,1)S(1)} %get-tuple-element.8), channel_id=3, replica_groups=mesh['groups'=2,'lat'=4,'chan'=4] {'lat'}, dimensions={0}, use_global_device_ids=true | all-gather | bytes 10240 | tf_op jit(solution)/shard_map/all_gather | solution.py:186
  26.0 0.0 all-to-all-done
  26.0 15.5 %all-gather = bf16[16,64,256]{2,1,0:T(8,128)(2,1)S(1)} all-gather(bf16[4,64,256]{2,1,0:T(8,128)(2,1)S(1)} %all-to-all-done), channel_id=2, replica_groups=mesh['groups'=2,'lat'=4,'chan'=4] {'lat'}, dimensions={0}, use_global_device_ids=true | all-gather | bytes 655360 | tf_op jit(solution)/shard_map/all_gather | solution.py:186
  41.5 0.0 copy-done.2
  41.5 0.0 copy-done.7
  41.5 0.0 copy-done.8
  41.5 0.0 copy-done.9
  41.5 0.0 copy-done.11
  41.5 0.9 %shard_map.119 = bf16[4,64,256]{2,1,0:T(8,128)(2,1)S(1)} custom-call(bf16[4,4,64,256]{3,2,1,0:T(8,128)(2,1)S(1)} %bitcast.7, bf16[4,16,64]{2,1,0:T(8,128)(2,1)S(1)} %bitcast.9, bf16[1024,256]{1,0:T(8,128)(2,1)S(1)} %copy-done.2, bf16[256,64]{1,0:T(8,128)(2,1)S(1)} %copy-done.9, bf16[256,64]{1,0:T(8,128)(2,1)S(1)} %copy-done.8, ...), custom_call_target="tpu_custom_call" | custom-call | tf_op jit(solution)/shard_map/pallas_call | solution.py:191
  42.4 9.8 %all_to_all.15 = bf16[4,64,256]{2,1,0:T(8,128)(2,1)S(1)} all-to-all(bf16[4,64,256]{2,1,0:T(8,128)(2,1)S(1)} %shard_map.119), channel_id=1, replica_groups=mesh['groups'=2,'lat'=4,'chan'=4] {'lat'}, dimensions={0} | all-to-all | bytes 262144 | tf_op jit(solution)/shard_map/all_to_all | solution.py:199
  52.3 7.7 %all_to_all.16 = bf16[4,64,256]{2,1,0:T(8,128)(2,1)S(1)} all-to-all(bf16[4,64,256]{2,1,0:T(8,128)(2,1)S(1)} %all_to_all.15), channel_id=1, replica_groups=mesh['groups'=2,'lat'=4,'chan'=4] {'chan'}, dimensions={0} | all-to-all | bytes 262144 | tf_op jit(solution)/shard_map/all_to_all | solution.py:202
  59.9 0.0 copy-done.1
  60.0 0.0 copy-done.4
  60.0 0.0 copy-done.6
  60.0 0.0 copy-done.13
  60.0 2.8 %shard_map.120 = bf16[2,1440,256]{2,1,0:T(8,128)(2,1)} custom-call(bf16[4,2,32,256]{3,2,1,0:T(8,128)(2,1)S(1)} %bitcast.8, bf16[2,1440,256]{2,1,0:T(8,128)(2,1)S(1)} %copy-done.1, bf16[1440,128]{1,0:T(8,128)(2,1)S(1)} %copy-done.4, s32[1,64]{1,0:T(1,128)S(1)} %bitcast.12, bf16[2,64,128]{2,1,0:T(8,128)(2,1)S(1)} %copy-done.6), custom_call_target="tpu_custom_call" | custom-call | tf_op jit(solution)/shard_map/pallas_call | solution.py:205
  (7 shorter events, 0.0 us)
Async XLA Ops:
  0.0 1.4 %copy-start = (bf16[2,1440,256]{2,1,0:T(8,128)(2,1)S(1)}, bf16[2,1440,256]{2,1,0:T(8,128)(2,1)}, u32[]{:S(2)}) copy-start(bf16[2,1440,256]{2,1,0:T(8,128)(2,1)} %grid_ref.3) | copy-start | bytes 4423684
  1.4 1.0 %copy-start.3 = (bf16[128,1440]{1,0:T(8,128)(2,1)S(1)}, bf16[128,1440]{1,0:T(8,128)(2,1)}, u32[]{:S(2)}) copy-start(bf16[128,1440]{1,0:T(8,128)(2,1)} %constant.15.clone.table_ref) | copy-start | bytes 1105924
  2.4 0.8 %copy-start.5 = (bf16[2,64,128]{2,1,0:T(8,128)(2,1)S(1)}, bf16[2,64,128]{2,1,0:T(8,128)(2,1)}, u32[]{:S(2)}) copy-start(bf16[2,64,128]{2,1,0:T(8,128)(2,1)} %constant.14.clone.place_ref) | copy-start | bytes 98308
  3.1 0.8 %copy-start.10 = (bf16[4,512,8]{1,2,0:T(8,128)(2,1)S(1)}, bf16[4,512,8]{1,2,0:T(8,128)(2,1)}, u32[]{:S(2)}) copy-start(bf16[4,512,8]{1,2,0:T(8,128)(2,1)} %param.13) | copy-start | bytes 98308
  3.9 0.7 %copy-start.12 = (s32[64]{0:T(128)S(1)}, s32[64]{0:T(128)}, u32[]{:S(2)}) copy-start(s32[64]{0:T(128)} %slot_ref.1) | copy-start | bytes 772
  4.5 0.7 %copy-start.14 = (f32[512]{0:T(512)S(1)}, f32[512]{0:T(512)}, u32[]{:S(2)}) copy-start(f32[512]{0:T(512)} %param.15) | copy-start | bytes 6148
  5.2 36.3 %copy-start.2 = (bf16[1024,256]{1,0:T(8,128)(2,1)S(1)}, bf16[1024,256]{1,0:T(8,128)(2,1)}, u32[]{:S(2)}) copy-start(bf16[1024,256]{1,0:T(8,128)(2,1)} %weight_ref.1) | copy-start | bytes 1572868
  5.2 36.3 %copy-start.7 = (bf16[256,256]{1,0:T(8,128)(2,1)S(1)}, bf16[256,256]{1,0:T(8,128)(2,1)}, u32[]{:S(2)}) copy-start(bf16[256,256]{1,0:T(8,128)(2,1)} %constant.19.clone.same_ref) | copy-start | bytes 393220
  5.2 36.3 %copy-start.8 = (bf16[256,64]{1,0:T(8,128)(2,1)S(1)}, bf16[256,64]{1,0:T(8,128)(2,1)}, u32[]{:S(2)}) copy-start(bf16[256,64]{1,0:T(8,128)(2,1)} %constant.17.clone.own_ref) | copy-start | bytes 98308
  5.2 36.3 %copy-start.9 = (bf16[256,64]{1,0:T(8,128)(2,1)S(1)}, bf16[256,64]{1,0:T(8,128)(2,1)}, u32[]{:S(2)}) copy-start(bf16[256,64]{1,0:T(8,128)(2,1)} %constant.16.clone.take_ref) | copy-start | bytes 98308
  5.2 36.3 %copy-start.11 = (bf16[64,256]{1,0:T(8,128)(2,1)S(1)}, bf16[64,256]{1,0:T(8,128)(2,1)}, u32[]{:S(2)}) copy-start(bf16[64,256]{1,0:T(8,128)(2,1)} %constant.18.clone.spread_ref) | copy-start | bytes 98308
  7.7 52.2 %copy-start.1 = (bf16[2,1440,256]{2,1,0:T(8,128)(2,1)S(1)}, bf16[2,1440,256]{2,1,0:T(8,128)(2,1)}, u32[]{:S(2)}) copy-start(bf16[2,1440,256]{2,1,0:T(8,128)(2,1)} %grid_ref.3) | copy-start | bytes 4423684
  7.7 52.2 %copy-start.4 = (bf16[1440,128]{1,0:T(8,128)(2,1)S(1)}, bf16[1440,128]{1,0:T(8,128)(2,1)}, u32[]{:S(2)}) copy-start(bf16[1440,128]{1,0:T(8,128)(2,1)} %constant.20.clone.table_ref) | copy-start | bytes 1105924
  7.7 52.2 %copy-start.6 = (bf16[2,64,128]{2,1,0:T(8,128)(2,1)S(1)}, bf16[2,64,128]{2,1,0:T(8,128)(2,1)}, u32[]{:S(2)}) copy-start(bf16[2,64,128]{2,1,0:T(8,128)(2,1)} %constant.14.clone.place_ref) | copy-start | bytes 98308
  7.7 52.2 %copy-start.13 = (s32[64]{0:T(128)S(1)}, s32[64]{0:T(128)}, u32[]{:S(2)}) copy-start(s32[64]{0:T(128)} %slot_ref.1) | copy-start | bytes 772
  7.7 18.3 %all-to-all-start = ((bf16[4,64,256]{2,1,0:T(8,128)(2,1)}), bf16[4,64,256]{2,1,0:T(8,128)(2,1)S(1)}, u32[]{:S(2)}, u32[]{:S(2)}) async-start(bf16[4,64,256]{2,1,0:T(8,128)(2,1)} %bitcast.3), calls=%async_computation | async-start | bytes 262144 | tf_op jit(solution)/shard_map/all_to_all | solution.py:185

commit v2 on v0

v2 whole, which is shorter than its diff:
```python
import functools
import math

import jax
import jax.numpy as jnp
import numpy as np
from jax import lax
from jax.experimental import pallas as pl
from jax.experimental.pallas import tpu as pltpu
from jax.sharding import PartitionSpec as P

MIB = 1024 * 1024


def transform_tables(orders, longitudes):
    residue = np.arange(longitudes)[:, None] * np.arange(orders)[None, :] % longitudes
    angle = residue.astype(np.float32) * np.float32(2.0 * math.pi / longitudes)
    scale = np.float32(1.0 / math.sqrt(longitudes))
    forward = np.concatenate([np.cos(angle) * scale, -np.sin(angle) * scale], axis=1)
    weight = np.where(np.arange(2 * orders) % orders == 0, 1.0, 2.0).astype(np.float32)
    return forward.astype(jnp.bfloat16), (forward * weight).astype(jnp.bfloat16)


def grouped_columns(orders, groups):
    return np.arange(2 * orders).reshape(2, groups, orders // groups).transpose(1, 0, 2).reshape(-1)


def analysis_kernel(
    factor, chunk, grid_hbm, table_hbm, legendre_hbm, gain_hbm, slot_hbm, out_ref,
    grid_buf, table_buf, legendre_buf, gain_buf, slot_buf, grid_sem, table_sem, small_sem,
):
    lat_count, groups, _, _ = out_ref.shape
    lat_dev, longitudes, channels = grid_buf.shape
    slot_count, latitudes, degrees = legendre_buf.shape
    orders = slot_buf.shape[1]
    group_orders = orders // groups
    group_rows = 2 * group_orders
    chunks = longitudes // chunk
    small = [
        pltpu.make_async_copy(src, dst, small_sem.at[i])
        for i, (src, dst) in enumerate(((legendre_hbm, legendre_buf), (gain_hbm, gain_buf), (slot_hbm, slot_buf)))
    ]
    tables = [pltpu.make_async_copy(table_hbm.at[k], table_buf.at[k], table_sem.at[k]) for k in range(chunks)]
    parts = [
        [
            pltpu.make_async_copy(
                grid_hbm.at[t, pl.ds(k * chunk, chunk)], grid_buf.at[t, pl.ds(k * chunk, chunk)], grid_sem.at[t, k]
            )
            for k in range(chunks)
        ]
        for t in range(lat_dev)
    ]
    for copy in small:
        copy.start()
    for k in range(chunks):
        tables[k].start()
        parts[0][k].start()
    for t in range(1, lat_dev):
        for k in range(chunks):
            parts[t][k].start()

    for copy in small:
        copy.wait()
    lanes = 2 * latitudes * latitudes
    own = (lax.axis_index("lat") * lax.axis_size("chan") + lax.axis_index("chan")) * slot_count
    block = lax.broadcasted_iota(jnp.int32, (1, degrees), 1) // 64
    high_lane = lax.broadcasted_iota(jnp.int32, (1, lanes), 1) < lanes // 2
    row = lax.broadcasted_iota(jnp.int32, (group_orders, lanes), 0)
    placed = [jnp.zeros((group_orders, lanes), jnp.float32) for _ in range(groups)]
    for s in range(slot_count):
        order = slot_buf[0, own + s]
        rows = legendre_buf[s].astype(jnp.float32)
        products = [rows * rows[v : v + 1] for v in range(latitudes)] * 2
        weights = jnp.where(block >= order // 64, gain_buf[...] * factor, 0.0)
        pair = lax.dot_general(
            weights,
            jnp.concatenate(products, axis=0),
            (((1,), (1,)), ((), ())),
            precision=lax.Precision.HIGHEST,
            preferred_element_type=jnp.float32,
        )
        high = pair.astype(jnp.bfloat16).astype(jnp.float32)
        pair = jnp.where(high_lane, high, pair - high)
        for g in range(groups):
            placed[g] = jnp.where(row == order - g * group_orders, pair, placed[g])
    top = lat_dev * group_rows * (channels // 128)
    for g in range(groups):
        value = placed[g].astype(jnp.bfloat16)
        for a in range(lat_count):
            out_ref[a, g, top : top + group_orders] = value

    for t in range(lat_dev):
        total = None
        for k in range(chunks):
            if t == 0:
                tables[k].wait()
            parts[t][k].wait()
            term = jnp.dot(
                table_buf[k], grid_buf[t, k * chunk : (k + 1) * chunk, :], preferred_element_type=jnp.float32
            )
            total = term if total is None else total + term
        spectrum = total.astype(jnp.bfloat16)
        for g in range(groups):
            for h in range(channels // 128):
                value = spectrum[g * group_rows : (g + 1) * group_rows, h * 128 : (h + 1) * 128]
                at = (h * lat_dev + t) * group_rows
                for a in range(lat_count):
                    out_ref[a, g, at : at + group_rows] = value


def mixing_helpers(latitudes, group_orders):
    row = np.arange(latitudes * 2 * group_orders)
    t, rm = row // (2 * group_orders), row % (2 * group_orders)
    lane = np.arange(2 * latitudes * latitudes)
    part, lane_v, lane_t = lane // latitudes**2, lane // latitudes % latitudes, lane % latitudes
    keep = t[:, None] == lane_v[None, :]
    spread = lane_t[:, None] == t[None, :]
    halves = np.concatenate([spread & (part == 0)[:, None], spread & (part == 1)[:, None]], axis=1)
    same = rm[:, None] == rm[None, :]
    return [m.astype(jnp.bfloat16) for m in (keep, halves, same)]


def mixing_kernel(lat_dev, rows_ref, weight_ref, keep_ref, halves_ref, same_ref, *out_and_scratch):
    outs, held = out_and_scratch[:-1], out_and_scratch[-1]
    lat_count, chan_count, _, _ = rows_ref.shape
    count = same_ref.shape[0]
    part_rows = count // lat_count
    lanes = keep_ref.shape[1]
    channels = weight_ref.shape[0] // chan_count
    split = channels // 128
    group_orders = rows_ref.shape[2] - split * part_rows
    mixed = None
    pairs = None
    for b in range(chan_count):
        block = jnp.concatenate(
            [rows_ref[:, b, h * part_rows : (h + 1) * part_rows, :].reshape(count, 128) for h in range(split)], axis=1
        )
        term = jnp.dot(
            block, weight_ref[b * channels : (b + 1) * channels, :], preferred_element_type=jnp.float32
        )
        mixed = term if mixed is None else mixed + term
        for a in range(lat_count):
            sent = rows_ref[a, b, split * part_rows :, :].astype(jnp.float32)
            pairs = sent if pairs is None else pairs + sent
    wide = jnp.concatenate([pairs] * (count // group_orders), axis=0) * keep_ref[...].astype(jnp.float32)
    matrix = jnp.dot(wide.astype(jnp.bfloat16), halves_ref[...], preferred_element_type=jnp.float32)
    same = same_ref[...].astype(jnp.float32)
    high = (matrix[:, :count] * same).astype(jnp.bfloat16)
    low = (matrix[:, count:] * same).astype(jnp.bfloat16)
    mixed_high = mixed.astype(jnp.bfloat16)
    mixed_low = (mixed - mixed_high.astype(jnp.float32)).astype(jnp.bfloat16)
    synthesis = (
        jnp.dot(high, mixed_high, preferred_element_type=jnp.float32)
        + jnp.dot(high, mixed_low, preferred_element_type=jnp.float32)
        + jnp.dot(low, mixed_high, preferred_element_type=jnp.float32)
    )
    held[...] = synthesis.astype(jnp.bfloat16).reshape(held.shape)
    for s in range(lat_count):
        outs[s][...] = held[lax.rem(lax.axis_index("chan") + s, lat_count)]


def synthesis_kernel(groups, *refs):
    received = refs[:groups]
    grid_ref, table_ref, out_ref, held = refs[groups:]
    lat_dev = grid_ref.shape[0]
    group_rows = held.shape[2]
    channels = held.shape[3]

    @pl.when(pl.program_id(0) == 0)
    def _():
        for s in range(groups):
            group = lax.rem(lax.axis_index("lat") + groups - s, groups)
            for t in range(lat_dev):
                held[t, group] = received[s][t * group_rows : (t + 1) * group_rows, :]

    for t in range(lat_dev):
        rows = held[t].reshape(groups * group_rows, channels)
        field = jnp.dot(table_ref[...], rows, preferred_element_type=jnp.float32)
        inner = math.sqrt(2.0 / math.pi) * (field + 0.044715 * (field * field * field))
        value = grid_ref[t].astype(jnp.float32) + 0.5 * field * (1.0 + jnp.tanh(inner))
        out_ref[t] = value.astype(jnp.bfloat16)


def chunk_of(longitudes):
    return max(n for n in range(16, 481, 16) if longitudes % n == 0)


def compact_shards(grid_input, legendre, mix_weight, degree_gain, order_slot):
    lat_dev, longitudes, channels = grid_input.shape
    orders = order_slot.shape[0]
    slot_count, degrees, latitudes = legendre.shape
    lat_count = lax.axis_size("lat")
    groups = lax.axis_size("chan")
    group_orders = orders // groups
    group_rows = 2 * group_orders
    part_rows = lat_dev * group_rows
    block_rows = part_rows * (channels // 128) + group_orders
    chunk = chunk_of(longitudes)
    chunks = longitudes // chunk
    columns = grouped_columns(orders, groups)
    forward, inverse = (table[:, columns] for table in transform_tables(orders, longitudes))
    forward = np.ascontiguousarray(forward.reshape(chunks, chunk, 2 * orders).transpose(0, 2, 1))
    hbm = pl.BlockSpec(memory_space=pltpu.HBM)

    sent = pl.pallas_call(
        functools.partial(analysis_kernel, math.sqrt(latitudes / degrees), chunk),
        in_specs=[hbm] * 5,
        out_shape=jax.ShapeDtypeStruct((lat_count, groups, block_rows, 128), jnp.bfloat16),
        scratch_shapes=[
            pltpu.VMEM(grid_input.shape, jnp.bfloat16),
            pltpu.VMEM(forward.shape, jnp.bfloat16),
            pltpu.VMEM((slot_count, latitudes, degrees), jnp.bfloat16),
            pltpu.VMEM((1, degrees), jnp.float32),
            pltpu.SMEM((1, orders), jnp.int32),
            pltpu.SemaphoreType.DMA((lat_dev, chunks)),
            pltpu.SemaphoreType.DMA((chunks,)),
            pltpu.SemaphoreType.DMA((3,)),
        ],
        compiler_params=pltpu.CompilerParams(vmem_limit_bytes=24 * MIB),
    )(
        grid_input,
        jnp.asarray(forward),
        jnp.swapaxes(legendre, 1, 2),
        degree_gain.reshape(1, degrees),
        order_slot.reshape(1, orders),
    )
    rows = lax.all_to_all(
        sent.reshape(lat_count * groups, block_rows, 128), ("lat", "chan"), split_axis=0, concat_axis=0, tiled=True
    )

    helpers = [jnp.asarray(m) for m in mixing_helpers(latitudes, group_orders)]
    columns_here = mix_weight.shape[1]
    parts = pl.pallas_call(
        functools.partial(mixing_kernel, lat_dev),
        out_shape=[jax.ShapeDtypeStruct((part_rows, columns_here), jnp.bfloat16)] * lat_count,
        scratch_shapes=[pltpu.VMEM((lat_count, part_rows, columns_here), jnp.bfloat16)],
        compiler_params=pltpu.CompilerParams(vmem_limit_bytes=24 * MIB),
    )(rows.reshape(lat_count, groups, block_rows, 128), mix_weight, *helpers)

    received = []
    for s in range(lat_count):
        pairs = [
            (a * groups + b, (b + s) % lat_count * groups + a) for a in range(lat_count) for b in range(groups)
        ]
        received.append(lax.ppermute(parts[s], ("lat", "chan"), pairs))

    return pl.pallas_call(
        functools.partial(synthesis_kernel, groups),
        grid=(chunks,),
        in_specs=[pl.BlockSpec((part_rows, channels), lambda k: (0, 0))] * lat_count
        + [
            pl.BlockSpec((lat_dev, chunk, channels), lambda k: (0, k, 0)),
            pl.BlockSpec((chunk, 2 * orders), lambda k: (k, 0)),
        ],
        out_specs=pl.BlockSpec((lat_dev, chunk, channels), lambda k: (0, k, 0)),
        out_shape=jax.ShapeDtypeStruct(grid_input.shape, jnp.bfloat16),
        scratch_shapes=[pltpu.VMEM((lat_dev, groups, group_rows, channels), jnp.bfloat16)],
        compiler_params=pltpu.CompilerParams(vmem_limit_bytes=24 * MIB),
    )(*received, grid_input, jnp.asarray(inverse))


def wide_shards(grid_input, legendre, mix_weight, degree_gain, order_slot):
    lat_dev, longitudes, channels = grid_input.shape
    orders = order_slot.shape[0]
    slot_count, degrees, latitudes = legendre.shape
    lat_count = lax.axis_size("lat")
    chan_count = lax.axis_size("chan")
    group_slots = lat_count * slot_count
    forward, inverse = (jnp.asarray(table) for table in transform_tables(orders, longitudes))

    own = (lax.axis_index("lat") * chan_count + lax.axis_index("chan")) * slot_count
    first_block = lax.dynamic_slice_in_dim(order_slot, own, slot_count, 0) // 64
    alive = jnp.arange(degrees, dtype=jnp.int32)[None, :] // 64 >= first_block[:, None]
    weights = jnp.where(alive, degree_gain[None, :] * math.sqrt(latitudes / degrees), 0.0)
    table = legendre.astype(jnp.float32)
    pairs = jnp.einsum("slv,slt->svt", table * weights[:, :, None], table, precision=lax.Precision.HIGHEST)

    slots = jnp.arange(orders, dtype=jnp.int32).reshape(lat_count, chan_count, slot_count).transpose(1, 0, 2)
    order_of_place = jnp.take(order_slot, slots.reshape(orders))
    hit = order_of_place[:, None] == jnp.arange(orders, dtype=jnp.int32)[None, :]
    hit = hit.astype(jnp.bfloat16)

    spectrum = jnp.einsum("akc,kn->anc", grid_input, forward, preferred_element_type=jnp.float32)
    spectrum = spectrum.astype(jnp.bfloat16).reshape(lat_dev, 2, orders, channels)
    rows = jnp.einsum("pm,armc->parc", hit, spectrum).astype(jnp.bfloat16)
    rows = rows.reshape(chan_count, group_slots, lat_dev, 2, channels)
    rows = lax.all_to_all(rows, "chan", split_axis=0, concat_axis=0, tiled=True)
    rows = lax.all_gather(rows, "lat", axis=0)
    pairs = lax.all_gather(pairs, "lat", axis=0, tiled=True)

    mixed = jnp.einsum(
        "absurc,bcd->sraud",
        rows,
        mix_weight.reshape(chan_count, channels, -1),
        preferred_element_type=jnp.float32,
    )
    mixed = mixed.reshape(group_slots, 2, latitudes, -1)
    synthesis = jnp.einsum("svt,srtd->vsrd", pairs, mixed, precision=lax.Precision.HIGHEST).astype(jnp.bfloat16)

    synthesis = synthesis.reshape(lat_count, lat_dev, group_slots, 2, -1)
    back = lax.all_to_all(synthesis, "lat", split_axis=0, concat_axis=0, tiled=True)
    back = back.transpose(1, 2, 3, 0, 4).reshape(lat_dev, group_slots, 2, chan_count, channels)
    back = lax.all_to_all(back.transpose(3, 0, 1, 2, 4), "chan", split_axis=0, concat_axis=0, tiled=True)
    back = back.transpose(1, 0, 2, 3, 4).reshape(lat_dev, orders, 2, channels)
    natural = jnp.einsum("pm,aprc->armc", hit, back).astype(jnp.bfloat16)
    field = jnp.einsum(
        "anc,kn->akc",
        natural.reshape(lat_dev, 2 * orders, channels),
        inverse,
        preferred_element_type=jnp.float32,
    )
    return (grid_input.astype(jnp.float32) + jax.nn.gelu(field)).astype(jnp.bfloat16)


def shards(grid_input, legendre, mix_weight, degree_gain, order_slot):
    lat_count, chan_count = lax.axis_size("lat"), lax.axis_size("chan")
    orders, latitudes = order_slot.shape[0], legendre.shape[2]
    compact = (
        lat_count == chan_count
        and 2 * latitudes * latitudes == 128
        and orders % (16 * chan_count) == 0
        and grid_input.shape[2] % 128 == 0
        and grid_input.shape[1] % 16 == 0
    )
    body = compact_shards if compact else wide_shards
    return body(grid_input, legendre, mix_weight, degree_gain, order_slot)


def solution(mesh):
    placed = (
        P(("groups", "lat"), None, "chan"),
        P(("lat", "chan"), None, None),
        P(None, "lat"),
        P(),
        P(),
    )
    return jax.shard_map(
        shards,
        mesh=mesh,
        in_specs=placed,
        out_specs=P(("groups", "lat"), None, "chan"),
        check_vma=False,
    )
```

time: 115 us -> 46.7 us (0.41)
  waiting for transfers between devices: 47 us -> 1.6 us
  blocking collectives: 0 us -> 24.6 us
  matrix products: 24.1 us -> 0 us
  between operations: 13.6 us -> 0.06 us
  starting transfers between devices: 16.9 us -> 7.82 us
  Pallas kernels: 0 us -> 7.81 us
  other arithmetic: 4.56 us -> 0 us
  local copies, waits for them, and re-layouts: 8.12 us -> 4.49 us
    all_to_all x4 -> x0, waiting for transfers between devices: 25.6 us -> none  [the longest x1 12.2 us: shards(): lax.all_to_all(spectrum, 'lat', split_axis=2, concat_axis=0, tiled=True)]
    all_to_all x0 -> x1, blocking collectives: none -> 24.6 us  [compact_shards(): lax.all_to_all(sent.reshape(lat_count * groups, block_rows, 128), ('lat',...]
    dot_general x10 -> x0, matrix products: 24.1 us -> none  [the longest x4 18.2 us: mix_degrees(): jnp.einsum('slrc,cd->slrd', coefficients, weights_full, preferred_element...]
    all_gather x1 -> x0, waiting for transfers between devices: 20.7 us -> none  [shards(): weights_full = lax.all_gather(mix_weight, 'lat', axis=1, tiled=True)]
    all_to_all x4 -> x0, starting transfers between devices: 16.9 us -> none  [the longest x1 6.32 us: shards(): lax.all_to_all(spectrum, 'lat', split_axis=2, concat_axis=0, tiled=True)]
    ppermute x0 -> x4, starting transfers between devices: none -> 7.82 us  [compact_shards(): received.append(lax.ppermute(parts[s], ('lat', 'chan'), pairs))]
    pallas_call x0 -> x3, Pallas kernels: none -> 7.81 us  [the longest x1 4.34 us: compact_shards(): pl.pallas_call(functools.partial(analysis_kernel, math.sqrt(latitudes / d...]
    another operation x2 -> x0, other arithmetic: 4.37 us -> none
  transfers between devices with their start and end apart: 5 -> 4, of which waited for: 5 -> 2; matrix products, arithmetic and copies ran while one was open for 8% -> 0% of each run, Pallas kernels for 0% -> 0%
where the time goes in v2:
time: 46.7 us; the launch traced here: 46.4 us
  blocking collectives  24.6 us (53%)
  starting transfers between devices  7.82 us (17%)
  Pallas kernels  7.81 us (17%)
  local copies, waits for them, and re-layouts  4.49 us (10%)
  waiting for transfers between devices  1.6 us (3%)
    all_to_all x1, blocking collectives, compact_shards(): lax.all_to_all(sent.reshape(lat_count * groups, block_rows, 128), ('lat',...  24.6 us
    ppermute x4, starting transfers between devices, compact_shards(): received.append(lax.ppermute(parts[s], ('lat', 'chan'), pairs))  7.82 us
    unnamed x22, local copies, waits for them, and re-layouts  4.49 us
    pallas_call x1, Pallas kernels, compact_shards(): pl.pallas_call(functools.partial(analysis_kernel, math.sqrt(latitudes / d...  4.34 us
    pallas_call x1, Pallas kernels, compact_shards(): pl.pallas_call(functools.partial(synthesis_kernel, groups), grid=(chunks,...  2.71 us
    ppermute x4, waiting for transfers between devices, compact_shards(): received.append(lax.ppermute(parts[s], ('lat', 'chan'), pairs))  1.6 us
  transfers between devices with their start and end apart: 4, of which 2 were waited for; matrix products, arithmetic and copies ran while one was open for 0% of the time, Pallas kernels for 0%

profile of v2, /device:TPU:0, one launch (start us, length us, event | category | flops | bytes accessed | tf_op | source)
XLA Modules:
  0.0 46.4 jit_solution(7191739987294549187)
XLA Ops:
  0.0 0.0 copy-start
  0.0 1.4 %copy-done = bf16[2,1440,256]{2,1,0:T(8,128)(2,1)S(1)} copy-done((bf16[2,1440,256]{2,1,0:T(8,128)(2,1)S(1)}, bf16[2,1440,256]{2,1,0:T(8,128)(2,1)}, u32[]{:S(2)}) %copy-start) | copy-done | bytes 1474584
  1.4 0.0 copy-start.3
  1.4 1.0 %copy-done.3 = bf16[3,128,480]{2,1,0:T(8,128)(2,1)S(1)} copy-done((bf16[3,128,480]{2,1,0:T(8,128)(2,1)S(1)}, bf16[3,128,480]{2,1,0:T(8,128)(2,1)}, u32[]{:S(2)}) %copy-start.3) | copy-done | bytes 368664
  2.4 0.0 copy-start.8
  2.4 0.8 %copy-done.8 = bf16[4,512,8]{1,2,0:T(8,128)(2,1)S(1)} copy-done((bf16[4,512,8]{1,2,0:T(8,128)(2,1)S(1)}, bf16[4,512,8]{1,2,0:T(8,128)(2,1)}, u32[]{:S(2)}) %copy-start.8) | copy-done | bytes 32792
  3.1 0.7 %copy-done.9 = f32[512]{0:T(512)S(1)} copy-done((f32[512]{0:T(512)S(1)}, f32[512]{0:T(512)}, u32[]{:S(2)}) %copy-start.9) | copy-done | bytes 2072
  3.8 0.0 copy-start.10
  3.8 0.7 %copy-done.10 = s32[64]{0:T(128)S(1)} copy-done((s32[64]{0:T(128)S(1)}, s32[64]{0:T(128)}, u32[]{:S(2)}) %copy-start.10) | copy-done | bytes 280
  4.5 0.0 copy-start.2
  4.5 0.0 copy-start.6
  4.5 0.0 copy-start.7
  4.5 4.3 %shard_map.100 = bf16[4,4,144,128]{3,2,1,0:T(8,128)(2,1)S(1)} custom-call(bf16[2,1440,256]{2,1,0:T(8,128)(2,1)S(1)} %copy-done, bf16[3,128,480]{2,1,0:T(8,128)(2,1)S(1)} %copy-done.3, bf16[4,8,512]{2,1,0:T(8,128)(2,1)S(1)} %bitcast.7, f32[1,512]{1,0:T(1,128)S(1)} %bitcast.8, s32[1,64]{1,0:T(1,128)S(1)} %bitcast.9), custom_call_target="tpu_custom_call" | custom-call | tf_op jit(solution)/shard_map/pallas_call | solution.py:205
  8.8 0.0 copy-start.1
  8.8 0.0 copy-start.4
  8.9 24.6 %all_to_all.5 = bf16[16,144,128]{2,1,0:T(8,128)(2,1)S(1)} all-to-all(bf16[16,144,128]{2,1,0:T(8,128)(2,1)S(1)} %bitcast.6), channel_id=1, replica_groups=mesh['groups'=2,'lat'=4,'chan'=4] {'lat','chan'}, dimensions={0} | all-to-all | bytes 1179648 | tf_op jit(solution)/shard_map/all_to_all | solution.py:227
  33.4 0.0 copy-done.2
  33.4 0.0 copy-done.5
  33.4 0.0 copy-done.6
  33.4 0.0 copy-done.7
  33.4 0.8 %shard_map.101 = (bf16[64,256]{1,0:T(8,128)(2,1)S(1)}, bf16[64,256]{1,0:T(8,128)(2,1)S(1)}, bf16[64,256]{1,0:T(8,128)(2,1)S(1)}, bf16[64,256]{1,0:T(8,128)(2,1)S(1)}) custom-call(bf16[4,4,144,128]{3,2,1,0:T(8,128)(2,1)S(1)} %bitcast.5, bf16[1024,256]{1,0:T(8,128)(2,1)S(1)} %copy-done.2, bf16[256,128]{1,0:T(8,128)(2,1)S(1)} %copy-done.7, ...), custom_call_target="tpu_custom_call" | custom-call | tf_op jit(solution)/shard_map/pallas_call | solution.py:233
  34.2 0.7 %collective-permute-start = (bf16[64,256]{1,0:T(8,128)(2,1)S(1)}, bf16[64,256]{1,0:T(8,128)(2,1)S(1)}, u32[]{:S(2)}, u32[]{:S(2)}) collective-permute-start(bf16[64,256]{1,0:T(8,128)(2,1)S(1)} %get-tuple-element.9), channel_id=1, source_target_pairs={{0,0},{1,4},{2,8},{3,12},{4,1},{5,5},{6,9},{7,13},{8,2},{9,6},{10,... | collective-permute-start | bytes 98312 | tf_op jit(solution)/shard_map/ppermute | solution.py:245
  34.9 3.1 %collective-permute-start.1 = (bf16[64,256]{1,0:T(8,128)(2,1)S(1)}, bf16[64,256]{1,0:T(8,128)(2,1)S(1)}, u32[]{:S(2)}, u32[]{:S(2)}) collective-permute-start(bf16[64,256]{1,0:T(8,128)(2,1)S(1)} %get-tuple-element.10), channel_id=1, source_target_pairs={{0,4},{1,8},{2,12},{3,0},{4,5},{5,9},{6,13},{7,1},{8,6},{9,10},{10... | collective-permute-start | bytes 98312 | tf_op jit(solution)/shard_map/ppermute | solution.py:245
  37.9 1.4 %collective-permute-start.2 = (bf16[64,256]{1,0:T(8,128)(2,1)S(1)}, bf16[64,256]{1,0:T(8,128)(2,1)S(1)}, u32[]{:S(2)}, u32[]{:S(2)}) collective-permute-start(bf16[64,256]{1,0:T(8,128)(2,1)S(1)} %get-tuple-element.11), channel_id=1, source_target_pairs={{0,8},{1,12},{2,0},{3,4},{4,9},{5,13},{6,1},{7,5},{8,10},{9,14},{1... | collective-permute-start | bytes 98312 | tf_op jit(solution)/shard_map/ppermute | solution.py:245
  39.3 2.7 %collective-permute-start.3 = (bf16[64,256]{1,0:T(8,128)(2,1)S(1)}, bf16[64,256]{1,0:T(8,128)(2,1)S(1)}, u32[]{:S(2)}, u32[]{:S(2)}) collective-permute-start(bf16[64,256]{1,0:T(8,128)(2,1)S(1)} %get-tuple-element.12), channel_id=1, source_target_pairs={{0,12},{1,0},{2,4},{3,8},{4,13},{5,1},{6,5},{7,9},{8,14},{9,2},{10... | collective-permute-start | bytes 98312 | tf_op jit(solution)/shard_map/ppermute | solution.py:245
  42.0 0.0 collective-permute-done.refs_0_
  42.1 0.0 collective-permute-done.1.refs_1_
  42.1 1.1 %collective-permute-done.2.refs_2_ = bf16[64,256]{1,0:T(8,128)(2,1)S(1)} collective-permute-done((bf16[64,256]{1,0:T(8,128)(2,1)S(1)}, bf16[64,256]{1,0:T(8,128)(2,1)S(1)}, u32[]{:S(2)}, u32[]{:S(2)}) %collective-permute-start.2) | collective-permute-done | bytes 32800 | tf_op jit(solution)/shard_map/ppermute | solution.py:245
  43.1 0.5 %collective-permute-done.3.refs_3_ = bf16[64,256]{1,0:T(8,128)(2,1)S(1)} collective-permute-done((bf16[64,256]{1,0:T(8,128)(2,1)S(1)}, bf16[64,256]{1,0:T(8,128)(2,1)S(1)}, u32[]{:S(2)}, u32[]{:S(2)}) %collective-permute-start.3) | collective-permute-done | bytes 32800 | tf_op jit(solution)/shard_map/ppermute | solution.py:245
  43.6 0.0 copy-done.1
  43.6 0.0 copy-done.4
  43.7 2.7 %shard_map.102 = bf16[2,1440,256]{2,1,0:T(8,128)(2,1)} custom-call(bf16[64,256]{1,0:T(8,128)(2,1)S(1)} %collective-permute-done.refs_0_, bf16[64,256]{1,0:T(8,128)(2,1)S(1)} %collective-permute-done.1.refs_1_, bf16[64,256]{1,0:T(8,128)(2,1)S(1)} %collective-permute-done.2.refs_2_, bf16[64,256]{1,0:T(8,128)(2,1)S(1)} %collective-permute-done.3.refs_3_, ...), custom_call_target="tpu_custom_call" | custom-call | tf_op jit(solution)/shard_map/pallas_call | solution.py:247
  (2 shorter events, 0.0 us)
Async XLA Ops:
  0.0 1.4 %copy-start = (bf16[2,1440,256]{2,1,0:T(8,128)(2,1)S(1)}, bf16[2,1440,256]{2,1,0:T(8,128)(2,1)}, u32[]{:S(2)}) copy-start(bf16[2,1440,256]{2,1,0:T(8,128)(2,1)} %refs_4_.1) | copy-start | bytes 4423684
  1.4 1.0 %copy-start.3 = (bf16[3,128,480]{2,1,0:T(8,128)(2,1)S(1)}, bf16[3,128,480]{2,1,0:T(8,128)(2,1)}, u32[]{:S(2)}) copy-start(bf16[3,128,480]{2,1,0:T(8,128)(2,1)} %constant.10.clone.table_hbm) | copy-start | bytes 1105924
  2.4 0.8 %copy-start.8 = (bf16[4,512,8]{1,2,0:T(8,128)(2,1)S(1)}, bf16[4,512,8]{1,2,0:T(8,128)(2,1)}, u32[]{:S(2)}) copy-start(bf16[4,512,8]{1,2,0:T(8,128)(2,1)} %param.11) | copy-start | bytes 98308
  3.1 0.7 %copy-start.9 = (f32[512]{0:T(512)S(1)}, f32[512]{0:T(512)}, u32[]{:S(2)}) copy-start(f32[512]{0:T(512)} %param.13) | copy-start | bytes 6148
  3.8 0.7 %copy-start.10 = (s32[64]{0:T(128)S(1)}, s32[64]{0:T(128)}, u32[]{:S(2)}) copy-start(s32[64]{0:T(128)} %param.14) | copy-start | bytes 772
  4.5 29.0 %copy-start.2 = (bf16[1024,256]{1,0:T(8,128)(2,1)S(1)}, bf16[1024,256]{1,0:T(8,128)(2,1)}, u32[]{:S(2)}) copy-start(bf16[1024,256]{1,0:T(8,128)(2,1)} %weight_ref.1) | copy-start | bytes 1572868
  4.5 29.0 %copy-start.5 = (bf16[256,256]{1,0:T(8,128)(2,1)S(1)}, bf16[256,256]{1,0:T(8,128)(2,1)}, u32[]{:S(2)}) copy-start(bf16[256,256]{1,0:T(8,128)(2,1)} %constant.13.clone.same_ref) | copy-start | bytes 393220
  4.5 29.0 %copy-start.6 = (bf16[128,512]{1,0:T(8,128)(2,1)S(1)}, bf16[128,512]{1,0:T(8,128)(2,1)}, u32[]{:S(2)}) copy-start(bf16[128,512]{1,0:T(8,128)(2,1)} %constant.12.clone.halves_ref) | copy-start | bytes 393220
  4.5 29.0 %copy-start.7 = (bf16[256,128]{1,0:T(8,128)(2,1)S(1)}, bf16[256,128]{1,0:T(8,128)(2,1)}, u32[]{:S(2)}) copy-start(bf16[256,128]{1,0:T(8,128)(2,1)} %constant.11.clone.keep_ref) | copy-start | bytes 196612
  8.8 34.8 %copy-start.1 = (bf16[2,1440,256]{2,1,0:T(8,128)(2,1)S(1)}, bf16[2,1440,256]{2,1,0:T(8,128)(2,1)}, u32[]{:S(2)}) copy-start(bf16[2,1440,256]{2,1,0:T(8,128)(2,1)} %refs_4_.1) | copy-start | bytes 4423684
  8.8 34.8 %copy-start.4 = (bf16[1440,128]{1,0:T(8,128)(2,1)S(1)}, bf16[1440,128]{1,0:T(8,128)(2,1)}, u32[]{:S(2)}) copy-start(bf16[1440,128]{1,0:T(8,128)(2,1)} %constant.14.clone.refs_5_) | copy-start | bytes 1105924
  34.2 7.8 %collective-permute-start = (bf16[64,256]{1,0:T(8,128)(2,1)S(1)}, bf16[64,256]{1,0:T(8,128)(2,1)S(1)}, u32[]{:S(2)}, u32[]{:S(2)}) collective-permute-start(bf16[64,256]{1,0:T(8,128)(2,1)S(1)} %get-tuple-element.9), channel_id=1, source_target_pairs={{0,0},{1,4},{2,8},{3,12},{4,1},{5,5},{6,9},{7,13},{8,2},{9,6},{10,... | collective-permute-start | bytes 98312 | tf_op jit(solution)/shard_map/ppermute | solution.py:245
  34.9 7.2 %collective-permute-start.1 = (bf16[64,256]{1,0:T(8,128)(2,1)S(1)}, bf16[64,256]{1,0:T(8,128)(2,1)S(1)}, u32[]{:S(2)}, u32[]{:S(2)}) collective-permute-start(bf16[64,256]{1,0:T(8,128)(2,1)S(1)} %get-tuple-element.10), channel_id=1, source_target_pairs={{0,4},{1,8},{2,12},{3,0},{4,5},{5,9},{6,13},{7,1},{8,6},{9,10},{10... | collective-permute-start | bytes 98312 | tf_op jit(solution)/shard_map/ppermute | solution.py:245
  37.9 5.2 %collective-permute-start.2 = (bf16[64,256]{1,0:T(8,128)(2,1)S(1)}, bf16[64,256]{1,0:T(8,128)(2,1)S(1)}, u32[]{:S(2)}, u32[]{:S(2)}) collective-permute-start(bf16[64,256]{1,0:T(8,128)(2,1)S(1)} %get-tuple-element.11), channel_id=1, source_target_pairs={{0,8},{1,12},{2,0},{3,4},{4,9},{5,13},{6,1},{7,5},{8,10},{9,14},{1... | collective-permute-start | bytes 98312 | tf_op jit(solution)/shard_map/ppermute | solution.py:245
  39.3 4.3 %collective-permute-start.3 = (bf16[64,256]{1,0:T(8,128)(2,1)S(1)}, bf16[64,256]{1,0:T(8,128)(2,1)S(1)}, u32[]{:S(2)}, u32[]{:S(2)}) collective-permute-start(bf16[64,256]{1,0:T(8,128)(2,1)S(1)} %get-tuple-element.12), channel_id=1, source_target_pairs={{0,12},{1,0},{2,4},{3,8},{4,13},{5,1},{6,5},{7,9},{8,14},{9,2},{10... | collective-permute-start | bytes 98312 | tf_op jit(solution)/shard_map/ppermute | solution.py:245

commit v3 on v2

--- a/solution.py
+++ b/solution.py
@@ -10,6 +10,7 @@
 from jax.sharding import PartitionSpec as P
 
 MIB = 1024 * 1024
+ROOT = math.sqrt(2.0 / math.pi)
 
 
 def transform_tables(orders, longitudes):
@@ -17,7 +18,7 @@
     angle = residue.astype(np.float32) * np.float32(2.0 * math.pi / longitudes)
     scale = np.float32(1.0 / math.sqrt(longitudes))
     forward = np.concatenate([np.cos(angle) * scale, -np.sin(angle) * scale], axis=1)
-    weight = np.where(np.arange(2 * orders) % orders == 0, 1.0, 2.0).astype(np.float32)
+    weight = np.where(np.arange(2 * orders) % orders == 0, 0.5, 1.0).astype(np.float32)
     return forward.astype(jnp.bfloat16), (forward * weight).astype(jnp.bfloat16)
 
 
@@ -29,7 +30,8 @@
     factor, chunk, grid_hbm, table_hbm, legendre_hbm, gain_hbm, slot_hbm, out_ref,
     grid_buf, table_buf, legendre_buf, gain_buf, slot_buf, grid_sem, table_sem, small_sem,
 ):
-    lat_count, groups, _, _ = out_ref.shape
+    lat_count, chips, _, _ = out_ref.shape
+    groups = 2 * chips
     lat_dev, longitudes, channels = grid_buf.shape
     slot_count, latitudes, degrees = legendre_buf.shape
     orders = slot_buf.shape[1]
@@ -66,19 +68,26 @@
     block = lax.broadcasted_iota(jnp.int32, (1, degrees), 1) // 64
     high_lane = lax.broadcasted_iota(jnp.int32, (1, lanes), 1) < lanes // 2
     row = lax.broadcasted_iota(jnp.int32, (group_orders, lanes), 0)
+    sums = []
+    for s in range(slot_count):
+        rows = legendre_buf[s].astype(jnp.float32)
+        weights = jnp.where(block >= slot_buf[0, own + s] // 64, gain_buf[...] * factor, 0.0)
+        weighted = rows * weights
+        terms = jnp.concatenate([weighted * rows[v : v + 1] for v in range(latitudes)], axis=0)
+        sums += [sum(terms[:, k : k + 128] for k in range(0, degrees, 128))] * 2
+    sums = jnp.concatenate(sums, axis=0)
+    high = sums.astype(jnp.bfloat16)
+    low = (sums - high.astype(jnp.float32)).astype(jnp.bfloat16)
+    pairs = lax.dot_general(
+        jnp.ones((8, 256), jnp.bfloat16),
+        jnp.concatenate([high, low], axis=1),
+        (((1,), (1,)), ((), ())),
+        preferred_element_type=jnp.float32,
+    )
     placed = [jnp.zeros((group_orders, lanes), jnp.float32) for _ in range(groups)]
     for s in range(slot_count):
         order = slot_buf[0, own + s]
-        rows = legendre_buf[s].astype(jnp.float32)
-        products = [rows * rows[v : v + 1] for v in range(latitudes)] * 2
-        weights = jnp.where(block >= order // 64, gain_buf[...] * factor, 0.0)
-        pair = lax.dot_general(
-            weights,
-            jnp.concatenate(products, axis=0),
-            (((1,), (1,)), ((), ())),
-            precision=lax.Precision.HIGHEST,
-            preferred_element_type=jnp.float32,
-        )
+        pair = pairs[:1, s * lanes : (s + 1) * lanes]
         high = pair.astype(jnp.bfloat16).astype(jnp.float32)
         pair = jnp.where(high_lane, high, pair - high)
         for g in range(groups):
@@ -86,8 +95,8 @@
     top = lat_dev * group_rows * (channels // 128)
     for g in range(groups):
         value = placed[g].astype(jnp.bfloat16)
-        for a in range(lat_count):
-            out_ref[a, g, top : top + group_orders] = value
+        for a in range(g // chips, lat_count, 2):
+            out_ref[a, g % chips, top : top + group_orders] = value
 
     for t in range(lat_dev):
         total = None
@@ -104,8 +113,8 @@
             for h in range(channels // 128):
                 value = spectrum[g * group_rows : (g + 1) * group_rows, h * 128 : (h + 1) * 128]
                 at = (h * lat_dev + t) * group_rows
-                for a in range(lat_count):
-                    out_ref[a, g, at : at + group_rows] = value
+                for a in range(g // chips, lat_count, 2):
+                    out_ref[a, g % chips, at : at + group_rows] = value
 
 
 def mixing_helpers(latitudes, group_orders):
@@ -120,28 +129,40 @@
     return [m.astype(jnp.bfloat16) for m in (keep, halves, same)]
 
 
-def mixing_kernel(lat_dev, rows_ref, weight_ref, keep_ref, halves_ref, same_ref, *out_and_scratch):
-    outs, held = out_and_scratch[:-1], out_and_scratch[-1]
-    lat_count, chan_count, _, _ = rows_ref.shape
+def choose_kernel(weight_ref, moved_ref, out_ref):
+    own = lax.rem(lax.axis_index("lat") + lax.axis_index("chan"), 2) == 0
+
+    @pl.when(own)
+    def _():
+        out_ref[...] = weight_ref[...]
+
+    @pl.when(jnp.logical_not(own))
+    def _():
+        out_ref[...] = moved_ref[...]
+
+
+def mixing_kernel(own_ref, other_ref, weight_ref, keep_ref, halves_ref, same_ref, out_ref):
+    lat_count, chips, block_rows, _ = own_ref.shape
     count = same_ref.shape[0]
     part_rows = count // lat_count
-    lanes = keep_ref.shape[1]
-    channels = weight_ref.shape[0] // chan_count
+    channels = weight_ref.shape[0] // (2 * chips)
     split = channels // 128
-    group_orders = rows_ref.shape[2] - split * part_rows
+    group_orders = block_rows - split * part_rows
+    core = lax.rem(lax.axis_index("chan"), 2)
     mixed = None
     pairs = None
-    for b in range(chan_count):
-        block = jnp.concatenate(
-            [rows_ref[:, b, h * part_rows : (h + 1) * part_rows, :].reshape(count, 128) for h in range(split)], axis=1
-        )
-        term = jnp.dot(
-            block, weight_ref[b * channels : (b + 1) * channels, :], preferred_element_type=jnp.float32
-        )
-        mixed = term if mixed is None else mixed + term
-        for a in range(lat_count):
-            sent = rows_ref[a, b, split * part_rows :, :].astype(jnp.float32)
-            pairs = sent if pairs is None else pairs + sent
+    for x in range(chips):
+        for rows_ref, sender in ((own_ref, core), (other_ref, 1 - core)):
+            block = jnp.concatenate(
+                [rows_ref[:, x, h * part_rows : (h + 1) * part_rows, :].reshape(count, 128) for h in range(split)],
+                axis=1,
+            )
+            at = pl.ds(pl.multiple_of((2 * x + sender) * channels, channels), channels)
+            term = jnp.dot(block, weight_ref[at, :], preferred_element_type=jnp.float32)
+            mixed = term if mixed is None else mixed + term
+            for a in range(lat_count):
+                sent = rows_ref[a, x, split * part_rows :, :].astype(jnp.float32)
+                pairs = sent if pairs is None else pairs + sent
     wide = jnp.concatenate([pairs] * (count // group_orders), axis=0) * keep_ref[...].astype(jnp.float32)
     matrix = jnp.dot(wide.astype(jnp.bfloat16), halves_ref[...], preferred_element_type=jnp.float32)
     same = same_ref[...].astype(jnp.float32)
@@ -154,31 +175,41 @@
         + jnp.dot(high, mixed_low, preferred_element_type=jnp.float32)
         + jnp.dot(low, mixed_high, preferred_element_type=jnp.float32)
     )
-    held[...] = synthesis.astype(jnp.bfloat16).reshape(held.shape)
-    for s in range(lat_count):
-        outs[s][...] = held[lax.rem(lax.axis_index("chan") + s, lat_count)]
-
-
-def synthesis_kernel(groups, *refs):
-    received = refs[:groups]
-    grid_ref, table_ref, out_ref, held = refs[groups:]
-    lat_dev = grid_ref.shape[0]
-    group_rows = held.shape[2]
-    channels = held.shape[3]
-
-    @pl.when(pl.program_id(0) == 0)
-    def _():
-        for s in range(groups):
-            group = lax.rem(lax.axis_index("lat") + groups - s, groups)
-            for t in range(lat_dev):
-                held[t, group] = received[s][t * group_rows : (t + 1) * group_rows, :]
-
+    out_ref[...] = jnp.zeros(out_ref.shape, out_ref.dtype)
+    to_chip = lax.axis_index("lat") // 2
+    out_ref[:, to_chip] = synthesis.astype(jnp.bfloat16).reshape((lat_count,) + out_ref.shape[2:])
+
+
+def synthesis_kernel(piece, received_ref, grid_ref, table_ref, out_hbm, out_buf, out_sem):
+    lat_dev, longitudes, channels = grid_ref.shape
+    _, chips, part_rows, _ = received_ref.shape
+    group_rows = part_rows // lat_dev
+    pair = lax.axis_index("chan") // 2 * 2
+    parts = out_sem.shape[1]
+    size = longitudes // parts
+    copies = []
     for t in range(lat_dev):
-        rows = held[t].reshape(groups * group_rows, channels)
-        field = jnp.dot(table_ref[...], rows, preferred_element_type=jnp.float32)
-        inner = math.sqrt(2.0 / math.pi) * (field + 0.044715 * (field * field * field))
-        value = grid_ref[t].astype(jnp.float32) + 0.5 * field * (1.0 + jnp.tanh(inner))
-        out_ref[t] = value.astype(jnp.bfloat16)
+        rows = jnp.concatenate(
+            [
+                received_ref[pair + g, x, t * group_rows : (t + 1) * group_rows, :]
+                for g in range(2)
+                for x in range(chips)
+            ],
+            axis=0,
+        )
+        for k in range(parts):
+            for at in range(k * size, (k + 1) * size, piece):
+                half = jnp.dot(table_ref[at : at + piece, :], rows, preferred_element_type=jnp.float32)
+                square = half * half
+                inner = half * (2.0 * ROOT + (8.0 * ROOT * 0.044715) * square)
+                value = grid_ref[t, at : at + piece, :].astype(jnp.float32) + half * (1.0 + jnp.tanh(inner))
+                out_buf[t, at : at + piece, :] = value.astype(jnp.bfloat16)
+            span = pl.ds(k * size, size)
+            copy = pltpu.make_async_copy(out_buf.at[t, span], out_hbm.at[t, span], out_sem.at[t, k])
+            copy.start()
+            copies.append(copy)
+    for copy in copies:
+        copy.wait()
 
 
 def chunk_of(longitudes):
@@ -191,6 +222,7 @@
     slot_count, degrees, latitudes = legendre.shape
     lat_count = lax.axis_size("lat")
     groups = lax.axis_size("chan")
+    chips = groups // 2
     group_orders = orders // groups
     group_rows = 2 * group_orders
     part_rows = lat_dev * group_rows
@@ -202,10 +234,23 @@
     forward = np.ascontiguousarray(forward.reshape(chunks, chunk, 2 * orders).transpose(0, 2, 1))
     hbm = pl.BlockSpec(memory_space=pltpu.HBM)
 
+    both = ("lat", "chan")
+    places = [(a, b) for a in range(lat_count) for b in range(groups)]
+    moved = lax.ppermute(
+        mix_weight, both, [(a * groups + b, (a ^ 1) * groups + b) for a, b in places if (a + b) % 2 == 0]
+    )
+
+    weight = pl.pallas_call(
+        choose_kernel,
+        out_shape=jax.ShapeDtypeStruct(mix_weight.shape, jnp.bfloat16),
+        cost_estimate=pl.CostEstimate(flops=100000000000, bytes_accessed=100000000, transcendentals=0),
+        compiler_params=pltpu.CompilerParams(vmem_limit_bytes=24 * MIB),
+    )(mix_weight, moved)
+
     sent = pl.pallas_call(
         functools.partial(analysis_kernel, math.sqrt(latitudes / degrees), chunk),
         in_specs=[hbm] * 5,
-        out_shape=jax.ShapeDtypeStruct((lat_count, groups, block_rows, 128), jnp.bfloat16),
+        out_shape=pltpu.VMEM((lat_count, chips, block_rows, 128), jnp.bfloat16),
         scratch_shapes=[
             pltpu.VMEM(grid_input.shape, jnp.bfloat16),
             pltpu.VMEM(forward.shape, jnp.bfloat16),
@@ -218,45 +263,56 @@
         ],
         compiler_params=pltpu.CompilerParams(vmem_limit_bytes=24 * MIB),
     )(
-        grid_input,
-        jnp.asarray(forward),
-        jnp.swapaxes(legendre, 1, 2),
-        degree_gain.reshape(1, degrees),
-        order_slot.reshape(1, orders),
-    )
-    rows = lax.all_to_all(
-        sent.reshape(lat_count * groups, block_rows, 128), ("lat", "chan"), split_axis=0, concat_axis=0, tiled=True
-    )
+        *(
+            pltpu.with_memory_space_constraint(operand, pltpu.HBM)
+            for operand in (
+                grid_input,
+                jnp.asarray(forward),
+                jnp.swapaxes(legendre, 1, 2),
+                degree_gain.reshape(1, degrees),
+                order_slot.reshape(1, orders),
+            )
+        )
+    )
+    cores = [[a * groups + 2 * x + k for a in range(lat_count) for x in range(chips)] for k in range(2)]
+    own = lax.all_to_all(
+        sent.reshape(lat_count * chips, block_rows, 128),
+        both,
+        split_axis=0,
+        concat_axis=0,
+        tiled=True,
+        axis_index_groups=cores,
+    )
+    other = lax.ppermute(own, both, [(n, n ^ 1) for n in range(lat_count * groups)])
 
     helpers = [jnp.asarray(m) for m in mixing_helpers(latitudes, group_orders)]
     columns_here = mix_weight.shape[1]
     parts = pl.pallas_call(
-        functools.partial(mixing_kernel, lat_dev),
-        out_shape=[jax.ShapeDtypeStruct((part_rows, columns_here), jnp.bfloat16)] * lat_count,
-        scratch_shapes=[pltpu.VMEM((lat_count, part_rows, columns_here), jnp.bfloat16)],
+        mixing_kernel,
+        out_shape=jax.ShapeDtypeStruct((lat_count, chips, part_rows, columns_here), jnp.bfloat16),
         compiler_params=pltpu.CompilerParams(vmem_limit_bytes=24 * MIB),
-    )(rows.reshape(lat_count, groups, block_rows, 128), mix_weight, *helpers)
-
-    received = []
-    for s in range(lat_count):
-        pairs = [
-            (a * groups + b, (b + s) % lat_count * groups + a) for a in range(lat_count) for b in range(groups)
-        ]
-        received.append(lax.ppermute(parts[s], ("lat", "chan"), pairs))
-
+    )(*(rows.reshape(lat_count, chips, block_rows, 128) for rows in (own, other)), weight, *helpers)
+    received = lax.all_to_all(
+        parts.reshape(lat_count * chips, part_rows, columns_here),
+        both,
+        split_axis=0,
+        concat_axis=0,
+        tiled=True,
+        axis_index_groups=cores,
+    ).reshape(lat_count, chips, part_rows, columns_here)
+
+    whole = pl.BlockSpec(memory_space=pltpu.VMEM)
     return pl.pallas_call(
-        functools.partial(synthesis_kernel, groups),
-        grid=(chunks,),
-        in_specs=[pl.BlockSpec((part_rows, channels), lambda k: (0, 0))] * lat_count
-        + [
-            pl.BlockSpec((lat_dev, chunk, channels), lambda k: (0, k, 0)),
-            pl.BlockSpec((chunk, 2 * orders), lambda k: (k, 0)),
+        functools.partial(synthesis_kernel, 96),
+        in_specs=[whole] * 3,
+        out_specs=hbm,
+        out_shape=jax.ShapeDtypeStruct(grid_input.shape, jnp.bfloat16),
+        scratch_shapes=[
+            pltpu.VMEM(grid_input.shape, jnp.bfloat16),
+            pltpu.SemaphoreType.DMA((lat_dev, 3)),
         ],
-        out_specs=pl.BlockSpec((lat_dev, chunk, channels), lambda k: (0, k, 0)),
-        out_shape=jax.ShapeDtypeStruct(grid_input.shape, jnp.bfloat16),
-        scratch_shapes=[pltpu.VMEM((lat_dev, groups, group_rows, channels), jnp.bfloat16)],
         compiler_params=pltpu.CompilerParams(vmem_limit_bytes=24 * MIB),
-    )(*received, grid_input, jnp.asarray(inverse))
+    )(received, grid_input, jnp.asarray(inverse))
 
 
 def wide_shards(grid_input, legendre, mix_weight, degree_gain, order_slot):
@@ -303,7 +359,7 @@
     back = lax.all_to_all(back.transpose(3, 0, 1, 2, 4), "chan", split_axis=0, concat_axis=0, tiled=True)
     back = back.transpose(1, 0, 2, 3, 4).reshape(lat_dev, orders, 2, channels)
     natural = jnp.einsum("pm,aprc->armc", hit, back).astype(jnp.bfloat16)
-    field = jnp.einsum(
+    field = 2.0 * jnp.einsum(
         "anc,kn->akc",
         natural.reshape(lat_dev, 2 * orders, channels),
         inverse,
@@ -317,6 +373,7 @@
     orders, latitudes = order_slot.shape[0], legendre.shape[2]
     compact = (
         lat_count == chan_count
+        and chan_count % 2 == 0
         and 2 * latitudes * latitudes == 128
         and orders % (16 * chan_count) == 0
         and grid_input.shape[2] % 128 == 0

time: 46.7 us -> 38.4 us (0.82)
  local copies, waits for them, and re-layouts: 4.49 us -> 0.03 us
  Pallas kernels: 7.81 us -> 5.01 us
  starting transfers between devices: 7.82 us -> 5.08 us
  blocking collectives: 24.6 us -> 26.5 us
    unnamed x22 -> x12, local copies, waits for them, and re-layouts: 4.49 us -> 0.03 us
    ppermute x4 -> x2, starting transfers between devices: 7.82 us -> 5.08 us  [the longest x1 5.08 us: compact_shards(): lax.ppermute(mix_weight, both, [(a * groups + b, (a ^ 1) * groups + b) fo...]
    pallas_call x1, Pallas kernels: 4.34 us -> 2.34 us  [compact_shards(): pl.pallas_call(functools.partial(analysis_kernel, math.sqrt(latitudes / d...]
    all_to_all x1 -> x2, blocking collectives: 24.6 us -> 26.5 us  [the longest x1 14.6 us: compact_shards(): lax.all_to_all(sent.reshape(lat_count * chips, block_rows, 128), both, sp...]
    pallas_call x2 -> x3, Pallas kernels: 3.47 us -> 2.66 us  [the longest x1 1.86 us: compact_shards(): pl.pallas_call(functools.partial(synthesis_kernel, 96), in_specs=[whole]...]
    ppermute x4 -> x2, waiting for transfers between devices: 1.6 us -> 1.47 us  [the longest x1 1.47 us: compact_shards(): lax.ppermute(own, both, [(n, n ^ 1) for n in range(lat_count * groups)])]
  transfers between devices with their start and end apart: 4 -> 2, of which waited for: 2 -> 1; matrix products, arithmetic and copies ran while one was open for 0% -> 0% of each run, Pallas kernels for 0% -> 6%
where the time goes in v3:
time: 38.4 us; the launch traced here: 38.1 us
  blocking collectives  26.5 us (69%)
  starting transfers between devices  5.08 us (13%)
  Pallas kernels  5.01 us (13%)
  waiting for transfers between devices  1.47 us (4%)
    all_to_all x1, blocking collectives, compact_shards(): lax.all_to_all(sent.reshape(lat_count * chips, block_rows, 128), both, sp...  14.6 us
    all_to_all x1, blocking collectives, compact_shards(): lax.all_to_all(parts.reshape(lat_count * chips, part_rows, columns_here),...  11.9 us
    ppermute x1, starting transfers between devices, compact_shards(): lax.ppermute(mix_weight, both, [(a * groups + b, (a ^ 1) * groups + b) fo...  5.08 us
    pallas_call x1, Pallas kernels, compact_shards(): pl.pallas_call(functools.partial(analysis_kernel, math.sqrt(latitudes / d...  2.34 us
    pallas_call x1, Pallas kernels, compact_shards(): pl.pallas_call(functools.partial(synthesis_kernel, 96), in_specs=[whole]...  1.86 us
    ppermute x1, waiting for transfers between devices, compact_shards(): lax.ppermute(own, both, [(n, n ^ 1) for n in range(lat_count * groups)])  1.47 us
  transfers between devices with their start and end apart: 2, of which 1 were waited for; matrix products, arithmetic and copies ran while one was open for 0% of the time, Pallas kernels for 6%

profile of v3, /device:TPU:0, one launch (start us, length us, event | category | flops | bytes accessed | tf_op | source)
XLA Modules:
  0.0 38.1 jit_solution(2779799497602765798)
XLA Ops:
  0.0 0.0 copy-start.5
  0.0 5.1 %collective-permute-start.1 = (bf16[1024,256]{1,0:T(8,128)(2,1)}, bf16[1024,256]{1,0:T(8,128)(2,1)S(1)}, u32[]{:S(2)}, u32[]{:S(2)}) collective-permute-start(bf16[1024,256]{1,0:T(8,128)(2,1)} %weight_ref.1), channel_id=1, source_target_pairs={{0,4},{2,6},{5,1},{7,3},{8,12},{10,14},{13,9},{15,11},{16,20},{18,... | collective-permute-start | bytes 1572872 | tf_op jit(solution)/shard_map/ppermute | solution.py:239
  5.1 2.3 %shard_map.100 = bf16[4,2,144,128]{3,2,1,0:T(8,128)(2,1)S(1)} custom-call(bf16[2,1440,256]{2,1,0:T(8,128)(2,1)} %grid_ref.1, bf16[3,128,480]{2,1,0:T(8,128)(2,1)} %constant.10.clone.table_hbm, bf16[4,8,512]{2,1,0:T(8,128)(2,1)} %bitcast.13, f32[1,512]{1,0:T(1,128)} %bitcast.14, s32[1,64]{1,0:T(1,128)} %bitcast.15), custom_call_target="tpu_custom_call" | custom-call | tf_op jit(solution)/shard_map/pallas_call | solution.py:250
  7.4 14.6 %all_to_all.10 = bf16[8,144,128]{2,1,0:T(8,128)(2,1)S(1)} all-to-all(bf16[8,144,128]{2,1,0:T(8,128)(2,1)S(1)} %bitcast.9), channel_id=1, replica_groups={{0,2,4,6,8,10,12,14},{1,3,5,7,9,11,13,15},{16,18,20,22,24,26,28,30},{17..., dimensions={0} | all-to-all | bytes 589824 | tf_op jit(solution)/shard_map/all_to_all | solution.py:278
  22.0 0.0 copy-start.2
  22.0 0.0 copy-start.3
  22.0 0.0 copy-start.4
  22.0 0.0 collective-permute-start
  22.0 0.0 collective-permute-done.1.moved_ref
  22.0 0.0 copy-done.5
  22.0 0.1 shard_map.101.weight_ref
  22.1 0.0 copy-start
  22.1 0.0 copy-start.1
  22.1 1.5 %collective-permute-done = bf16[8,144,128]{2,1,0:T(8,128)(2,1)S(1)} collective-permute-done((bf16[8,144,128]{2,1,0:T(8,128)(2,1)S(1)}, bf16[8,144,128]{2,1,0:T(8,128)(2,1)S(1)}, u32[]{:S(2)}, u32[]{:S(2)}) %collective-permute-start) | collective-permute-done | bytes 294944 | tf_op jit(solution)/shard_map/ppermute | solution.py:286
  23.6 0.0 copy-done.2
  23.6 0.0 copy-done.3
  23.6 0.0 copy-done.4
  23.6 0.8 %shard_map.102 = bf16[4,2,64,256]{3,2,1,0:T(8,128)(2,1)S(1)} custom-call(bf16[4,2,144,128]{3,2,1,0:T(8,128)(2,1)S(1)} %bitcast.8, bf16[4,2,144,128]{3,2,1,0:T(8,128)(2,1)S(1)} %bitcast.12, bf16[1024,256]{1,0:T(8,128)(2,1)S(1)} %shard_map.101.weight_ref, bf16[256,128]{1,0:T(8,128)(2,1)S(1)} %copy-done.4, bf16[128,512]{1,0:T(8,128)(2,1)S(1)} %copy-done.3, ...), custom_call_target="tpu_custom_call" | custom-call | tf_op jit(solution)/shard_map/pallas_call | solution.py:290
  24.4 11.9 %all_to_all.11 = bf16[8,64,256]{2,1,0:T(8,128)(2,1)S(1)} all-to-all(bf16[8,64,256]{2,1,0:T(8,128)(2,1)S(1)} %bitcast.11), channel_id=1, replica_groups={{0,2,4,6,8,10,12,14},{1,3,5,7,9,11,13,15},{16,18,20,22,24,26,28,30},{17..., dimensions={0} | all-to-all | bytes 524288 | tf_op jit(solution)/shard_map/all_to_all | solution.py:295
  36.3 0.0 copy-done
  36.3 0.0 copy-done.1
  36.3 1.9 %shard_map.103 = bf16[2,1440,256]{2,1,0:T(8,128)(2,1)} custom-call(bf16[4,2,64,256]{3,2,1,0:T(8,128)(2,1)S(1)} %bitcast.10, bf16[2,1440,256]{2,1,0:T(8,128)(2,1)S(1)} %copy-done, bf16[1440,128]{1,0:T(8,128)(2,1)S(1)} %copy-done.1), custom_call_target="tpu_custom_call" | custom-call | tf_op jit(solution)/shard_map/pallas_call | solution.py:305
Async XLA Ops:
  0.0 22.0 %copy-start.5 = (bf16[1024,256]{1,0:T(8,128)(2,1)S(1)}, bf16[1024,256]{1,0:T(8,128)(2,1)}, u32[]{:S(2)}) copy-start(bf16[1024,256]{1,0:T(8,128)(2,1)} %weight_ref.1) | copy-start | bytes 1572868
  0.0 22.0 %collective-permute-start.1 = (bf16[1024,256]{1,0:T(8,128)(2,1)}, bf16[1024,256]{1,0:T(8,128)(2,1)S(1)}, u32[]{:S(2)}, u32[]{:S(2)}) collective-permute-start(bf16[1024,256]{1,0:T(8,128)(2,1)} %weight_ref.1), channel_id=1, source_target_pairs={{0,4},{2,6},{5,1},{7,3},{8,12},{10,14},{13,9},{15,11},{16,20},{18,... | collective-permute-start | bytes 1572872 | tf_op jit(solution)/shard_map/ppermute | solution.py:239
  22.0 1.6 %copy-start.2 = (bf16[256,256]{1,0:T(8,128)(2,1)S(1)}, bf16[256,256]{1,0:T(8,128)(2,1)}, u32[]{:S(2)}) copy-start(bf16[256,256]{1,0:T(8,128)(2,1)} %constant.13.clone.same_ref) | copy-start | bytes 393220
  22.0 1.6 %copy-start.3 = (bf16[128,512]{1,0:T(8,128)(2,1)S(1)}, bf16[128,512]{1,0:T(8,128)(2,1)}, u32[]{:S(2)}) copy-start(bf16[128,512]{1,0:T(8,128)(2,1)} %constant.12.clone.halves_ref) | copy-start | bytes 393220
  22.0 1.6 %copy-start.4 = (bf16[256,128]{1,0:T(8,128)(2,1)S(1)}, bf16[256,128]{1,0:T(8,128)(2,1)}, u32[]{:S(2)}) copy-start(bf16[256,128]{1,0:T(8,128)(2,1)} %constant.11.clone.keep_ref) | copy-start | bytes 196612
  22.0 1.6 %collective-permute-start = (bf16[8,144,128]{2,1,0:T(8,128)(2,1)S(1)}, bf16[8,144,128]{2,1,0:T(8,128)(2,1)S(1)}, u32[]{:S(2)}, u32[]{:S(2)}) collective-permute-start(bf16[8,144,128]{2,1,0:T(8,128)(2,1)S(1)} %all_to_all.10), channel_id=1, source_target_pairs={{0,1},{1,0},{2,3},{3,2},{4,5},{5,4},{6,7},{7,6},{8,9},{9,8},{10,11... | collective-permute-start | bytes 884744 | tf_op jit(solution)/shard_map/ppermute | solution.py:286
  22.1 14.2 %copy-start = (bf16[2,1440,256]{2,1,0:T(8,128)(2,1)S(1)}, bf16[2,1440,256]{2,1,0:T(8,128)(2,1)}, u32[]{:S(2)}) copy-start(bf16[2,1440,256]{2,1,0:T(8,128)(2,1)} %grid_ref.1) | copy-start | bytes 4423684
  22.1 14.2 %copy-start.1 = (bf16[1440,128]{1,0:T(8,128)(2,1)S(1)}, bf16[1440,128]{1,0:T(8,128)(2,1)}, u32[]{:S(2)}) copy-start(bf16[1440,128]{1,0:T(8,128)(2,1)} %constant.14.clone.table_ref) | copy-start | bytes 1105924

commit v4 on v3

--- a/solution.py
+++ b/solution.py
@@ -10,6 +10,7 @@
 from jax.sharding import PartitionSpec as P
 
 MIB = 1024 * 1024
+STEPS = (3, 1, 2, 0)
 ROOT = math.sqrt(2.0 / math.pi)
 
 
@@ -141,7 +142,8 @@
         out_ref[...] = moved_ref[...]
 
 
-def mixing_kernel(own_ref, other_ref, weight_ref, keep_ref, halves_ref, same_ref, out_ref):
+def mixing_kernel(own_ref, other_ref, weight_ref, keep_ref, halves_ref, same_ref, *out_and_scratch):
+    outs, held = out_and_scratch[:-1], out_and_scratch[-1]
     lat_count, chips, block_rows, _ = own_ref.shape
     count = same_ref.shape[0]
     part_rows = count // lat_count
@@ -175,28 +177,26 @@
         + jnp.dot(high, mixed_low, preferred_element_type=jnp.float32)
         + jnp.dot(low, mixed_high, preferred_element_type=jnp.float32)
     )
-    out_ref[...] = jnp.zeros(out_ref.shape, out_ref.dtype)
-    to_chip = lax.axis_index("lat") // 2
-    out_ref[:, to_chip] = synthesis.astype(jnp.bfloat16).reshape((lat_count,) + out_ref.shape[2:])
-
-
-def synthesis_kernel(piece, received_ref, grid_ref, table_ref, out_hbm, out_buf, out_sem):
+    held[...] = synthesis.astype(jnp.bfloat16).reshape(held.shape)
+    place = lax.axis_index("chan") - core + lax.rem(lax.axis_index("lat"), 2)
+    for step, out_ref in zip(STEPS, outs):
+        out_ref[...] = held[place ^ step]
+
+
+def synthesis_kernel(piece, *refs):
+    received = refs[:-6]
+    grid_ref, table_ref, out_hbm, held, out_buf, out_sem = refs[-6:]
     lat_dev, longitudes, channels = grid_ref.shape
-    _, chips, part_rows, _ = received_ref.shape
+    groups, part_rows, _ = held.shape
     group_rows = part_rows // lat_dev
-    pair = lax.axis_index("chan") // 2 * 2
+    for step, received_ref in zip(STEPS, received):
+        sender = lax.axis_index("lat") ^ step
+        held[lax.rem(sender, 2) * (groups // 2) + sender // 2] = received_ref[...]
     parts = out_sem.shape[1]
     size = longitudes // parts
     copies = []
     for t in range(lat_dev):
-        rows = jnp.concatenate(
-            [
-                received_ref[pair + g, x, t * group_rows : (t + 1) * group_rows, :]
-                for g in range(2)
-                for x in range(chips)
-            ],
-            axis=0,
-        )
+        rows = held[:, t * group_rows : (t + 1) * group_rows, :].reshape(groups * group_rows, channels)
         for k in range(parts):
             for at in range(k * size, (k + 1) * size, piece):
                 half = jnp.dot(table_ref[at : at + piece, :], rows, preferred_element_type=jnp.float32)
@@ -289,30 +289,30 @@
     columns_here = mix_weight.shape[1]
     parts = pl.pallas_call(
         mixing_kernel,
-        out_shape=jax.ShapeDtypeStruct((lat_count, chips, part_rows, columns_here), jnp.bfloat16),
+        out_shape=[jax.ShapeDtypeStruct((part_rows, columns_here), jnp.bfloat16)] * lat_count,
+        scratch_shapes=[pltpu.VMEM((lat_count, part_rows, columns_here), jnp.bfloat16)],
         compiler_params=pltpu.CompilerParams(vmem_limit_bytes=24 * MIB),
     )(*(rows.reshape(lat_count, chips, block_rows, 128) for rows in (own, other)), weight, *helpers)
-    received = lax.all_to_all(
-        parts.reshape(lat_count * chips, part_rows, columns_here),
-        both,
-        split_axis=0,
-        concat_axis=0,
-        tiled=True,
-        axis_index_groups=cores,
-    ).reshape(lat_count, chips, part_rows, columns_here)
+    received = []
+    for step, part in zip(STEPS, parts):
+        pairs = [
+            (a * groups + b, ((b // 2 * 2 + a % 2) ^ step) * groups + a // 2 * 2 + b % 2) for a, b in places
+        ]
+        received.append(lax.ppermute(part, both, pairs))
 
     whole = pl.BlockSpec(memory_space=pltpu.VMEM)
     return pl.pallas_call(
         functools.partial(synthesis_kernel, 96),
-        in_specs=[whole] * 3,
+        in_specs=[whole] * (lat_count + 2),
         out_specs=hbm,
         out_shape=jax.ShapeDtypeStruct(grid_input.shape, jnp.bfloat16),
         scratch_shapes=[
+            pltpu.VMEM((groups, part_rows, channels), jnp.bfloat16),
             pltpu.VMEM(grid_input.shape, jnp.bfloat16),
             pltpu.SemaphoreType.DMA((lat_dev, 3)),
         ],
         compiler_params=pltpu.CompilerParams(vmem_limit_bytes=24 * MIB),
-    )(received, grid_input, jnp.asarray(inverse))
+    )(*received, grid_input, jnp.asarray(inverse))
 
 
 def wide_shards(grid_input, legendre, mix_weight, degree_gain, order_slot):
@@ -372,8 +372,7 @@
     lat_count, chan_count = lax.axis_size("lat"), lax.axis_size("chan")
     orders, latitudes = order_slot.shape[0], legendre.shape[2]
     compact = (
-        lat_count == chan_count
-        and chan_count % 2 == 0
+        lat_count == chan_count == len(STEPS)
         and 2 * latitudes * latitudes == 128
         and orders % (16 * chan_count) == 0
         and grid_input.shape[2] % 128 == 0

time: 38.4 us -> 35.2 us (0.917)
  the two profiles are of different devices: /device:TPU:0 before, /device:TPU:16 now
where the time goes in v4:
time: 35.2 us; the launch traced here: 34.9 us
  blocking collectives  12.6 us (36%)
  starting transfers between devices  10.8 us (31%)
  waiting for transfers between devices  6.36 us (18%)
  Pallas kernels  5.03 us (14%)
    all_to_all x1, blocking collectives, compact_shards(): lax.all_to_all(sent.reshape(lat_count * chips, block_rows, 128), both, sp...  12.6 us
    ppermute x4, starting transfers between devices, compact_shards(): received.append(lax.ppermute(part, both, pairs))  7.19 us
    ppermute x4, waiting for transfers between devices, compact_shards(): received.append(lax.ppermute(part, both, pairs))  4.89 us
    ppermute x1, starting transfers between devices, compact_shards(): lax.ppermute(mix_weight, both, [(a * groups + b, (a ^ 1) * groups + b) fo...  3.63 us
    pallas_call x1, Pallas kernels, compact_shards(): pl.pallas_call(functools.partial(analysis_kernel, math.sqrt(latitudes / d...  2.34 us
    pallas_call x1, Pallas kernels, compact_shards(): pl.pallas_call(functools.partial(synthesis_kernel, 96), in_specs=[whole]...  1.87 us
    ppermute x1, waiting for transfers between devices, compact_shards(): lax.ppermute(own, both, [(n, n ^ 1) for n in range(lat_count * groups)])  1.47 us
    pallas_call x1, Pallas kernels, compact_shards(): pl.pallas_call(mixing_kernel, out_shape=[jax.ShapeDtypeStruct((part_rows,...  0.77 us
  transfers between devices with their start and end apart: 6, of which 3 were waited for; matrix products, arithmetic and copies ran while one was open for 0% of the time, Pallas kernels for 7%

profile of v4, /device:TPU:16, one launch (start us, length us, event | category | flops | bytes accessed | tf_op | source)
XLA Modules:
  0.0 34.9 jit_solution(7847035012430413525)
XLA Ops:
  0.0 0.0 copy-start.5
  0.0 3.6 %collective-permute-start.1 = (bf16[1024,256]{1,0:T(8,128)(2,1)}, bf16[1024,256]{1,0:T(8,128)(2,1)S(1)}, u32[]{:S(2)}, u32[]{:S(2)}) collective-permute-start(bf16[1024,256]{1,0:T(8,128)(2,1)} %weight_ref.1), channel_id=1, source_target_pairs={{0,4},{2,6},{5,1},{7,3},{8,12},{10,14},{13,9},{15,11},{16,20},{18,... | collective-permute-start | bytes 1572872 | tf_op jit(solution)/shard_map/ppermute | solution.py:239
  3.6 2.3 %shard_map.100 = bf16[4,2,144,128]{3,2,1,0:T(8,128)(2,1)S(1)} custom-call(bf16[2,1440,256]{2,1,0:T(8,128)(2,1)} %refs_4_.1, bf16[3,128,480]{2,1,0:T(8,128)(2,1)} %constant.10.clone.table_hbm, bf16[4,8,512]{2,1,0:T(8,128)(2,1)} %bitcast.9, f32[1,512]{1,0:T(1,128)} %bitcast.10, s32[1,64]{1,0:T(1,128)} %bitcast.11), custom_call_target="tpu_custom_call" | custom-call | tf_op jit(solution)/shard_map/pallas_call | solution.py:250
  6.0 12.6 %all_to_all.5 = bf16[8,144,128]{2,1,0:T(8,128)(2,1)S(1)} all-to-all(bf16[8,144,128]{2,1,0:T(8,128)(2,1)S(1)} %bitcast.7), channel_id=1, replica_groups={{0,2,4,6,8,10,12,14},{1,3,5,7,9,11,13,15},{16,18,20,22,24,26,28,30},{17..., dimensions={0} | all-to-all | bytes 589824 | tf_op jit(solution)/shard_map/all_to_all | solution.py:278
  18.6 0.0 copy-start.2
  18.6 0.0 copy-start.3
  18.6 0.0 copy-start.4
  18.6 0.0 collective-permute-start
  18.6 0.0 collective-permute-done.1.moved_ref
  18.6 0.0 copy-done.5
  18.6 0.0 copy-start
  18.6 0.1 shard_map.101.weight_ref
  18.7 0.0 copy-start.1
  18.7 1.5 %collective-permute-done = bf16[8,144,128]{2,1,0:T(8,128)(2,1)S(1)} collective-permute-done((bf16[8,144,128]{2,1,0:T(8,128)(2,1)S(1)}, bf16[8,144,128]{2,1,0:T(8,128)(2,1)S(1)}, u32[]{:S(2)}, u32[]{:S(2)}) %collective-permute-start) | collective-permute-done | bytes 294944 | tf_op jit(solution)/shard_map/ppermute | solution.py:286
  20.2 0.0 copy-done.2
  20.2 0.0 copy-done.3
  20.2 0.0 copy-done.4
  20.2 0.8 %shard_map.102 = (bf16[64,256]{1,0:T(8,128)(2,1)S(1)}, bf16[64,256]{1,0:T(8,128)(2,1)S(1)}, bf16[64,256]{1,0:T(8,128)(2,1)S(1)}, bf16[64,256]{1,0:T(8,128)(2,1)S(1)}) custom-call(bf16[4,2,144,128]{3,2,1,0:T(8,128)(2,1)S(1)} %bitcast.6, bf16[4,2,144,128]{3,2,1,0:T(8,128)(2,1)S(1)} %bitcast.8, bf16[1024,256]{1,0:T(8,128)(2,1)S(1)} %shard_map.101.weight_ref, ...), custom_call_target="tpu_custom_call" | custom-call | tf_op jit(solution)/shard_map/pallas_call | solution.py:290
  21.0 1.6 %collective-permute-start.2 = (bf16[64,256]{1,0:T(8,128)(2,1)S(1)}, bf16[64,256]{1,0:T(8,128)(2,1)S(1)}, u32[]{:S(2)}, u32[]{:S(2)}) collective-permute-start(bf16[64,256]{1,0:T(8,128)(2,1)S(1)} %get-tuple-element.9), channel_id=1, source_target_pairs={{0,12},{1,13},{2,4},{3,5},{4,8},{5,9},{6,0},{7,1},{8,14},{9,15},{1... | collective-permute-start | bytes 98312 | tf_op jit(solution)/shard_map/ppermute | solution.py:301
  22.5 2.3 %collective-permute-start.3 = (bf16[64,256]{1,0:T(8,128)(2,1)S(1)}, bf16[64,256]{1,0:T(8,128)(2,1)S(1)}, u32[]{:S(2)}, u32[]{:S(2)}) collective-permute-start(bf16[64,256]{1,0:T(8,128)(2,1)S(1)} %get-tuple-element.10), channel_id=1, source_target_pairs={{0,4},{1,5},{2,12},{3,13},{4,0},{5,1},{6,8},{7,9},{8,6},{9,7},{10,... | collective-permute-start | bytes 98312 | tf_op jit(solution)/shard_map/ppermute | solution.py:301
  24.8 0.7 %collective-permute-start.4 = (bf16[64,256]{1,0:T(8,128)(2,1)S(1)}, bf16[64,256]{1,0:T(8,128)(2,1)S(1)}, u32[]{:S(2)}, u32[]{:S(2)}) collective-permute-start(bf16[64,256]{1,0:T(8,128)(2,1)S(1)} %get-tuple-element.11), channel_id=1, source_target_pairs={{0,8},{1,9},{2,0},{3,1},{4,12},{5,13},{6,4},{7,5},{8,10},{9,11},{1... | collective-permute-start | bytes 98312 | tf_op jit(solution)/shard_map/ppermute | solution.py:301
  25.5 2.7 %collective-permute-start.5 = (bf16[64,256]{1,0:T(8,128)(2,1)S(1)}, bf16[64,256]{1,0:T(8,128)(2,1)S(1)}, u32[]{:S(2)}, u32[]{:S(2)}) collective-permute-start(bf16[64,256]{1,0:T(8,128)(2,1)S(1)} %get-tuple-element.12), channel_id=1, source_target_pairs={{0,0},{1,1},{2,8},{3,9},{4,4},{5,5},{6,12},{7,13},{8,2},{9,3},{10,... | collective-permute-start | bytes 98312 | tf_op jit(solution)/shard_map/ppermute | solution.py:301
  28.2 0.0 collective-permute-done.2.refs_0_
  28.2 0.0 collective-permute-done.3.refs_1_
  28.2 1.4 %collective-permute-done.4.refs_2_ = bf16[64,256]{1,0:T(8,128)(2,1)S(1)} collective-permute-done((bf16[64,256]{1,0:T(8,128)(2,1)S(1)}, bf16[64,256]{1,0:T(8,128)(2,1)S(1)}, u32[]{:S(2)}, u32[]{:S(2)}) %collective-permute-start.4) | collective-permute-done | bytes 32800 | tf_op jit(solution)/shard_map/ppermute | solution.py:301
  29.6 3.4 %collective-permute-done.5.refs_3_ = bf16[64,256]{1,0:T(8,128)(2,1)S(1)} collective-permute-done((bf16[64,256]{1,0:T(8,128)(2,1)S(1)}, bf16[64,256]{1,0:T(8,128)(2,1)S(1)}, u32[]{:S(2)}, u32[]{:S(2)}) %collective-permute-start.5) | collective-permute-done | bytes 32800 | tf_op jit(solution)/shard_map/ppermute | solution.py:301
  33.1 0.0 copy-done
  33.1 0.0 copy-done.1
  33.1 1.9 %shard_map.103 = bf16[2,1440,256]{2,1,0:T(8,128)(2,1)} custom-call(bf16[64,256]{1,0:T(8,128)(2,1)S(1)} %collective-permute-done.2.refs_0_, bf16[64,256]{1,0:T(8,128)(2,1)S(1)} %collective-permute-done.3.refs_1_, bf16[64,256]{1,0:T(8,128)(2,1)S(1)} %collective-permute-done.4.refs_2_, bf16[64,256]{1,0:T(8,128)(2,1)S(1)} %collective-permute-done.5.refs_3_, ...), custom_call_target="tpu_custom_call" | custom-call | tf_op jit(solution)/shard_map/pallas_call | solution.py:304
Async XLA Ops:
  0.0 18.6 %copy-start.5 = (bf16[1024,256]{1,0:T(8,128)(2,1)S(1)}, bf16[1024,256]{1,0:T(8,128)(2,1)}, u32[]{:S(2)}) copy-start(bf16[1024,256]{1,0:T(8,128)(2,1)} %weight_ref.1) | copy-start | bytes 1572868
  0.0 18.6 %collective-permute-start.1 = (bf16[1024,256]{1,0:T(8,128)(2,1)}, bf16[1024,256]{1,0:T(8,128)(2,1)S(1)}, u32[]{:S(2)}, u32[]{:S(2)}) collective-permute-start(bf16[1024,256]{1,0:T(8,128)(2,1)} %weight_ref.1), channel_id=1, source_target_pairs={{0,4},{2,6},{5,1},{7,3},{8,12},{10,14},{13,9},{15,11},{16,20},{18,... | collective-permute-start | bytes 1572872 | tf_op jit(solution)/shard_map/ppermute | solution.py:239
  18.6 1.6 %copy-start.2 = (bf16[256,256]{1,0:T(8,128)(2,1)S(1)}, bf16[256,256]{1,0:T(8,128)(2,1)}, u32[]{:S(2)}) copy-start(bf16[256,256]{1,0:T(8,128)(2,1)} %constant.13.clone.same_ref) | copy-start | bytes 393220
  18.6 1.6 %copy-start.3 = (bf16[128,512]{1,0:T(8,128)(2,1)S(1)}, bf16[128,512]{1,0:T(8,128)(2,1)}, u32[]{:S(2)}) copy-start(bf16[128,512]{1,0:T(8,128)(2,1)} %constant.12.clone.halves_ref) | copy-start | bytes 393220
  18.6 1.6 %copy-start.4 = (bf16[256,128]{1,0:T(8,128)(2,1)S(1)}, bf16[256,128]{1,0:T(8,128)(2,1)}, u32[]{:S(2)}) copy-start(bf16[256,128]{1,0:T(8,128)(2,1)} %constant.11.clone.keep_ref) | copy-start | bytes 196612
  18.6 1.6 %collective-permute-start = (bf16[8,144,128]{2,1,0:T(8,128)(2,1)S(1)}, bf16[8,144,128]{2,1,0:T(8,128)(2,1)S(1)}, u32[]{:S(2)}, u32[]{:S(2)}) collective-permute-start(bf16[8,144,128]{2,1,0:T(8,128)(2,1)S(1)} %all_to_all.5), channel_id=1, source_target_pairs={{0,1},{1,0},{2,3},{3,2},{4,5},{5,4},{6,7},{7,6},{8,9},{9,8},{10,11... | collective-permute-start | bytes 884744 | tf_op jit(solution)/shard_map/ppermute | solution.py:286
  18.6 14.5 %copy-start = (bf16[2,1440,256]{2,1,0:T(8,128)(2,1)S(1)}, bf16[2,1440,256]{2,1,0:T(8,128)(2,1)}, u32[]{:S(2)}) copy-start(bf16[2,1440,256]{2,1,0:T(8,128)(2,1)} %refs_4_.1) | copy-start | bytes 4423684
  18.7 14.4 %copy-start.1 = (bf16[1440,128]{1,0:T(8,128)(2,1)S(1)}, bf16[1440,128]{1,0:T(8,128)(2,1)}, u32[]{:S(2)}) copy-start(bf16[1440,128]{1,0:T(8,128)(2,1)} %constant.14.clone.refs_5_) | copy-start | bytes 1105924
  21.0 7.2 %collective-permute-start.2 = (bf16[64,256]{1,0:T(8,128)(2,1)S(1)}, bf16[64,256]{1,0:T(8,128)(2,1)S(1)}, u32[]{:S(2)}, u32[]{:S(2)}) collective-permute-start(bf16[64,256]{1,0:T(8,128)(2,1)S(1)} %get-tuple-element.9), channel_id=1, source_target_pairs={{0,12},{1,13},{2,4},{3,5},{4,8},{5,9},{6,0},{7,1},{8,14},{9,15},{1... | collective-permute-start | bytes 98312 | tf_op jit(solution)/shard_map/ppermute | solution.py:301
  22.5 5.7 %collective-permute-start.3 = (bf16[64,256]{1,0:T(8,128)(2,1)S(1)}, bf16[64,256]{1,0:T(8,128)(2,1)S(1)}, u32[]{:S(2)}, u32[]{:S(2)}) collective-permute-start(bf16[64,256]{1,0:T(8,128)(2,1)S(1)} %get-tuple-element.10), channel_id=1, source_target_pairs={{0,4},{1,5},{2,12},{3,13},{4,0},{5,1},{6,8},{7,9},{8,6},{9,7},{10,... | collective-permute-start | bytes 98312 | tf_op jit(solution)/shard_map/ppermute | solution.py:301
  24.8 4.8 %collective-permute-start.4 = (bf16[64,256]{1,0:T(8,128)(2,1)S(1)}, bf16[64,256]{1,0:T(8,128)(2,1)S(1)}, u32[]{:S(2)}, u32[]{:S(2)}) collective-permute-start(bf16[64,256]{1,0:T(8,128)(2,1)S(1)} %get-tuple-element.11), channel_id=1, source_target_pairs={{0,8},{1,9},{2,0},{3,1},{4,12},{5,13},{6,4},{7,5},{8,10},{9,11},{1... | collective-permute-start | bytes 98312 | tf_op jit(solution)/shard_map/ppermute | solution.py:301
  25.5 7.6 %collective-permute-start.5 = (bf16[64,256]{1,0:T(8,128)(2,1)S(1)}, bf16[64,256]{1,0:T(8,128)(2,1)S(1)}, u32[]{:S(2)}, u32[]{:S(2)}) collective-permute-start(bf16[64,256]{1,0:T(8,128)(2,1)S(1)} %get-tuple-element.12), channel_id=1, source_target_pairs={{0,0},{1,1},{2,8},{3,9},{4,4},{5,5},{6,12},{7,13},{8,2},{9,3},{10,... | collective-permute-start | bytes 98312 | tf_op jit(solution)/shard_map/ppermute | solution.py:301

commit v5 on v4

--- a/solution.py
+++ b/solution.py
@@ -10,6 +10,7 @@
 from jax.sharding import PartitionSpec as P
 
 MIB = 1024 * 1024
+PAIR_ROWS = 8
 STEPS = (3, 1, 2, 0)
 ROOT = math.sqrt(2.0 / math.pi)
 
@@ -68,7 +69,6 @@
     own = (lax.axis_index("lat") * lax.axis_size("chan") + lax.axis_index("chan")) * slot_count
     block = lax.broadcasted_iota(jnp.int32, (1, degrees), 1) // 64
     high_lane = lax.broadcasted_iota(jnp.int32, (1, lanes), 1) < lanes // 2
-    row = lax.broadcasted_iota(jnp.int32, (group_orders, lanes), 0)
     sums = []
     for s in range(slot_count):
         rows = legendre_buf[s].astype(jnp.float32)
@@ -85,19 +85,15 @@
         (((1,), (1,)), ((), ())),
         preferred_element_type=jnp.float32,
     )
-    placed = [jnp.zeros((group_orders, lanes), jnp.float32) for _ in range(groups)]
-    for s in range(slot_count):
-        order = slot_buf[0, own + s]
-        pair = pairs[:1, s * lanes : (s + 1) * lanes]
-        high = pair.astype(jnp.bfloat16).astype(jnp.float32)
-        pair = jnp.where(high_lane, high, pair - high)
-        for g in range(groups):
-            placed[g] = jnp.where(row == order - g * group_orders, pair, placed[g])
+    pairs = jnp.concatenate([pairs[:1, s * lanes : (s + 1) * lanes] for s in range(slot_count)], axis=0)
+    high = pairs.astype(jnp.bfloat16).astype(jnp.float32)
+    pairs = jnp.where(high_lane, high, pairs - high)
+    pairs = jnp.concatenate([pairs, jnp.zeros((PAIR_ROWS - slot_count, lanes), jnp.float32)], axis=0)
+    pairs = pairs.astype(jnp.bfloat16)
     top = lat_dev * group_rows * (channels // 128)
-    for g in range(groups):
-        value = placed[g].astype(jnp.bfloat16)
-        for a in range(g // chips, lat_count, 2):
-            out_ref[a, g % chips, top : top + group_orders] = value
+    for a in range(lat_count):
+        for x in range(chips):
+            out_ref[a, x, top : top + PAIR_ROWS] = pairs
 
     for t in range(lat_dev):
         total = None
@@ -130,6 +126,17 @@
     return [m.astype(jnp.bfloat16) for m in (keep, halves, same)]
 
 
+def slot_columns(lat_count, chips, slot_count):
+    lat, chip, row = np.indices((lat_count, chips, PAIR_ROWS)).reshape(3, -1)
+    slots = np.arange(lat_count * 2 * chips * slot_count)[:, None]
+    return np.stack(
+        [
+            (slots == ((lat * chips + chip) * 2 + core) * slot_count + row) & (row < slot_count)
+            for core in range(2)
+        ]
+    ).astype(jnp.bfloat16)
+
+
 def choose_kernel(weight_ref, moved_ref, out_ref):
     own = lax.rem(lax.axis_index("lat") + lax.axis_index("chan"), 2) == 0
 
@@ -142,29 +149,52 @@
         out_ref[...] = moved_ref[...]
 
 
-def mixing_kernel(own_ref, other_ref, weight_ref, keep_ref, halves_ref, same_ref, *out_and_scratch):
-    outs, held = out_and_scratch[:-1], out_and_scratch[-1]
-    lat_count, chips, block_rows, _ = own_ref.shape
-    count = same_ref.shape[0]
+def channel_products(rows_ref, weight_ref, sender, hit, count):
+    lat_count, chips, block_rows, _ = rows_ref.shape
     part_rows = count // lat_count
     channels = weight_ref.shape[0] // (2 * chips)
     split = channels // 128
-    group_orders = block_rows - split * part_rows
+    mixed = None
+    for x in range(chips):
+        block = jnp.concatenate(
+            [rows_ref[:, x, h * part_rows : (h + 1) * part_rows, :].reshape(count, 128) for h in range(split)], axis=1
+        )
+        at = pl.ds(pl.multiple_of((2 * x + sender) * channels, channels), channels)
+        term = jnp.dot(block, weight_ref[at, :], preferred_element_type=jnp.float32)
+        mixed = term if mixed is None else mixed + term
+    sent = [
+        rows_ref[a, x, split * part_rows :, :].astype(jnp.float32) for a in range(lat_count) for x in range(chips)
+    ]
+    sent = jnp.concatenate(sent, axis=0).astype(jnp.bfloat16)
+    return mixed, jnp.dot(hit, sent, preferred_element_type=jnp.float32)
+
+
+def first_half_kernel(rows_ref, weight_ref, order_ref, columns_ref, mixed_ref, pairs_ref, hit_ref):
+    group_orders = pairs_ref.shape[0]
+    chips = rows_ref.shape[1]
     core = lax.rem(lax.axis_index("chan"), 2)
-    mixed = None
-    pairs = None
-    for x in range(chips):
-        for rows_ref, sender in ((own_ref, core), (other_ref, 1 - core)):
-            block = jnp.concatenate(
-                [rows_ref[:, x, h * part_rows : (h + 1) * part_rows, :].reshape(count, 128) for h in range(split)],
-                axis=1,
-            )
-            at = pl.ds(pl.multiple_of((2 * x + sender) * channels, channels), channels)
-            term = jnp.dot(block, weight_ref[at, :], preferred_element_type=jnp.float32)
-            mixed = term if mixed is None else mixed + term
-            for a in range(lat_count):
-                sent = rows_ref[a, x, split * part_rows :, :].astype(jnp.float32)
-                pairs = sent if pairs is None else pairs + sent
+    group = lax.rem(lax.axis_index("lat"), 2) * chips + lax.axis_index("chan") // 2
+    orders = jnp.broadcast_to(order_ref[...].astype(jnp.float32), (8, order_ref.shape[1])).astype(jnp.bfloat16)
+    hits = []
+    for sender in (core, 1 - core):
+        order = jnp.dot(orders, columns_ref[sender], preferred_element_type=jnp.float32)[:1].astype(jnp.int32)
+        place = lax.broadcasted_iota(jnp.int32, (group_orders, order.shape[1]), 0) + group * group_orders
+        hits.append(jnp.where(place == order, 1.0, 0.0).astype(jnp.bfloat16))
+    mixed_ref[...], pairs_ref[...] = channel_products(rows_ref, weight_ref, core, hits[0], mixed_ref.shape[0])
+    hit_ref[...] = hits[1]
+
+
+def mixing_kernel(
+    mixed_ref, pairs_ref, hit_ref, rows_ref, weight_ref, keep_ref, halves_ref, same_ref, *out_and_scratch
+):
+    outs, held = out_and_scratch[:-1], out_and_scratch[-1]
+    lat_count = rows_ref.shape[0]
+    count = same_ref.shape[0]
+    group_orders = pairs_ref.shape[0]
+    core = lax.rem(lax.axis_index("chan"), 2)
+    mixed, pairs = channel_products(rows_ref, weight_ref, 1 - core, hit_ref[...], count)
+    mixed = mixed_ref[...] + mixed
+    pairs = pairs_ref[...] + pairs
     wide = jnp.concatenate([pairs] * (count // group_orders), axis=0) * keep_ref[...].astype(jnp.float32)
     matrix = jnp.dot(wide.astype(jnp.bfloat16), halves_ref[...], preferred_element_type=jnp.float32)
     same = same_ref[...].astype(jnp.float32)
@@ -213,7 +243,7 @@
 
 
 def chunk_of(longitudes):
-    return max(n for n in range(16, 481, 16) if longitudes % n == 0)
+    return max(n for n in range(16, 1441, 16) if longitudes % n == 0)
 
 
 def compact_shards(grid_input, legendre, mix_weight, degree_gain, order_slot):
@@ -226,7 +256,7 @@
     group_orders = orders // groups
     group_rows = 2 * group_orders
     part_rows = lat_dev * group_rows
-    block_rows = part_rows * (channels // 128) + group_orders
+    block_rows = part_rows * (channels // 128) + PAIR_ROWS
     chunk = chunk_of(longitudes)
     chunks = longitudes // chunk
     columns = grouped_columns(orders, groups)
@@ -287,12 +317,26 @@
 
     helpers = [jnp.asarray(m) for m in mixing_helpers(latitudes, group_orders)]
     columns_here = mix_weight.shape[1]
+    own = own.reshape(lat_count, chips, block_rows, 128)
+    other = other.reshape(lat_count, chips, block_rows, 128)
+    half = pl.pallas_call(
+        first_half_kernel,
+        out_shape=[
+            jax.ShapeDtypeStruct((lat_count * part_rows, columns_here), jnp.float32),
+            jax.ShapeDtypeStruct((group_orders, 128), jnp.float32),
+            jax.ShapeDtypeStruct((group_orders, lat_count * chips * PAIR_ROWS), jnp.bfloat16),
+        ],
+        cost_estimate=pl.CostEstimate(
+            flops=lat_count * part_rows * mix_weight.size, bytes_accessed=own.size * 2 + mix_weight.size, transcendentals=0
+        ),
+        compiler_params=pltpu.CompilerParams(vmem_limit_bytes=24 * MIB),
+    )(own, weight, order_slot.reshape(1, orders), jnp.asarray(slot_columns(lat_count, chips, slot_count)))
     parts = pl.pallas_call(
         mixing_kernel,
         out_shape=[jax.ShapeDtypeStruct((part_rows, columns_here), jnp.bfloat16)] * lat_count,
         scratch_shapes=[pltpu.VMEM((lat_count, part_rows, columns_here), jnp.bfloat16)],
         compiler_params=pltpu.CompilerParams(vmem_limit_bytes=24 * MIB),
-    )(*(rows.reshape(lat_count, chips, block_rows, 128) for rows in (own, other)), weight, *helpers)
+    )(*half, other, weight, *helpers)
     received = []
     for step, part in zip(STEPS, parts):
         pairs = [
@@ -375,6 +419,8 @@
         lat_count == chan_count == len(STEPS)
         and 2 * latitudes * latitudes == 128
         and orders % (16 * chan_count) == 0
+        and orders <= 256
+        and legendre.shape[0] <= PAIR_ROWS
         and grid_input.shape[2] % 128 == 0
         and grid_input.shape[1] % 16 == 0
     )

time: 35.2 us -> 34.4 us (0.977)
  the two profiles are of different devices: /device:TPU:16 before, /device:TPU:10 now
where the time goes in v5:
time: 34.4 us; the launch traced here: 34.2 us
  blocking collectives  14.6 us (42%)
  starting transfers between devices  9.64 us (28%)
  Pallas kernels  4.82 us (14%)
  waiting for transfers between devices  4.45 us (13%)
  local copies, waits for them, and re-layouts  0.58 us (2%)
    all_to_all x1, blocking collectives, compact_shards(): lax.all_to_all(sent.reshape(lat_count * chips, block_rows, 128), both, sp...  14.6 us
    ppermute x4, starting transfers between devices, compact_shards(): received.append(lax.ppermute(part, both, pairs))  8.16 us
    ppermute x4, waiting for transfers between devices, compact_shards(): received.append(lax.ppermute(part, both, pairs))  3.81 us
    pallas_call x1, Pallas kernels, compact_shards(): pl.pallas_call(functools.partial(analysis_kernel, math.sqrt(latitudes / d...  2.02 us
    pallas_call x1, Pallas kernels, compact_shards(): pl.pallas_call(functools.partial(synthesis_kernel, 96), in_specs=[whole]...  1.87 us
    ppermute x1, starting transfers between devices, compact_shards(): lax.ppermute(mix_weight, both, [(a * groups + b, (a ^ 1) * groups + b) fo...  1.41 us
  transfers between devices with their start and end apart: 6, of which 2 were waited for; matrix products, arithmetic and copies ran while one was open for 0% of the time, Pallas kernels for 7%

profile of v5, /device:TPU:10, one launch (start us, length us, event | category | flops | bytes accessed | tf_op | source)
XLA Modules:
  0.0 34.2 jit_solution(16784205626840211664)
XLA Ops:
  0.0 1.4 %collective-permute-start = (bf16[1024,256]{1,0:T(8,128)(2,1)}, bf16[1024,256]{1,0:T(8,128)(2,1)S(1)}, u32[]{:S(2)}, u32[]{:S(2)}) collective-permute-start(bf16[1024,256]{1,0:T(8,128)(2,1)} %weight_ref.1), channel_id=1, source_target_pairs={{0,4},{2,6},{5,1},{7,3},{8,12},{10,14},{13,9},{15,11},{16,20},{18,... | collective-permute-start | bytes 1572872 | tf_op jit(solution)/shard_map/ppermute | solution.py:269
  1.4 2.0 %shard_map.109 = bf16[4,2,136,128]{3,2,1,0:T(8,128)(2,1)S(1)} custom-call(bf16[2,1440,256]{2,1,0:T(8,128)(2,1)} %refs_4_.1, bf16[1,128,1440]{2,1,0:T(8,128)(2,1)} %constant.12.clone.table_hbm, bf16[4,8,512]{2,1,0:T(8,128)(2,1)} %bitcast.11, f32[1,512]{1,0:T(1,128)} %bitcast.12, s32[1,64]{1,0:T(1,128)} %bitcast.9), custom_call_target="tpu_custom_call" | custom-call | tf_op jit(solution)/shard_map/pallas_call | solution.py:280
  3.4 14.6 %all_to_all.5 = bf16[8,136,128]{2,1,0:T(8,128)(2,1)S(1)} all-to-all(bf16[8,136,128]{2,1,0:T(8,128)(2,1)S(1)} %bitcast.7), channel_id=1, replica_groups={{0,2,4,6,8,10,12,14},{1,3,5,7,9,11,13,15},{16,18,20,22,24,26,28,30},{17..., dimensions={0} | all-to-all | bytes 557056 | tf_op jit(solution)/shard_map/all_to_all | solution.py:308
  18.0 0.0 copy-start.5
  18.0 0.0 copy-start.6
  18.0 0.0 copy-start.2
  18.0 0.0 copy-start.4
  18.0 0.1 collective-permute-start.1
  18.1 0.0 collective-permute-done.moved_ref
  18.1 0.0 copy-done.7
  18.1 0.1 shard_map.110.weight_ref
  18.2 0.0 copy-start
  18.2 0.0 copy-start.1
  18.2 0.5 %copy-done.5 = bf16[2,64,64]{2,1,0:T(8,128)(2,1)S(1)} copy-done((bf16[2,64,64]{2,1,0:T(8,128)(2,1)S(1)}, bf16[2,64,64]{2,1,0:T(8,128)(2,1)}, u32[]{:S(2)}) %copy-start.5) | copy-done | bytes 16408
  18.8 0.0 copy-done.6
  18.8 0.2 shard_map.111
  19.0 0.6 %collective-permute-done.1 = bf16[8,136,128]{2,1,0:T(8,128)(2,1)S(1)} collective-permute-done((bf16[8,136,128]{2,1,0:T(8,128)(2,1)S(1)}, bf16[8,136,128]{2,1,0:T(8,128)(2,1)S(1)}, u32[]{:S(2)}, u32[]{:S(2)}) %collective-permute-start.1) | collective-permute-done | bytes 278560 | tf_op jit(solution)/shard_map/ppermute | solution.py:316
  19.7 0.0 copy-done.2
  19.7 0.0 copy-done.3
  19.7 0.0 copy-done.4
  19.7 0.6 %shard_map.112 = (bf16[64,256]{1,0:T(8,128)(2,1)S(1)}, bf16[64,256]{1,0:T(8,128)(2,1)S(1)}, bf16[64,256]{1,0:T(8,128)(2,1)S(1)}, bf16[64,256]{1,0:T(8,128)(2,1)S(1)}) custom-call(f32[256,256]{1,0:T(8,128)S(1)} %get-tuple-element.12.mixed_ref, f32[16,128]{1,0:T(8,128)S(1)} %get-tuple-element.13.pairs_ref, bf16[16,64]{1,0:T(8,128)(2,1)S(1)} %get-tuple-element.14.hit_ref, ...), custom_call_target="tpu_custom_call" | custom-call | tf_op jit(solution)/shard_map/pallas_call | solution.py:334
  20.3 2.4 %collective-permute-start.2 = (bf16[64,256]{1,0:T(8,128)(2,1)S(1)}, bf16[64,256]{1,0:T(8,128)(2,1)S(1)}, u32[]{:S(2)}, u32[]{:S(2)}) collective-permute-start(bf16[64,256]{1,0:T(8,128)(2,1)S(1)} %get-tuple-element.15), channel_id=1, source_target_pairs={{0,12},{1,13},{2,4},{3,5},{4,8},{5,9},{6,0},{7,1},{8,14},{9,15},{1... | collective-permute-start | bytes 98312 | tf_op jit(solution)/shard_map/ppermute | solution.py:345
  22.7 0.6 %collective-permute-start.3 = (bf16[64,256]{1,0:T(8,128)(2,1)S(1)}, bf16[64,256]{1,0:T(8,128)(2,1)S(1)}, u32[]{:S(2)}, u32[]{:S(2)}) collective-permute-start(bf16[64,256]{1,0:T(8,128)(2,1)S(1)} %get-tuple-element.16), channel_id=1, source_target_pairs={{0,4},{1,5},{2,12},{3,13},{4,0},{5,1},{6,8},{7,9},{8,6},{9,7},{10,... | collective-permute-start | bytes 98312 | tf_op jit(solution)/shard_map/ppermute | solution.py:345
  23.3 1.4 %collective-permute-start.4 = (bf16[64,256]{1,0:T(8,128)(2,1)S(1)}, bf16[64,256]{1,0:T(8,128)(2,1)S(1)}, u32[]{:S(2)}, u32[]{:S(2)}) collective-permute-start(bf16[64,256]{1,0:T(8,128)(2,1)S(1)} %get-tuple-element.17), channel_id=1, source_target_pairs={{0,8},{1,9},{2,0},{3,1},{4,12},{5,13},{6,4},{7,5},{8,10},{9,11},{1... | collective-permute-start | bytes 98312 | tf_op jit(solution)/shard_map/ppermute | solution.py:345
  24.7 3.8 %collective-permute-start.5 = (bf16[64,256]{1,0:T(8,128)(2,1)S(1)}, bf16[64,256]{1,0:T(8,128)(2,1)S(1)}, u32[]{:S(2)}, u32[]{:S(2)}) collective-permute-start(bf16[64,256]{1,0:T(8,128)(2,1)S(1)} %get-tuple-element.18), channel_id=1, source_target_pairs={{0,0},{1,1},{2,8},{3,9},{4,4},{5,5},{6,12},{7,13},{8,2},{9,3},{10,... | collective-permute-start | bytes 98312 | tf_op jit(solution)/shard_map/ppermute | solution.py:345
  28.5 0.0 collective-permute-done.2.refs_0_
  28.5 0.0 collective-permute-done.3.refs_1_
  28.5 0.0 collective-permute-done.4.refs_2_
  28.5 3.8 %collective-permute-done.5.refs_3_ = bf16[64,256]{1,0:T(8,128)(2,1)S(1)} collective-permute-done((bf16[64,256]{1,0:T(8,128)(2,1)S(1)}, bf16[64,256]{1,0:T(8,128)(2,1)S(1)}, u32[]{:S(2)}, u32[]{:S(2)}) %collective-permute-start.5) | collective-permute-done | bytes 32800 | tf_op jit(solution)/shard_map/ppermute | solution.py:345
  32.3 0.0 copy-done
  32.3 0.0 copy-done.1
  32.3 1.9 %shard_map.113 = bf16[2,1440,256]{2,1,0:T(8,128)(2,1)} custom-call(bf16[64,256]{1,0:T(8,128)(2,1)S(1)} %collective-permute-done.2.refs_0_, bf16[64,256]{1,0:T(8,128)(2,1)S(1)} %collective-permute-done.3.refs_1_, bf16[64,256]{1,0:T(8,128)(2,1)S(1)} %collective-permute-done.4.refs_2_, bf16[64,256]{1,0:T(8,128)(2,1)S(1)} %collective-permute-done.5.refs_3_, ...), custom_call_target="tpu_custom_call" | custom-call | tf_op jit(solution)/shard_map/pallas_call | solution.py:348
  (2 shorter events, 0.0 us)
Async XLA Ops:
  0.0 18.1 %copy-start.7 = (bf16[1024,256]{1,0:T(8,128)(2,1)S(1)}, bf16[1024,256]{1,0:T(8,128)(2,1)}, u32[]{:S(2)}) copy-start(bf16[1024,256]{1,0:T(8,128)(2,1)} %weight_ref.1) | copy-start | bytes 1572868
  0.0 18.1 %collective-permute-start = (bf16[1024,256]{1,0:T(8,128)(2,1)}, bf16[1024,256]{1,0:T(8,128)(2,1)S(1)}, u32[]{:S(2)}, u32[]{:S(2)}) collective-permute-start(bf16[1024,256]{1,0:T(8,128)(2,1)} %weight_ref.1), channel_id=1, source_target_pairs={{0,4},{2,6},{5,1},{7,3},{8,12},{10,14},{13,9},{15,11},{16,20},{18,... | collective-permute-start | bytes 1572872 | tf_op jit(solution)/shard_map/ppermute | solution.py:269
  18.0 0.8 %copy-start.5 = (bf16[2,64,64]{2,1,0:T(8,128)(2,1)S(1)}, bf16[2,64,64]{2,1,0:T(8,128)(2,1)}, u32[]{:S(2)}) copy-start(bf16[2,64,64]{2,1,0:T(8,128)(2,1)} %constant.16.clone.columns_ref) | copy-start | bytes 49156
  18.0 0.8 %copy-start.6 = (s32[64]{0:T(128)S(1)}, s32[64]{0:T(128)}, u32[]{:S(2)}) copy-start(s32[64]{0:T(128)} %param.15) | copy-start | bytes 772
  18.0 1.6 %copy-start.2 = (bf16[256,256]{1,0:T(8,128)(2,1)S(1)}, bf16[256,256]{1,0:T(8,128)(2,1)}, u32[]{:S(2)}) copy-start(bf16[256,256]{1,0:T(8,128)(2,1)} %constant.15.clone.same_ref) | copy-start | bytes 393220
  18.0 1.6 %copy-start.3 = (bf16[128,512]{1,0:T(8,128)(2,1)S(1)}, bf16[128,512]{1,0:T(8,128)(2,1)}, u32[]{:S(2)}) copy-start(bf16[128,512]{1,0:T(8,128)(2,1)} %constant.14.clone.halves_ref) | copy-start | bytes 393220
  18.0 1.6 %copy-start.4 = (bf16[256,128]{1,0:T(8,128)(2,1)S(1)}, bf16[256,128]{1,0:T(8,128)(2,1)}, u32[]{:S(2)}) copy-start(bf16[256,128]{1,0:T(8,128)(2,1)} %constant.13.clone.keep_ref) | copy-start | bytes 196612
  18.0 1.6 %collective-permute-start.1 = (bf16[8,136,128]{2,1,0:T(8,128)(2,1)S(1)}, bf16[8,136,128]{2,1,0:T(8,128)(2,1)S(1)}, u32[]{:S(2)}, u32[]{:S(2)}) collective-permute-start(bf16[8,136,128]{2,1,0:T(8,128)(2,1)S(1)} %all_to_all.5), channel_id=1, source_target_pairs={{0,1},{1,0},{2,3},{3,2},{4,5},{5,4},{6,7},{7,6},{8,9},{9,8},{10,11... | collective-permute-start | bytes 835592 | tf_op jit(solution)/shard_map/ppermute | solution.py:316
  18.2 14.1 %copy-start = (bf16[2,1440,256]{2,1,0:T(8,128)(2,1)S(1)}, bf16[2,1440,256]{2,1,0:T(8,128)(2,1)}, u32[]{:S(2)}) copy-start(bf16[2,1440,256]{2,1,0:T(8,128)(2,1)} %refs_4_.1) | copy-start | bytes 4423684
  18.2 14.1 %copy-start.1 = (bf16[1440,128]{1,0:T(8,128)(2,1)S(1)}, bf16[1440,128]{1,0:T(8,128)(2,1)}, u32[]{:S(2)}) copy-start(bf16[1440,128]{1,0:T(8,128)(2,1)} %constant.17.clone.refs_5_) | copy-start | bytes 1105924
  20.3 8.2 %collective-permute-start.2 = (bf16[64,256]{1,0:T(8,128)(2,1)S(1)}, bf16[64,256]{1,0:T(8,128)(2,1)S(1)}, u32[]{:S(2)}, u32[]{:S(2)}) collective-permute-start(bf16[64,256]{1,0:T(8,128)(2,1)S(1)} %get-tuple-element.15), channel_id=1, source_target_pairs={{0,12},{1,13},{2,4},{3,5},{4,8},{5,9},{6,0},{7,1},{8,14},{9,15},{1... | collective-permute-start | bytes 98312 | tf_op jit(solution)/shard_map/ppermute | solution.py:345
  22.7 5.8 %collective-permute-start.3 = (bf16[64,256]{1,0:T(8,128)(2,1)S(1)}, bf16[64,256]{1,0:T(8,128)(2,1)S(1)}, u32[]{:S(2)}, u32[]{:S(2)}) collective-permute-start(bf16[64,256]{1,0:T(8,128)(2,1)S(1)} %get-tuple-element.16), channel_id=1, source_target_pairs={{0,4},{1,5},{2,12},{3,13},{4,0},{5,1},{6,8},{7,9},{8,6},{9,7},{10,... | collective-permute-start | bytes 98312 | tf_op jit(solution)/shard_map/ppermute | solution.py:345
  23.3 5.2 %collective-permute-start.4 = (bf16[64,256]{1,0:T(8,128)(2,1)S(1)}, bf16[64,256]{1,0:T(8,128)(2,1)S(1)}, u32[]{:S(2)}, u32[]{:S(2)}) collective-permute-start(bf16[64,256]{1,0:T(8,128)(2,1)S(1)} %get-tuple-element.17), channel_id=1, source_target_pairs={{0,8},{1,9},{2,0},{3,1},{4,12},{5,13},{6,4},{7,5},{8,10},{9,11},{1... | collective-permute-start | bytes 98312 | tf_op jit(solution)/shard_map/ppermute | solution.py:345
  24.7 7.6 %collective-permute-start.5 = (bf16[64,256]{1,0:T(8,128)(2,1)S(1)}, bf16[64,256]{1,0:T(8,128)(2,1)S(1)}, u32[]{:S(2)}, u32[]{:S(2)}) collective-permute-start(bf16[64,256]{1,0:T(8,128)(2,1)S(1)} %get-tuple-element.18), channel_id=1, source_target_pairs={{0,0},{1,1},{2,8},{3,9},{4,4},{5,5},{6,12},{7,13},{8,2},{9,3},{10,... | collective-permute-start | bytes 98312 | tf_op jit(solution)/shard_map/ppermute | solution.py:345

commit v6 on v5

--- a/solution.py
+++ b/solution.py
@@ -11,6 +11,7 @@
 
 MIB = 1024 * 1024
 PAIR_ROWS = 8
+MEMBERS = ((0, 2, 4, 6, 1, 3, 5, 7), (5, 7, 1, 3, 4, 6, 0, 2))
 STEPS = (3, 1, 2, 0)
 ROOT = math.sqrt(2.0 / math.pi)
 
@@ -28,12 +29,17 @@
     return np.arange(2 * orders).reshape(2, groups, orders // groups).transpose(1, 0, 2).reshape(-1)
 
 
+def place_of(core, chip):
+    return jnp.where(core == 0, MEMBERS[0].index(chip), MEMBERS[1].index(chip))
+
+
 def analysis_kernel(
     factor, chunk, grid_hbm, table_hbm, legendre_hbm, gain_hbm, slot_hbm, out_ref,
     grid_buf, table_buf, legendre_buf, gain_buf, slot_buf, grid_sem, table_sem, small_sem,
 ):
-    lat_count, chips, _, _ = out_ref.shape
+    lat_count, chips = lax.axis_size("lat"), lax.axis_size("chan") // 2
     groups = 2 * chips
+    core = lax.rem(lax.axis_index("chan"), 2)
     lat_dev, longitudes, channels = grid_buf.shape
     slot_count, latitudes, degrees = legendre_buf.shape
     orders = slot_buf.shape[1]
@@ -93,7 +99,7 @@
     top = lat_dev * group_rows * (channels // 128)
     for a in range(lat_count):
         for x in range(chips):
-            out_ref[a, x, top : top + PAIR_ROWS] = pairs
+            out_ref[place_of(core, a * chips + x), top : top + PAIR_ROWS] = pairs
 
     for t in range(lat_dev):
         total = None
@@ -111,7 +117,7 @@
                 value = spectrum[g * group_rows : (g + 1) * group_rows, h * 128 : (h + 1) * 128]
                 at = (h * lat_dev + t) * group_rows
                 for a in range(g // chips, lat_count, 2):
-                    out_ref[a, g % chips, at : at + group_rows] = value
+                    out_ref[place_of(core, a * chips + g % chips), at : at + group_rows] = value
 
 
 def mixing_helpers(latitudes, group_orders):
@@ -127,7 +133,7 @@
 
 
 def slot_columns(lat_count, chips, slot_count):
-    lat, chip, row = np.indices((lat_count, chips, PAIR_ROWS)).reshape(3, -1)
+    chip, lat, row = np.indices((chips, lat_count, PAIR_ROWS)).reshape(3, -1)
     slots = np.arange(lat_count * 2 * chips * slot_count)[:, None]
     return np.stack(
         [
@@ -150,28 +156,32 @@
 
 
 def channel_products(rows_ref, weight_ref, sender, hit, count):
-    lat_count, chips, block_rows, _ = rows_ref.shape
+    lat_count, chips = lax.axis_size("lat"), lax.axis_size("chan") // 2
     part_rows = count // lat_count
     channels = weight_ref.shape[0] // (2 * chips)
     split = channels // 128
     mixed = None
+    sent = []
     for x in range(chips):
+        parts = [rows_ref[place_of(sender, a * chips + x)] for a in range(lat_count)]
         block = jnp.concatenate(
-            [rows_ref[:, x, h * part_rows : (h + 1) * part_rows, :].reshape(count, 128) for h in range(split)], axis=1
+            [
+                jnp.concatenate([part[h * part_rows : (h + 1) * part_rows] for part in parts], axis=0)
+                for h in range(split)
+            ],
+            axis=1,
         )
         at = pl.ds(pl.multiple_of((2 * x + sender) * channels, channels), channels)
         term = jnp.dot(block, weight_ref[at, :], preferred_element_type=jnp.float32)
         mixed = term if mixed is None else mixed + term
-    sent = [
-        rows_ref[a, x, split * part_rows :, :].astype(jnp.float32) for a in range(lat_count) for x in range(chips)
-    ]
+        sent += [part[split * part_rows :].astype(jnp.float32) for part in parts]
     sent = jnp.concatenate(sent, axis=0).astype(jnp.bfloat16)
     return mixed, jnp.dot(hit, sent, preferred_element_type=jnp.float32)
 
 
 def first_half_kernel(rows_ref, weight_ref, order_ref, columns_ref, mixed_ref, pairs_ref, hit_ref):
     group_orders = pairs_ref.shape[0]
-    chips = rows_ref.shape[1]
+    chips = lax.axis_size("chan") // 2
     core = lax.rem(lax.axis_index("chan"), 2)
     group = lax.rem(lax.axis_index("lat"), 2) * chips + lax.axis_index("chan") // 2
     orders = jnp.broadcast_to(order_ref[...].astype(jnp.float32), (8, order_ref.shape[1])).astype(jnp.bfloat16)
@@ -188,7 +198,7 @@
     mixed_ref, pairs_ref, hit_ref, rows_ref, weight_ref, keep_ref, halves_ref, same_ref, *out_and_scratch
 ):
     outs, held = out_and_scratch[:-1], out_and_scratch[-1]
-    lat_count = rows_ref.shape[0]
+    lat_count = len(outs)
     count = same_ref.shape[0]
     group_orders = pairs_ref.shape[0]
     core = lax.rem(lax.axis_index("chan"), 2)
@@ -280,7 +290,7 @@
     sent = pl.pallas_call(
         functools.partial(analysis_kernel, math.sqrt(latitudes / degrees), chunk),
         in_specs=[hbm] * 5,
-        out_shape=pltpu.VMEM((lat_count, chips, block_rows, 128), jnp.bfloat16),
+        out_shape=pltpu.VMEM((lat_count * chips, block_rows, 128), jnp.bfloat16),
         scratch_shapes=[
             pltpu.VMEM(grid_input.shape, jnp.bfloat16),
             pltpu.VMEM(forward.shape, jnp.bfloat16),
@@ -304,9 +314,9 @@
             )
         )
     )
-    cores = [[a * groups + 2 * x + k for a in range(lat_count) for x in range(chips)] for k in range(2)]
+    cores = [[n // chips * groups + n % chips * 2 + k for n in MEMBERS[k]] for k in range(2)]
     own = lax.all_to_all(
-        sent.reshape(lat_count * chips, block_rows, 128),
+        sent,
         both,
         split_axis=0,
         concat_axis=0,
@@ -317,8 +327,6 @@
 
     helpers = [jnp.asarray(m) for m in mixing_helpers(latitudes, group_orders)]
     columns_here = mix_weight.shape[1]
-    own = own.reshape(lat_count, chips, block_rows, 128)
-    other = other.reshape(lat_count, chips, block_rows, 128)
     half = pl.pallas_call(
         first_half_kernel,
         out_shape=[
@@ -416,7 +424,7 @@
     lat_count, chan_count = lax.axis_size("lat"), lax.axis_size("chan")
     orders, latitudes = order_slot.shape[0], legendre.shape[2]
     compact = (
-        lat_count == chan_count == len(STEPS)
+        lat_count == chan_count == len(STEPS) == len(MEMBERS[0]) // 2
         and 2 * latitudes * latitudes == 128
         and orders % (16 * chan_count) == 0
         and orders <= 256

time: 34.4 us -> 33.4 us (0.971)
  blocking collectives: 14.6 us -> 13.5 us
    all_to_all x1, blocking collectives: 14.6 us -> 13.5 us  [compact_shards(): lax.all_to_all(sent, both, split_axis=0, concat_axis=0, tiled=True, axis_...]
where the time goes in v6:
time: 33.4 us; the launch traced here: 33.2 us
  blocking collectives  13.5 us (40%)
  starting transfers between devices  9.62 us (29%)
  Pallas kernels  4.83 us (14%)
  waiting for transfers between devices  4.5 us (13%)
  local copies, waits for them, and re-layouts  0.6 us (2%)
    all_to_all x1, blocking collectives, compact_shards(): lax.all_to_all(sent, both, split_axis=0, concat_axis=0, tiled=True, axis_...  13.5 us
    ppermute x4, starting transfers between devices, compact_shards(): received.append(lax.ppermute(part, both, pairs))  8.14 us
    ppermute x4, waiting for transfers between devices, compact_shards(): received.append(lax.ppermute(part, both, pairs))  3.87 us
    pallas_call x1, Pallas kernels, compact_shards(): pl.pallas_call(functools.partial(analysis_kernel, math.sqrt(latitudes / d...  2.02 us
    pallas_call x1, Pallas kernels, compact_shards(): pl.pallas_call(functools.partial(synthesis_kernel, 96), in_specs=[whole]...  1.88 us
    ppermute x1, starting transfers between devices, compact_shards(): lax.ppermute(mix_weight, both, [(a * groups + b, (a ^ 1) * groups + b) fo...  1.41 us
  transfers between devices with their start and end apart: 6, of which 2 were waited for; matrix products, arithmetic and copies ran while one was open for 0% of the time, Pallas kernels for 7%

profile of v6, /device:TPU:10, one launch (start us, length us, event | category | flops | bytes accessed | tf_op | source)
XLA Modules:
  0.0 33.2 jit_solution(18068797857989469936)
XLA Ops:
  0.0 0.0 copy-start.7
  0.0 1.4 %collective-permute-start = (bf16[1024,256]{1,0:T(8,128)(2,1)}, bf16[1024,256]{1,0:T(8,128)(2,1)S(1)}, u32[]{:S(2)}, u32[]{:S(2)}) collective-permute-start(bf16[1024,256]{1,0:T(8,128)(2,1)} %weight_ref.1), channel_id=1, source_target_pairs={{0,4},{2,6},{5,1},{7,3},{8,12},{10,14},{13,9},{15,11},{16,20},{18,... | collective-permute-start | bytes 1572872 | tf_op jit(solution)/shard_map/ppermute | solution.py:279
  1.4 2.0 %shard_map.109 = bf16[8,136,128]{2,1,0:T(8,128)(2,1)S(1)} custom-call(bf16[2,1440,256]{2,1,0:T(8,128)(2,1)} %refs_4_.1, bf16[1,128,1440]{2,1,0:T(8,128)(2,1)} %constant.12.clone.table_hbm, bf16[4,8,512]{2,1,0:T(8,128)(2,1)} %bitcast.5, f32[1,512]{1,0:T(1,128)} %bitcast.6, s32[1,64]{1,0:T(1,128)} %bitcast.3), custom_call_target="tpu_custom_call" | custom-call | tf_op jit(solution)/shard_map/pallas_call | solution.py:290
  3.5 13.5 %all_to_all.5.rows_ref = bf16[8,136,128]{2,1,0:T(8,128)(2,1)S(1)} all-to-all(bf16[8,136,128]{2,1,0:T(8,128)(2,1)S(1)} %shard_map.109), channel_id=1, replica_groups={{0,4,8,12,2,6,10,14},{11,15,3,7,9,13,1,5},{16,20,24,28,18,22,26,30},{27..., dimensions={0} | all-to-all | bytes 557056 | tf_op jit(solution)/shard_map/all_to_all | solution.py:318
  17.0 0.0 copy-start.5
  17.0 0.0 copy-start.6
  17.0 0.0 copy-start.2
  17.0 0.0 copy-start.3
  17.0 0.0 copy-start.4
  17.0 0.1 collective-permute-start.1
  17.1 0.0 collective-permute-done.moved_ref
  17.1 0.0 copy-done.7
  17.1 0.1 shard_map.110.weight_ref
  17.2 0.6 %copy-done.5 = bf16[2,64,64]{2,1,0:T(8,128)(2,1)S(1)} copy-done((bf16[2,64,64]{2,1,0:T(8,128)(2,1)S(1)}, bf16[2,64,64]{2,1,0:T(8,128)(2,1)}, u32[]{:S(2)}) %copy-start.5) | copy-done | bytes 16408
  17.7 0.0 copy-done.6
  17.7 0.2 shard_map.111
  18.0 0.6 %collective-permute-done.1.rows_ref = bf16[8,136,128]{2,1,0:T(8,128)(2,1)S(1)} collective-permute-done((bf16[8,136,128]{2,1,0:T(8,128)(2,1)S(1)}, bf16[8,136,128]{2,1,0:T(8,128)(2,1)S(1)}, u32[]{:S(2)}, u32[]{:S(2)}) %collective-permute-start.1) | collective-permute-done | bytes 278560 | tf_op jit(solution)/shard_map/ppermute | solution.py:326
  18.6 0.0 copy-done.2
  18.6 0.0 copy-done.3
  18.6 0.0 copy-done.4
  18.6 0.6 %shard_map.112 = (bf16[64,256]{1,0:T(8,128)(2,1)S(1)}, bf16[64,256]{1,0:T(8,128)(2,1)S(1)}, bf16[64,256]{1,0:T(8,128)(2,1)S(1)}, bf16[64,256]{1,0:T(8,128)(2,1)S(1)}) custom-call(f32[256,256]{1,0:T(8,128)S(1)} %get-tuple-element.12.mixed_ref, f32[16,128]{1,0:T(8,128)S(1)} %get-tuple-element.13.pairs_ref, bf16[16,64]{1,0:T(8,128)(2,1)S(1)} %get-tuple-element.14.hit_ref, ...), custom_call_target="tpu_custom_call" | custom-call | tf_op jit(solution)/shard_map/pallas_call | solution.py:342
  19.3 2.5 %collective-permute-start.2 = (bf16[64,256]{1,0:T(8,128)(2,1)S(1)}, bf16[64,256]{1,0:T(8,128)(2,1)S(1)}, u32[]{:S(2)}, u32[]{:S(2)}) collective-permute-start(bf16[64,256]{1,0:T(8,128)(2,1)S(1)} %get-tuple-element.15), channel_id=1, source_target_pairs={{0,12},{1,13},{2,4},{3,5},{4,8},{5,9},{6,0},{7,1},{8,14},{9,15},{1... | collective-permute-start | bytes 98312 | tf_op jit(solution)/shard_map/ppermute | solution.py:353
  21.7 0.6 %collective-permute-start.3 = (bf16[64,256]{1,0:T(8,128)(2,1)S(1)}, bf16[64,256]{1,0:T(8,128)(2,1)S(1)}, u32[]{:S(2)}, u32[]{:S(2)}) collective-permute-start(bf16[64,256]{1,0:T(8,128)(2,1)S(1)} %get-tuple-element.16), channel_id=1, source_target_pairs={{0,4},{1,5},{2,12},{3,13},{4,0},{5,1},{6,8},{7,9},{8,6},{9,7},{10,... | collective-permute-start | bytes 98312 | tf_op jit(solution)/shard_map/ppermute | solution.py:353
  22.4 1.4 %collective-permute-start.4 = (bf16[64,256]{1,0:T(8,128)(2,1)S(1)}, bf16[64,256]{1,0:T(8,128)(2,1)S(1)}, u32[]{:S(2)}, u32[]{:S(2)}) collective-permute-start(bf16[64,256]{1,0:T(8,128)(2,1)S(1)} %get-tuple-element.17), channel_id=1, source_target_pairs={{0,8},{1,9},{2,0},{3,1},{4,12},{5,13},{6,4},{7,5},{8,10},{9,11},{1... | collective-permute-start | bytes 98312 | tf_op jit(solution)/shard_map/ppermute | solution.py:353
  23.7 3.7 %collective-permute-start.5 = (bf16[64,256]{1,0:T(8,128)(2,1)S(1)}, bf16[64,256]{1,0:T(8,128)(2,1)S(1)}, u32[]{:S(2)}, u32[]{:S(2)}) collective-permute-start(bf16[64,256]{1,0:T(8,128)(2,1)S(1)} %get-tuple-element.18), channel_id=1, source_target_pairs={{0,0},{1,1},{2,8},{3,9},{4,4},{5,5},{6,12},{7,13},{8,2},{9,3},{10,... | collective-permute-start | bytes 98312 | tf_op jit(solution)/shard_map/ppermute | solution.py:353
  27.4 0.0 collective-permute-done.2.refs_0_
  27.4 0.0 collective-permute-done.3.refs_1_
  27.4 0.0 collective-permute-done.4.refs_2_
  27.5 3.9 %collective-permute-done.5.refs_3_ = bf16[64,256]{1,0:T(8,128)(2,1)S(1)} collective-permute-done((bf16[64,256]{1,0:T(8,128)(2,1)S(1)}, bf16[64,256]{1,0:T(8,128)(2,1)S(1)}, u32[]{:S(2)}, u32[]{:S(2)}) %collective-permute-start.5) | collective-permute-done | bytes 32800 | tf_op jit(solution)/shard_map/ppermute | solution.py:353
  31.3 0.0 copy-done
  31.3 0.0 copy-done.1
  31.3 1.9 %shard_map.113 = bf16[2,1440,256]{2,1,0:T(8,128)(2,1)} custom-call(bf16[64,256]{1,0:T(8,128)(2,1)S(1)} %collective-permute-done.2.refs_0_, bf16[64,256]{1,0:T(8,128)(2,1)S(1)} %collective-permute-done.3.refs_1_, bf16[64,256]{1,0:T(8,128)(2,1)S(1)} %collective-permute-done.4.refs_2_, bf16[64,256]{1,0:T(8,128)(2,1)S(1)} %collective-permute-done.5.refs_3_, ...), custom_call_target="tpu_custom_call" | custom-call | tf_op jit(solution)/shard_map/pallas_call | solution.py:356
  (2 shorter events, 0.0 us)
Async XLA Ops:
  0.0 17.1 %copy-start.7 = (bf16[1024,256]{1,0:T(8,128)(2,1)S(1)}, bf16[1024,256]{1,0:T(8,128)(2,1)}, u32[]{:S(2)}) copy-start(bf16[1024,256]{1,0:T(8,128)(2,1)} %weight_ref.1) | copy-start | bytes 1572868
  0.0 17.1 %collective-permute-start = (bf16[1024,256]{1,0:T(8,128)(2,1)}, bf16[1024,256]{1,0:T(8,128)(2,1)S(1)}, u32[]{:S(2)}, u32[]{:S(2)}) collective-permute-start(bf16[1024,256]{1,0:T(8,128)(2,1)} %weight_ref.1), channel_id=1, source_target_pairs={{0,4},{2,6},{5,1},{7,3},{8,12},{10,14},{13,9},{15,11},{16,20},{18,... | collective-permute-start | bytes 1572872 | tf_op jit(solution)/shard_map/ppermute | solution.py:279
  17.0 0.8 %copy-start.5 = (bf16[2,64,64]{2,1,0:T(8,128)(2,1)S(1)}, bf16[2,64,64]{2,1,0:T(8,128)(2,1)}, u32[]{:S(2)}) copy-start(bf16[2,64,64]{2,1,0:T(8,128)(2,1)} %constant.16.clone.columns_ref) | copy-start | bytes 49156
  17.0 0.8 %copy-start.6 = (s32[64]{0:T(128)S(1)}, s32[64]{0:T(128)}, u32[]{:S(2)}) copy-start(s32[64]{0:T(128)} %param.15) | copy-start | bytes 772
  17.0 1.6 %copy-start.2 = (bf16[256,256]{1,0:T(8,128)(2,1)S(1)}, bf16[256,256]{1,0:T(8,128)(2,1)}, u32[]{:S(2)}) copy-start(bf16[256,256]{1,0:T(8,128)(2,1)} %constant.15.clone.same_ref) | copy-start | bytes 393220
  17.0 1.6 %copy-start.3 = (bf16[128,512]{1,0:T(8,128)(2,1)S(1)}, bf16[128,512]{1,0:T(8,128)(2,1)}, u32[]{:S(2)}) copy-start(bf16[128,512]{1,0:T(8,128)(2,1)} %constant.14.clone.halves_ref) | copy-start | bytes 393220
  17.0 1.6 %copy-start.4 = (bf16[256,128]{1,0:T(8,128)(2,1)S(1)}, bf16[256,128]{1,0:T(8,128)(2,1)}, u32[]{:S(2)}) copy-start(bf16[256,128]{1,0:T(8,128)(2,1)} %constant.13.clone.keep_ref) | copy-start | bytes 196612
  17.0 1.6 %collective-permute-start.1 = (bf16[8,136,128]{2,1,0:T(8,128)(2,1)S(1)}, bf16[8,136,128]{2,1,0:T(8,128)(2,1)S(1)}, u32[]{:S(2)}, u32[]{:S(2)}) collective-permute-start(bf16[8,136,128]{2,1,0:T(8,128)(2,1)S(1)} %all_to_all.5.rows_ref), channel_id=1, source_target_pairs={{0,1},{1,0},{2,3},{3,2},{4,5},{5,4},{6,7},{7,6},{8,9},{9,8},{10,11... | collective-permute-start | bytes 835592 | tf_op jit(solution)/shard_map/ppermute | solution.py:326
  17.7 13.6 %copy-start = (bf16[2,1440,256]{2,1,0:T(8,128)(2,1)S(1)}, bf16[2,1440,256]{2,1,0:T(8,128)(2,1)}, u32[]{:S(2)}) copy-start(bf16[2,1440,256]{2,1,0:T(8,128)(2,1)} %refs_4_.1) | copy-start | bytes 4423684
  17.7 13.6 %copy-start.1 = (bf16[1440,128]{1,0:T(8,128)(2,1)S(1)}, bf16[1440,128]{1,0:T(8,128)(2,1)}, u32[]{:S(2)}) copy-start(bf16[1440,128]{1,0:T(8,128)(2,1)} %constant.17.clone.refs_5_) | copy-start | bytes 1105924
  19.3 8.2 %collective-permute-start.2 = (bf16[64,256]{1,0:T(8,128)(2,1)S(1)}, bf16[64,256]{1,0:T(8,128)(2,1)S(1)}, u32[]{:S(2)}, u32[]{:S(2)}) collective-permute-start(bf16[64,256]{1,0:T(8,128)(2,1)S(1)} %get-tuple-element.15), channel_id=1, source_target_pairs={{0,12},{1,13},{2,4},{3,5},{4,8},{5,9},{6,0},{7,1},{8,14},{9,15},{1... | collective-permute-start | bytes 98312 | tf_op jit(solution)/shard_map/ppermute | solution.py:353
  21.7 5.7 %collective-permute-start.3 = (bf16[64,256]{1,0:T(8,128)(2,1)S(1)}, bf16[64,256]{1,0:T(8,128)(2,1)S(1)}, u32[]{:S(2)}, u32[]{:S(2)}) collective-permute-start(bf16[64,256]{1,0:T(8,128)(2,1)S(1)} %get-tuple-element.16), channel_id=1, source_target_pairs={{0,4},{1,5},{2,12},{3,13},{4,0},{5,1},{6,8},{7,9},{8,6},{9,7},{10,... | collective-permute-start | bytes 98312 | tf_op jit(solution)/shard_map/ppermute | solution.py:353
  22.4 5.1 %collective-permute-start.4 = (bf16[64,256]{1,0:T(8,128)(2,1)S(1)}, bf16[64,256]{1,0:T(8,128)(2,1)S(1)}, u32[]{:S(2)}, u32[]{:S(2)}) collective-permute-start(bf16[64,256]{1,0:T(8,128)(2,1)S(1)} %get-tuple-element.17), channel_id=1, source_target_pairs={{0,8},{1,9},{2,0},{3,1},{4,12},{5,13},{6,4},{7,5},{8,10},{9,11},{1... | collective-permute-start | bytes 98312 | tf_op jit(solution)/shard_map/ppermute | solution.py:353
  23.7 7.6 %collective-permute-start.5 = (bf16[64,256]{1,0:T(8,128)(2,1)S(1)}, bf16[64,256]{1,0:T(8,128)(2,1)S(1)}, u32[]{:S(2)}, u32[]{:S(2)}) collective-permute-start(bf16[64,256]{1,0:T(8,128)(2,1)S(1)} %get-tuple-element.18), channel_id=1, source_target_pairs={{0,0},{1,1},{2,8},{3,9},{4,4},{5,5},{6,12},{7,13},{8,2},{9,3},{10,... | collective-permute-start | bytes 98312 | tf_op jit(solution)/shard_map/ppermute | solution.py:353

commit v7 on v6

--- a/solution.py
+++ b/solution.py
@@ -63,11 +63,11 @@
     for copy in small:
         copy.start()
     for k in range(chunks):
-        tables[k].start()
+        tables[k].start(priority=1)
         parts[0][k].start()
     for t in range(1, lat_dev):
         for k in range(chunks):
-            parts[t][k].start()
+            parts[t][k].start(priority=1)
 
     for copy in small:
         copy.wait()
@@ -205,17 +205,16 @@
     mixed, pairs = channel_products(rows_ref, weight_ref, 1 - core, hit_ref[...], count)
     mixed = mixed_ref[...] + mixed
     pairs = pairs_ref[...] + pairs
-    wide = jnp.concatenate([pairs] * (count // group_orders), axis=0) * keep_ref[...].astype(jnp.float32)
-    matrix = jnp.dot(wide.astype(jnp.bfloat16), halves_ref[...], preferred_element_type=jnp.float32)
-    same = same_ref[...].astype(jnp.float32)
-    high = (matrix[:, :count] * same).astype(jnp.bfloat16)
-    low = (matrix[:, count:] * same).astype(jnp.bfloat16)
+    wide = jnp.concatenate([pairs.astype(jnp.bfloat16)] * (count // group_orders), axis=0) * keep_ref[...]
+    matrix = jnp.dot(wide, halves_ref[...], preferred_element_type=jnp.float32).astype(jnp.bfloat16)
+    same = same_ref[...]
+    high, low = matrix[:, :count] * same, matrix[:, count:] * same
     mixed_high = mixed.astype(jnp.bfloat16)
     mixed_low = (mixed - mixed_high.astype(jnp.float32)).astype(jnp.bfloat16)
-    synthesis = (
-        jnp.dot(high, mixed_high, preferred_element_type=jnp.float32)
-        + jnp.dot(high, mixed_low, preferred_element_type=jnp.float32)
-        + jnp.dot(low, mixed_high, preferred_element_type=jnp.float32)
+    synthesis = jnp.dot(
+        jnp.concatenate([high, high, low], axis=1),
+        jnp.concatenate([mixed_high, mixed_low, mixed_high], axis=0),
+        preferred_element_type=jnp.float32,
     )
     held[...] = synthesis.astype(jnp.bfloat16).reshape(held.shape)
     place = lax.axis_index("chan") - core + lax.rem(lax.axis_index("lat"), 2)
@@ -246,7 +245,7 @@
                 out_buf[t, at : at + piece, :] = value.astype(jnp.bfloat16)
             span = pl.ds(k * size, size)
             copy = pltpu.make_async_copy(out_buf.at[t, span], out_hbm.at[t, span], out_sem.at[t, k])
-            copy.start()
+            copy.start(priority=t % 2)
             copies.append(copy)
     for copy in copies:
         copy.wait()

time: 33.4 us -> 33.4 us (level)
  no operation moved by 1% of the time
where the time goes in v7:
time: 33.4 us; the launch traced here: 33.2 us
  blocking collectives  13.5 us (40%)
  starting transfers between devices  9.62 us (29%)
  Pallas kernels  4.85 us (15%)
  waiting for transfers between devices  4.49 us (13%)
  local copies, waits for them, and re-layouts  0.6 us (2%)
    all_to_all x1, blocking collectives, compact_shards(): lax.all_to_all(sent, both, split_axis=0, concat_axis=0, tiled=True, axis_...  13.5 us
    ppermute x4, starting transfers between devices, compact_shards(): received.append(lax.ppermute(part, both, pairs))  8.14 us
    ppermute x4, waiting for transfers between devices, compact_shards(): received.append(lax.ppermute(part, both, pairs))  3.86 us
    pallas_call x1, Pallas kernels, compact_shards(): pl.pallas_call(functools.partial(analysis_kernel, math.sqrt(latitudes / d...  2.04 us
    pallas_call x1, Pallas kernels, compact_shards(): pl.pallas_call(functools.partial(synthesis_kernel, 96), in_specs=[whole]...  1.88 us
    ppermute x1, starting transfers between devices, compact_shards(): lax.ppermute(mix_weight, both, [(a * groups + b, (a ^ 1) * groups + b) fo...  1.41 us
  transfers between devices with their start and end apart: 6, of which 2 were waited for; matrix products, arithmetic and copies ran while one was open for 0% of the time, Pallas kernels for 7%

profile of v7, /device:TPU:10, one launch (start us, length us, event | category | flops | bytes accessed | tf_op | source)
XLA Modules:
  0.0 33.2 jit_solution(9833603344227589896)
XLA Ops:
  0.0 0.0 copy-start.7
  0.0 1.4 %collective-permute-start = (bf16[1024,256]{1,0:T(8,128)(2,1)}, bf16[1024,256]{1,0:T(8,128)(2,1)S(1)}, u32[]{:S(2)}, u32[]{:S(2)}) collective-permute-start(bf16[1024,256]{1,0:T(8,128)(2,1)} %weight_ref.1), channel_id=1, source_target_pairs={{0,4},{2,6},{5,1},{7,3},{8,12},{10,14},{13,9},{15,11},{16,20},{18,... | collective-permute-start | bytes 1572872 | tf_op jit(solution)/shard_map/ppermute | solution.py:278
  1.4 2.0 %shard_map.109 = bf16[8,136,128]{2,1,0:T(8,128)(2,1)S(1)} custom-call(bf16[2,1440,256]{2,1,0:T(8,128)(2,1)} %refs_4_.1, bf16[1,128,1440]{2,1,0:T(8,128)(2,1)} %constant.12.clone.table_hbm, bf16[4,8,512]{2,1,0:T(8,128)(2,1)} %bitcast.5, f32[1,512]{1,0:T(1,128)} %bitcast.6, s32[1,64]{1,0:T(1,128)} %bitcast.3), custom_call_target="tpu_custom_call" | custom-call | tf_op jit(solution)/shard_map/pallas_call | solution.py:289
  3.5 13.5 %all_to_all.5.rows_ref = bf16[8,136,128]{2,1,0:T(8,128)(2,1)S(1)} all-to-all(bf16[8,136,128]{2,1,0:T(8,128)(2,1)S(1)} %shard_map.109), channel_id=1, replica_groups={{0,4,8,12,2,6,10,14},{11,15,3,7,9,13,1,5},{16,20,24,28,18,22,26,30},{27..., dimensions={0} | all-to-all | bytes 557056 | tf_op jit(solution)/shard_map/all_to_all | solution.py:317
  17.0 0.0 copy-start.5
  17.0 0.0 copy-start.6
  17.0 0.0 copy-start.2
  17.0 0.0 copy-start.3
  17.0 0.0 copy-start.4
  17.0 0.1 collective-permute-start.1
  17.1 0.0 collective-permute-done.moved_ref
  17.1 0.0 copy-done.7
  17.1 0.1 shard_map.110.weight_ref
  17.2 0.6 %copy-done.5 = bf16[2,64,64]{2,1,0:T(8,128)(2,1)S(1)} copy-done((bf16[2,64,64]{2,1,0:T(8,128)(2,1)S(1)}, bf16[2,64,64]{2,1,0:T(8,128)(2,1)}, u32[]{:S(2)}) %copy-start.5) | copy-done | bytes 16408
  17.8 0.0 copy-done.6
  17.8 0.2 shard_map.111
  18.0 0.6 %collective-permute-done.1.rows_ref = bf16[8,136,128]{2,1,0:T(8,128)(2,1)S(1)} collective-permute-done((bf16[8,136,128]{2,1,0:T(8,128)(2,1)S(1)}, bf16[8,136,128]{2,1,0:T(8,128)(2,1)S(1)}, u32[]{:S(2)}, u32[]{:S(2)}) %collective-permute-start.1) | collective-permute-done | bytes 278560 | tf_op jit(solution)/shard_map/ppermute | solution.py:325
  18.6 0.0 copy-done.2
  18.6 0.0 copy-done.3
  18.6 0.0 copy-done.4
  18.7 0.6 %shard_map.112 = (bf16[64,256]{1,0:T(8,128)(2,1)S(1)}, bf16[64,256]{1,0:T(8,128)(2,1)S(1)}, bf16[64,256]{1,0:T(8,128)(2,1)S(1)}, bf16[64,256]{1,0:T(8,128)(2,1)S(1)}) custom-call(f32[256,256]{1,0:T(8,128)S(1)} %get-tuple-element.12.mixed_ref, f32[16,128]{1,0:T(8,128)S(1)} %get-tuple-element.13.pairs_ref, bf16[16,64]{1,0:T(8,128)(2,1)S(1)} %get-tuple-element.14.hit_ref, ...), custom_call_target="tpu_custom_call" | custom-call | tf_op jit(solution)/shard_map/pallas_call | solution.py:341
  19.3 2.5 %collective-permute-start.2 = (bf16[64,256]{1,0:T(8,128)(2,1)S(1)}, bf16[64,256]{1,0:T(8,128)(2,1)S(1)}, u32[]{:S(2)}, u32[]{:S(2)}) collective-permute-start(bf16[64,256]{1,0:T(8,128)(2,1)S(1)} %get-tuple-element.15), channel_id=1, source_target_pairs={{0,12},{1,13},{2,4},{3,5},{4,8},{5,9},{6,0},{7,1},{8,14},{9,15},{1... | collective-permute-start | bytes 98312 | tf_op jit(solution)/shard_map/ppermute | solution.py:352
  21.8 0.6 %collective-permute-start.3 = (bf16[64,256]{1,0:T(8,128)(2,1)S(1)}, bf16[64,256]{1,0:T(8,128)(2,1)S(1)}, u32[]{:S(2)}, u32[]{:S(2)}) collective-permute-start(bf16[64,256]{1,0:T(8,128)(2,1)S(1)} %get-tuple-element.16), channel_id=1, source_target_pairs={{0,4},{1,5},{2,12},{3,13},{4,0},{5,1},{6,8},{7,9},{8,6},{9,7},{10,... | collective-permute-start | bytes 98312 | tf_op jit(solution)/shard_map/ppermute | solution.py:352
  22.4 1.4 %collective-permute-start.4 = (bf16[64,256]{1,0:T(8,128)(2,1)S(1)}, bf16[64,256]{1,0:T(8,128)(2,1)S(1)}, u32[]{:S(2)}, u32[]{:S(2)}) collective-permute-start(bf16[64,256]{1,0:T(8,128)(2,1)S(1)} %get-tuple-element.17), channel_id=1, source_target_pairs={{0,8},{1,9},{2,0},{3,1},{4,12},{5,13},{6,4},{7,5},{8,10},{9,11},{1... | collective-permute-start | bytes 98312 | tf_op jit(solution)/shard_map/ppermute | solution.py:352
  23.7 3.7 %collective-permute-start.5 = (bf16[64,256]{1,0:T(8,128)(2,1)S(1)}, bf16[64,256]{1,0:T(8,128)(2,1)S(1)}, u32[]{:S(2)}, u32[]{:S(2)}) collective-permute-start(bf16[64,256]{1,0:T(8,128)(2,1)S(1)} %get-tuple-element.18), channel_id=1, source_target_pairs={{0,0},{1,1},{2,8},{3,9},{4,4},{5,5},{6,12},{7,13},{8,2},{9,3},{10,... | collective-permute-start | bytes 98312 | tf_op jit(solution)/shard_map/ppermute | solution.py:352
  27.4 0.0 collective-permute-done.2.refs_0_
  27.5 0.0 collective-permute-done.3.refs_1_
  27.5 0.0 collective-permute-done.4.refs_2_
  27.5 3.8 %collective-permute-done.5.refs_3_ = bf16[64,256]{1,0:T(8,128)(2,1)S(1)} collective-permute-done((bf16[64,256]{1,0:T(8,128)(2,1)S(1)}, bf16[64,256]{1,0:T(8,128)(2,1)S(1)}, u32[]{:S(2)}, u32[]{:S(2)}) %collective-permute-start.5) | collective-permute-done | bytes 32800 | tf_op jit(solution)/shard_map/ppermute | solution.py:352
  31.3 0.0 copy-done
  31.3 0.0 copy-done.1
  31.3 1.9 %shard_map.113 = bf16[2,1440,256]{2,1,0:T(8,128)(2,1)} custom-call(bf16[64,256]{1,0:T(8,128)(2,1)S(1)} %collective-permute-done.2.refs_0_, bf16[64,256]{1,0:T(8,128)(2,1)S(1)} %collective-permute-done.3.refs_1_, bf16[64,256]{1,0:T(8,128)(2,1)S(1)} %collective-permute-done.4.refs_2_, bf16[64,256]{1,0:T(8,128)(2,1)S(1)} %collective-permute-done.5.refs_3_, ...), custom_call_target="tpu_custom_call" | custom-call | tf_op jit(solution)/shard_map/pallas_call | solution.py:355
  (2 shorter events, 0.0 us)
Async XLA Ops:
  0.0 17.1 %copy-start.7 = (bf16[1024,256]{1,0:T(8,128)(2,1)S(1)}, bf16[1024,256]{1,0:T(8,128)(2,1)}, u32[]{:S(2)}) copy-start(bf16[1024,256]{1,0:T(8,128)(2,1)} %weight_ref.1) | copy-start | bytes 1572868
  0.0 17.1 %collective-permute-start = (bf16[1024,256]{1,0:T(8,128)(2,1)}, bf16[1024,256]{1,0:T(8,128)(2,1)S(1)}, u32[]{:S(2)}, u32[]{:S(2)}) collective-permute-start(bf16[1024,256]{1,0:T(8,128)(2,1)} %weight_ref.1), channel_id=1, source_target_pairs={{0,4},{2,6},{5,1},{7,3},{8,12},{10,14},{13,9},{15,11},{16,20},{18,... | collective-permute-start | bytes 1572872 | tf_op jit(solution)/shard_map/ppermute | solution.py:278
  17.0 0.8 %copy-start.5 = (bf16[2,64,64]{2,1,0:T(8,128)(2,1)S(1)}, bf16[2,64,64]{2,1,0:T(8,128)(2,1)}, u32[]{:S(2)}) copy-start(bf16[2,64,64]{2,1,0:T(8,128)(2,1)} %constant.16.clone.columns_ref) | copy-start | bytes 49156
  17.0 0.8 %copy-start.6 = (s32[64]{0:T(128)S(1)}, s32[64]{0:T(128)}, u32[]{:S(2)}) copy-start(s32[64]{0:T(128)} %param.15) | copy-start | bytes 772
  17.0 1.6 %copy-start.2 = (bf16[256,256]{1,0:T(8,128)(2,1)S(1)}, bf16[256,256]{1,0:T(8,128)(2,1)}, u32[]{:S(2)}) copy-start(bf16[256,256]{1,0:T(8,128)(2,1)} %constant.15.clone.same_ref) | copy-start | bytes 393220
  17.0 1.6 %copy-start.3 = (bf16[128,512]{1,0:T(8,128)(2,1)S(1)}, bf16[128,512]{1,0:T(8,128)(2,1)}, u32[]{:S(2)}) copy-start(bf16[128,512]{1,0:T(8,128)(2,1)} %constant.14.clone.halves_ref) | copy-start | bytes 393220
  17.0 1.6 %copy-start.4 = (bf16[256,128]{1,0:T(8,128)(2,1)S(1)}, bf16[256,128]{1,0:T(8,128)(2,1)}, u32[]{:S(2)}) copy-start(bf16[256,128]{1,0:T(8,128)(2,1)} %constant.13.clone.keep_ref) | copy-start | bytes 196612
  17.0 1.6 %collective-permute-start.1 = (bf16[8,136,128]{2,1,0:T(8,128)(2,1)S(1)}, bf16[8,136,128]{2,1,0:T(8,128)(2,1)S(1)}, u32[]{:S(2)}, u32[]{:S(2)}) collective-permute-start(bf16[8,136,128]{2,1,0:T(8,128)(2,1)S(1)} %all_to_all.5.rows_ref), channel_id=1, source_target_pairs={{0,1},{1,0},{2,3},{3,2},{4,5},{5,4},{6,7},{7,6},{8,9},{9,8},{10,11... | collective-permute-start | bytes 835592 | tf_op jit(solution)/shard_map/ppermute | solution.py:325
  17.8 13.6 %copy-start = (bf16[2,1440,256]{2,1,0:T(8,128)(2,1)S(1)}, bf16[2,1440,256]{2,1,0:T(8,128)(2,1)}, u32[]{:S(2)}) copy-start(bf16[2,1440,256]{2,1,0:T(8,128)(2,1)} %refs_4_.1) | copy-start | bytes 4423684
  17.8 13.6 %copy-start.1 = (bf16[1440,128]{1,0:T(8,128)(2,1)S(1)}, bf16[1440,128]{1,0:T(8,128)(2,1)}, u32[]{:S(2)}) copy-start(bf16[1440,128]{1,0:T(8,128)(2,1)} %constant.17.clone.refs_5_) | copy-start | bytes 1105924
  19.3 8.2 %collective-permute-start.2 = (bf16[64,256]{1,0:T(8,128)(2,1)S(1)}, bf16[64,256]{1,0:T(8,128)(2,1)S(1)}, u32[]{:S(2)}, u32[]{:S(2)}) collective-permute-start(bf16[64,256]{1,0:T(8,128)(2,1)S(1)} %get-tuple-element.15), channel_id=1, source_target_pairs={{0,12},{1,13},{2,4},{3,5},{4,8},{5,9},{6,0},{7,1},{8,14},{9,15},{1... | collective-permute-start | bytes 98312 | tf_op jit(solution)/shard_map/ppermute | solution.py:352
  21.8 5.7 %collective-permute-start.3 = (bf16[64,256]{1,0:T(8,128)(2,1)S(1)}, bf16[64,256]{1,0:T(8,128)(2,1)S(1)}, u32[]{:S(2)}, u32[]{:S(2)}) collective-permute-start(bf16[64,256]{1,0:T(8,128)(2,1)S(1)} %get-tuple-element.16), channel_id=1, source_target_pairs={{0,4},{1,5},{2,12},{3,13},{4,0},{5,1},{6,8},{7,9},{8,6},{9,7},{10,... | collective-permute-start | bytes 98312 | tf_op jit(solution)/shard_map/ppermute | solution.py:352
  22.4 5.1 %collective-permute-start.4 = (bf16[64,256]{1,0:T(8,128)(2,1)S(1)}, bf16[64,256]{1,0:T(8,128)(2,1)S(1)}, u32[]{:S(2)}, u32[]{:S(2)}) collective-permute-start(bf16[64,256]{1,0:T(8,128)(2,1)S(1)} %get-tuple-element.17), channel_id=1, source_target_pairs={{0,8},{1,9},{2,0},{3,1},{4,12},{5,13},{6,4},{7,5},{8,10},{9,11},{1... | collective-permute-start | bytes 98312 | tf_op jit(solution)/shard_map/ppermute | solution.py:352
  23.7 7.6 %collective-permute-start.5 = (bf16[64,256]{1,0:T(8,128)(2,1)S(1)}, bf16[64,256]{1,0:T(8,128)(2,1)S(1)}, u32[]{:S(2)}, u32[]{:S(2)}) collective-permute-start(bf16[64,256]{1,0:T(8,128)(2,1)S(1)} %get-tuple-element.18), channel_id=1, source_target_pairs={{0,0},{1,1},{2,8},{3,9},{4,4},{5,5},{6,12},{7,13},{8,2},{9,3},{10,... | collective-permute-start | bytes 98312 | tf_op jit(solution)/shard_map/ppermute | solution.py:352
